TPU v7x, 32 devices: a whole 2x2x4 slice. The times are simulated.
32 devices in a mesh: grp: 2 (over y), op: 4 (over z), sec: 2 (over x), rep: 2 (over core).
Axes of the slice: x: 2, y: 2, z: 4, core: 2. Of those that a mesh axis runs over, the one named last changes fastest.
Arguments:
- wavefunction: float32 [24, 256, 256], P(('grp', 'sec')), parts along dimension 0, may hold values from -6 to 6
- left_operators: float32 [64, 256, 256], P(('op', 'rep')), as said below
- right_operators: float32 [64, 256, 256], P(('op', 'rep')), as said below
- coupling: int32 [64, 12], P(('op', 'rep')), may hold values from 0 to 11, as said below
- left_sizes: int32 [24], P('grp'), parts along dimension 0, may hold values from 64 to 256, as said below
- right_sizes: int32 [24], P('grp'), parts along dimension 0, may hold values from 64 to 256, as said below
Outputs:
- sigma_next: float32 [24, 256, 256], P(('grp', 'sec'), ('op', 'rep')), parts along dimension 0
- residual: float32 [24, 256, 256], P(('grp', 'sec'), ('op', 'rep')), parts along dimension 0
There are 2 independent parts, one for each index of `grp`. A program takes and returns all parts, laid end to end along the dimension named above; an argument that names none is the same for every part. Nothing has to cross between parts.
Inputs may be any that keep to these rules, and one draw needn't show every extreme that they name: `left_sizes`: in every draw one sector has exactly 256 rows and another exactly 64. `right_sizes`: in every draw one sector has exactly 256 columns and another exactly 64. `coupling`: every row is a permutation of the 12 sectors; row k + 32 is the inverse of row k for k below 32; a quarter of the rows or more are the identity. `left_operators`: term k + 32 is the transpose of term k for k below 32. `right_operators`: term k + 32 is the transpose of term k for k below 32.
All inputs are finite; a program needn't handle non-finite values.
Results may differ from a plain program's by a relative error of at most 0.00017.
Values sent between devices are 32-bit elements; how exact they have to be, the bound alone decides.
No kernel may reach another device: no remote copies, remote signals or barrier semaphores. Data moves between devices by JAX's collectives and lax.ppermute only.
A program may use at most 128 MiB of HBM per device.

v0:
```python
import jax
import jax.numpy as jnp
from jax import lax
from jax.sharding import PartitionSpec as P


def build_mask(left_sizes, right_sizes, width):
    row_ids = jnp.arange(width, dtype=jnp.int32)
    row_ok = row_ids[None, :, None] < left_sizes[:, None, None]
    col_ok = row_ids[None, None, :] < right_sizes[:, None, None]
    return jnp.where(row_ok & col_ok, 1.0, 0.0).astype(jnp.float32)


def local_terms(field, left_operators, right_operators, coupling, own_mask):
    own_count = field.shape[0]
    first_own = lax.axis_index("sec") * own_count
    own_ids = first_own + jnp.arange(own_count, dtype=jnp.int32)
    gathered = lax.all_gather(field, "sec", axis=0, tiled=True)
    sources = jnp.take(coupling, own_ids, axis=1)
    picked = gathered[sources]
    halfway = jnp.einsum("kij,ksjl->ksil", left_operators, picked, precision=lax.Precision.HIGHEST)
    summed = jnp.einsum("ksil,kml->sim", halfway, right_operators, precision=lax.Precision.HIGHEST)
    return summed * own_mask


def on_device(wavefunction, left_operators, right_operators, coupling, left_sizes, right_sizes):
    own_count = wavefunction.shape[0]
    width = wavefunction.shape[1]
    first_own = lax.axis_index("sec") * own_count
    own_left = lax.dynamic_slice_in_dim(left_sizes, first_own, own_count, 0)
    own_right = lax.dynamic_slice_in_dim(right_sizes, first_own, own_count, 0)
    own_mask = build_mask(own_left, own_right, width)
    masked_wave = wavefunction * own_mask
    entries = coupling.shape[1] * width * width
    row_count = width // lax.axis_size(("op", "rep"))
    row_start = lax.axis_index(("op", "rep")) * row_count
    partial_first = local_terms(masked_wave, left_operators, right_operators, coupling, own_mask)
    sigma_first = lax.psum(partial_first, ("op", "rep"))
    correlation, wave_norm = lax.psum(
        (jnp.sum(masked_wave * sigma_first), jnp.sum(masked_wave * masked_wave)), "sec"
    )
    energy = correlation / wave_norm
    residual = sigma_first - energy * masked_wave
    res_norm = lax.psum(jnp.sum(residual * residual), "sec")
    direction = residual / jnp.sqrt(res_norm / entries + 1e-06)
    residual_out = lax.dynamic_slice_in_dim(residual, row_start, row_count, 1)
    partial_next = local_terms(direction, left_operators, right_operators, coupling, own_mask)
    sigma_next = lax.psum_scatter(partial_next, ("op", "rep"), scatter_dimension=1, tiled=True)
    return (sigma_next, residual_out)


def solution(mesh):
    in_specs = (
        P(("grp", "sec"), None, None),
        P(("op", "rep"), None, None),
        P(("op", "rep"), None, None),
        P(("op", "rep"), None),
        P("grp"),
        P("grp"),
    )
    out_specs = (P(("grp", "sec"), ("op", "rep"), None), P(("grp", "sec"), ("op", "rep"), None))
    return jax.shard_map(
        on_device, mesh=mesh, in_specs=in_specs, out_specs=out_specs, check_vma=False
    )
```

profile of v0, /device:TPU:0, one launch (start us, length us, event | category | flops | bytes accessed | tf_op | source)
XLA Modules:
  0.0 302.8 jit_solution(8888500823586629849)
XLA Ops:
  7.2 0.0 all-gather.3.cloned.1.call-start
  7.2 0.9 dynamic_slice.9
  8.1 0.7 dynamic_slice.10
  8.8 0.1 iota_compare_fusion
  8.9 2.9 select_multiply_fusion.2
  11.8 0.0 all-gather.3.cloned.1.call-update
  11.8 0.0 all-reduce.3.cloned.1.call-start
  11.8 0.1 copy.10
  11.9 0.6 gather_fusion.2
  12.5 0.1 compare_select_fusion
  12.6 0.1 copy.11
  12.7 0.1 reshape.65
  12.8 46.9 %all-gather.3.cloned.1.call-done = f32[12,256,256]{2,1,0:T(8,128)} async-done(((f32[6,256,256]{2,1,0:T(8,128)}), f32[12,256,256]{2,1,0:T(8,128)}) %all-gather.3.cloned.1.call-update) | async-done | bytes 3145744 | tf_op jit(solution)/shard_map/all_gather | solution.py:18
  59.6 9.5 %gather_fusion = f32[48,256,256]{2,1,0:T(8,128)} fusion(f32[12,256,256]{2,1,0:T(8,128)} %all-gather.3.cloned.1.call-done, s32[1024]{0:T(1024)S(1)} %pad_clamp_fusion), kind=kCustom, calls=%fused_computation.1 | custom fusion | bytes 25166016 | tf_op jit(solution)/shard_map/gather | solution.py:20
  69.2 15.8 %fusion.6 = f32[8,6,256,256]{2,3,0,1:T(8,128)S(1)} fusion(f32[8,6,256,256]{3,2,1,0:T(8,128)} %bitcast.35, f32[8,256,256]{2,1,0:T(8,128)S(1)} %copy-done), kind=kOutput, calls=%fused_computation.9 | convolution fusion | flops 9663676416 | bytes 27262976 | tf_op jit(solution)/shard_map/kij,ksjl->ksil/dot_general | solution.py:21
  85.0 11.1 %select_multiply_fusion.1 = f32[6,256,256]{2,1,0:T(8,128)} fusion(f32[8,256,256]{2,1,0:T(8,128)S(1)} %copy-done.1, f32[8,6,256,256]{2,3,0,1:T(8,128)S(1)} %fusion.6, pred[6,256]{1,0:T(8,128)(4,1)S(1)} %get-tuple-element.9, pred[6,256]{1,0:T(8,128)(4,1)S(1)} %get-tuple-element.10), kind=kOutput, calls=%fused_computation.12 | convolution fusion | flops 9664856064 | bytes 16256000 | tf_op jit(solution)/shard_map/ksil,kml->sim/dot_general | solution.py:22
  96.0 0.0 all-reduce.3.cloned.1.call-update
  96.0 0.2 all-gather.5.cloned.1.call-start
  96.3 62.0 %all-reduce.3.cloned.1.call-done = f32[6,256,256]{2,1,0:T(8,128)} async-done(((f32[6,256,256]{2,1,0:T(8,128)}), f32[6,256,256]{2,1,0:T(8,128)}) %all-reduce.3.cloned.1.call-update) | async-done | bytes 1572880 | tf_op jit(solution)/shard_map/psum | solution.py:38
  158.3 3.1 %multiply_reduce_fusion.1 = (f32[]{:T(128)}, f32[]{:T(128)}) fusion(f32[6,256,256]{2,1,0:T(8,128)} %all-reduce.3.cloned.1.call-done, f32[6,256,256]{2,1,0:T(8,128)} %param.8, pred[6,256]{1,0:T(8,128)(4,1)S(1)} %get-tuple-element.9, pred[6,256]{1,0:T(8,128)(4,1)S(1)} %get-tuple-element.10), kind=kLoop, calls=%fused_computation.20 | loop fusion | flops 2752510 | bytes 3148808 | tf_op jit(solution)/shard_map/reduce_sum | solution.py:40
  161.4 5.6 %all-reduce = (f32[]{:T(128)}, f32[]{:T(128)}) all-reduce(f32[]{:T(128)} %get-tuple-element.4, f32[]{:T(128)} %get-tuple-element.3), channel_id=1, replica_groups=mesh['grp'=2,'op'=4,'sec'=2,'rep'=2] {'sec'}, use_global_device_ids=true, to_apply=%region_2.4 | all-reduce | flops 2 | bytes 16 | tf_op jit(solution)/shard_map/psum | solution.py:39
  168.3 4.1 %multiply_reduce_fusion = (f32[]{:T(128)}, f32[6,256,256]{2,1,0:T(8,128)}) fusion(f32[6,256,256]{2,1,0:T(8,128)} %all-reduce.3.cloned.1.call-done, f32[]{:T(128)S(6)} %div.12, f32[6,256,256]{2,1,0:T(8,128)} %param.8, pred[6,256]{1,0:T(8,128)(4,1)S(1)} %get-tuple-element.9, pred[6,256]{1,0:T(8,128)(4,1)S(1)} %get-tuple-element.10), kind=kLoop, calls=%fused_computation.18 | loop fusion | flops 2752511 | bytes 4721672 | tf_op jit(solution)/shard_map/reduce_sum | solution.py:44
  172.4 5.5 %psum.31 = f32[]{:T(128)} all-reduce(f32[]{:T(128)} %get-tuple-element.7), channel_id=1, replica_groups=mesh['grp'=2,'op'=4,'sec'=2,'rep'=2] {'sec'}, use_global_device_ids=true, to_apply=%region_6.8 | all-reduce | flops 1 | bytes 8 | tf_op jit(solution)/shard_map/psum | solution.py:44
  178.6 2.7 broadcast_divide_fusion
  181.4 0.0 all-gather.5.cloned.1.call-update
  181.4 0.0 reduce-scatter.2.cloned.1.call-start
  181.4 44.0 %all-gather.5.cloned.1.call-done = f32[12,256,256]{2,1,0:T(8,128)} async-done(((f32[6,256,256]{2,1,0:T(8,128)}), f32[12,256,256]{2,1,0:T(8,128)}) %all-gather.5.cloned.1.call-update) | async-done | bytes 3145744 | tf_op jit(solution)/shard_map/all_gather | solution.py:18
  225.4 9.5 %gather_fusion.1 = f32[48,256,256]{2,1,0:T(8,128)} fusion(f32[12,256,256]{2,1,0:T(8,128)} %all-gather.5.cloned.1.call-done, s32[1024]{0:T(1024)S(1)} %pad_clamp_fusion), kind=kCustom, calls=%fused_computation.2 | custom fusion | bytes 25166016 | tf_op jit(solution)/shard_map/gather | solution.py:20
  235.0 15.8 %fusion.4 = f32[8,6,256,256]{2,3,0,1:T(8,128)S(1)} fusion(f32[8,6,256,256]{3,2,1,0:T(8,128)} %bitcast.34, f32[8,256,256]{2,1,0:T(8,128)S(1)} %copy-done), kind=kOutput, calls=%fused_computation.7 | convolution fusion | flops 9663676416 | bytes 27262976 | tf_op jit(solution)/shard_map/kij,ksjl->ksil/dot_general | solution.py:21
  250.8 11.1 %select_multiply_fusion = f32[6,256,256]{2,1,0:T(8,128)} fusion(f32[8,256,256]{2,1,0:T(8,128)S(1)} %copy-done.2, f32[8,6,256,256]{2,3,0,1:T(8,128)S(1)} %fusion.4, pred[6,256]{1,0:T(8,128)(4,1)S(1)} %get-tuple-element.9, pred[6,256]{1,0:T(8,128)(4,1)S(1)} %get-tuple-element.10), kind=kOutput, calls=%fused_computation.11 | convolution fusion | flops 9664856064 | bytes 16256000 | tf_op jit(solution)/shard_map/ksil,kml->sim/dot_general | solution.py:22
  261.9 1.6 constant_dynamic-slice_fusion
  263.5 32.8 %reduce-scatter.2.cloned.1.call-done = f32[6,32,256]{2,1,0:T(8,128)} async-done(((f32[6,256,256]{2,1,0:T(8,128)}), f32[6,32,256]{2,1,0:T(8,128)}) %reduce-scatter.2.cloned.1.call-update) | async-done | bytes 196624 | tf_op jit(solution)/shard_map/reduce_scatter | solution.py:48
  (13 shorter events, 0.1 us)
Async XLA Ops:
  7.2 62.0 %copy-start = (f32[8,256,256]{2,1,0:T(8,128)S(1)}, f32[8,256,256]{2,1,0:T(8,128)}, u32[]{:S(2)}) copy-start(f32[8,256,256]{2,1,0:T(8,128)} %param.9) | copy-start | bytes 6291460
  7.2 52.4 %all-gather.3.cloned.1.call-start = ((), (), s32[]{:S(2)}) async-start(), calls=%async_computation.1 | async-start | bytes 4718592 | tf_op jit(solution)/shard_map/all_gather | solution.py:18
  8.9 2.9 copy-start.3
  11.8 146.5 %all-reduce.3.cloned.1.call-start = ((), (), s32[]{:S(2)}) async-start(), calls=%async_computation.2 | async-start | bytes 3145728 | tf_op jit(solution)/shard_map/psum | solution.py:38
  69.2 15.8 %copy-start.1 = (f32[8,256,256]{2,1,0:T(8,128)S(1)}, f32[8,256,256]{2,1,0:T(8,128)}, u32[]{:S(2)}) copy-start(f32[8,256,256]{2,1,0:T(8,128)} %param.10) | copy-start | bytes 6291460
  96.0 129.4 %all-gather.5.cloned.1.call-start = ((), (), s32[]{:S(2)}) async-start(), calls=%async_computation.3 | async-start | bytes 4718592 | tf_op jit(solution)/shard_map/all_gather | solution.py:18
  181.4 114.9 %reduce-scatter.2.cloned.1.call-start = ((), (), s32[]{:S(2)}) async-start(), calls=%async_computation.4 | async-start | bytes 1769472 | tf_op jit(solution)/shard_map/reduce_scatter | solution.py:48
  235.0 15.8 %copy-start.2 = (f32[8,256,256]{2,1,0:T(8,128)S(1)}, f32[8,256,256]{2,1,0:T(8,128)}, u32[]{:S(2)}) copy-start(f32[8,256,256]{2,1,0:T(8,128)} %param.10) | copy-start | bytes 6291460
Sparse Core Ops, SparseCore 0:
  11.9 47.6 all-gather.2
  96.2 62.0 all-reduce.2
  181.5 43.8 all-gather.4
  262.0 34.2 reduce-scatter.1
where the time goes:
time: 303 us
  waiting for transfers between devices  186 us (61%)
  matrix products  53.7 us (18%)
  local copies, waits for them, and re-layouts  23.1 us (8%)
  between operations  15.9 us (5%)
  other arithmetic  12.9 us (4%)
  blocking collectives  11.1 us (4%)
    all_gather x2, waiting for transfers between devices, local_terms(): gathered = lax.all_gather(field, 'sec', axis=0, tiled=True)  90.9 us
    psum x1, waiting for transfers between devices, on_device(): sigma_first = lax.psum(partial_first, ('op', 'rep'))  62 us
    reduce_scatter x1, waiting for transfers between devices, on_device(): lax.psum_scatter(partial_next, ('op', 'rep'), scatter_dimension=1, tiled=...  32.8 us
    dot_general x2, matrix products, local_terms(): jnp.einsum('kij,ksjl->ksil', left_operators, picked, precision=lax.Precis...  31.5 us
    dot_general x2, matrix products, local_terms(): jnp.einsum('ksil,kml->sim', halfway, right_operators, precision=lax.Preci...  22.1 us
    gather x2, local copies, waits for them, and re-layouts, local_terms(): picked = gathered[sources]  19.1 us
  transfers between devices with their start and end apart: 4, of which 4 were waited for; matrix products, arithmetic and copies ran while one was open for 1% of the time, Pallas kernels for 0%

commit v1 on v0

v1 whole, which is shorter than its diff:
```python
import functools

import jax
import jax.numpy as jnp
from jax import lax
from jax.experimental import pallas as pl
from jax.experimental.pallas import tpu as pltpu
from jax.sharding import PartitionSpec as P

F32 = jnp.float32
BF16 = jnp.bfloat16
CONTRACT_LAST = (((1,), (1,)), ((), ()))
CONTRACT_FIRST = (((1,), (0,)), ((), ()))
EVERYONE = ("grp", "op", "sec", "rep")


def halves(value):
    high = value.astype(BF16)
    low = (value - high.astype(F32)).astype(BF16)
    return high, low


def wide_left(pair, width):
    high, low = pair[:, :width], pair[:, width:]
    return jnp.concatenate([high, high, low], axis=1)


def wide_right(pair, width, axis):
    high, low = pair[:, :width], pair[:, width:]
    return jnp.concatenate([high, low, high], axis=axis)


class Plan:
    def __init__(self, mesh_shape, wavefunction, operators, coupling):
        self.grp, self.op, self.sec, self.rep = (mesh_shape[a] for a in EVERYONE)
        self.half = self.op // 2
        self.own, self.width = wavefunction.shape[0], wavefunction.shape[1]
        self.terms = operators.shape[0]
        self.sectors = coupling.shape[1]
        self.rows = self.width // (self.op * self.rep)
        self.part = self.width // 2

    def perm(self, move):
        def flat(g, o, s, r):
            return ((g * self.op + o) * self.sec + s) * self.rep + r

        pairs = []
        for g in range(self.grp):
            for o in range(self.op):
                for s in range(self.sec):
                    for r in range(self.rep):
                        to = move(o, s, r)
                        if to is not None:
                            pairs.append((flat(g, o, s, r), flat(g, *to)))
        return pairs

    def across_cores(self, x):
        return lax.ppermute(x, EVERYONE, self.perm(lambda o, s, r: (o, s, 1 - r)))

    def next_sec(self, x):
        return lax.ppermute(x, EVERYONE, self.perm(lambda o, s, r: (o, (s + 1) % self.sec, r)))

    def next_in_half(self, x):
        def move(o, s, r):
            base = o // self.half * self.half
            return (base + (o - base + 1) % self.half, s, r)

        return lax.ppermute(x, EVERYONE, self.perm(move))

    def flip_op(self, x, bits):
        return lax.ppermute(x, EVERYONE, self.perm(lambda o, s, r: (o ^ bits, s, r)))

    def flip_sec(self, x, bits):
        return lax.ppermute(x, EVERYONE, self.perm(lambda o, s, r: (o, s ^ bits, r)))

    def onward(self, x):
        to = {0: 2, 2: 3, 3: 1, 1: 0}
        return lax.ppermute(x, EVERYONE, self.perm(lambda o, s, r: (to[o], s, r)))


def places(plan):
    op = lax.axis_index("op")
    return lax.div(op, plan.half), lax.rem(op, plan.half), lax.axis_index("sec"), lax.axis_index("rep")


def invert_rows(plan, coupling, inverse):
    for k in range(plan.terms):
        for s in range(plan.sectors):
            inverse[k, coupling[k, s]] = s


def prepare_left(plan, half_at, operators, a_pair):
    w, h = plan.width, plan.part
    for k in range(plan.terms):
        high, low = halves(operators[k, pl.ds(half_at, h), :])
        a_pair[k, :, :w], a_pair[k, :, w:] = high, low
        high, low = halves(operators[k, :, pl.ds(half_at, h)].T)
        a_pair[plan.terms + k, :, :w], a_pair[plan.terms + k, :, w:] = high, low


def prepare_right(plan, operators, b_pair):
    w = plan.width
    for k in range(plan.terms):
        high, low = halves(operators[k])
        b_pair[k, :, :w], b_pair[k, :, w:] = high, low


def apply_terms(plan, my_sec, coupling, inverse, a_pair, b_pair, s_pair, u_pair, total):
    w, h, terms, own = plan.width, plan.part, plan.terms, plan.own
    total[...] = jnp.zeros_like(total)

    def first_stage(t, carry):
        weights = wide_right(s_pair[t], w, 1)
        for side in range(2):
            left = a_pair[side * terms:(side + 1) * terms].reshape(terms * h, 2 * w)
            got = lax.dot_general(wide_left(left, w), weights, CONTRACT_LAST, preferred_element_type=F32)
            high, low = halves(got)
            for k in range(terms):
                at = pl.ds(pl.multiple_of(t * h, h), h)
                u_pair[side * terms + k, at, :w] = high[k * h:(k + 1) * h]
                u_pair[side * terms + k, at, w:] = low[k * h:(k + 1) * h]
        return carry

    lax.fori_loop(0, own, first_stage, 0)

    def second_stage(k, carry):
        first_own = my_sec * own
        left = wide_left(u_pair[k], w)
        got = lax.dot_general(left, wide_right(b_pair[k], w, 1), CONTRACT_LAST, preferred_element_type=F32)
        for t in range(own):
            total[inverse[k, first_own + t]] += got[t * h:(t + 1) * h]
        left = wide_left(u_pair[terms + k], w)
        got = lax.dot_general(left, wide_right(b_pair[k], w, 0), CONTRACT_FIRST, preferred_element_type=F32)
        for t in range(own):
            total[coupling[k, first_own + t]] += got[t * h:(t + 1) * h]
        return carry

    lax.fori_loop(0, terms, second_stage, 0)


def hand_out(plan, total, row_sizes, col_sizes, keep, send):
    side, mine, my_sec, my_rep = places(plan)
    row_id = lax.broadcasted_iota(jnp.int32, (plan.rows, plan.width), 0)
    col_id = lax.broadcasted_iota(jnp.int32, (plan.rows, plan.width), 1)
    for sec_off in range(plan.sec):
        for op_off in range(plan.half):
            for rep_off in range(plan.rep):
                at = (lax.rem(mine + op_off, plan.half) * plan.rep + lax.rem(my_rep + rep_off, plan.rep)) * plan.rows
                at = pl.multiple_of(at, plan.rows)
                goal = send if rep_off else keep
                for t in range(plan.own):
                    s = lax.rem(my_sec + sec_off, plan.sec) * plan.own + t
                    ok = (row_id + (side * plan.part + at) < row_sizes[s]) & (col_id < col_sizes[s])
                    goal[sec_off, op_off, t] = jnp.where(ok, total[s, pl.ds(at, plan.rows), :], 0.0)


def start_loads(pairs, sems):
    copies = [pltpu.make_async_copy(src, dst, sems.at[i]) for i, (src, dst) in enumerate(pairs)]
    for copy in copies:
        copy.start()
    return copies


def first_kernel(plan, coupling, left_sizes, right_sizes, wave, left_ops, right_ops,
                 keep, send, turned, piece,
                 wave_in, left_in, right_in, a_pair, b_pair, s_pair, u_pair, total, inverse, sems):
    side, mine, my_sec, my_rep = places(plan)
    copies = start_loads([(wave, wave_in), (right_ops, right_in), (left_ops, left_in)], sems)
    invert_rows(plan, coupling, inverse)
    w = plan.width
    copies[0].wait()
    row_id = lax.broadcasted_iota(jnp.int32, (w, w), 0)
    col_id = lax.broadcasted_iota(jnp.int32, (w, w), 1)
    at = pl.multiple_of((lax.axis_index("op") * plan.rep + my_rep) * plan.rows, plan.rows)
    for t in range(plan.own):
        s = my_sec * plan.own + t
        ok = (row_id < left_sizes[s]) & (col_id < right_sizes[s])
        masked = jnp.where(ok, wave_in[t], 0.0)
        high, low = halves(masked)
        s_pair[t, :, :w], s_pair[t, :, w:] = high, low
        turned[t] = masked.T
        piece[t] = turned[t, pl.ds(at, plan.rows), :]
    copies[1].wait()
    prepare_left(plan, pl.multiple_of(side * plan.part, plan.part), right_in, a_pair)
    copies[2].wait()
    prepare_right(plan, left_in, b_pair)
    apply_terms(plan, my_sec, coupling, inverse, a_pair, b_pair, s_pair, u_pair, total)
    hand_out(plan, total, right_sizes, left_sizes, keep, send)


def second_kernel(plan, coupling, left_sizes, right_sizes, scalars, turned, left_ops, right_ops, *rest):
    units, rest = rest[:2 * plan.op], rest[2 * plan.op:]
    (keep, send, residual, norm,
     turned_in, left_in, right_in, source, a_pair, b_pair, s_pair, u_pair, total, inverse, sems) = rest
    side, mine, my_sec, my_rep = places(plan)
    my_op = lax.axis_index("op")
    copies = start_loads([(turned, turned_in), (left_ops, left_in), (right_ops, right_in)], sems)
    invert_rows(plan, coupling, inverse)
    w, rows = plan.width, plan.rows

    for whose in range(2):
        for bits in range(plan.op):
            unit = units[whose * plan.op + bits]
            r = my_rep if whose == 0 else 1 - my_rep
            at = pl.multiple_of(((my_op ^ bits) * plan.rep + r) * rows, rows)
            for t in range(plan.own):
                source[t, pl.ds(at, rows), :] = unit[t]

    energy, level = scalars[0], scalars[1]
    copies[0].wait()
    at = pl.multiple_of((mine * plan.rep + my_rep) * rows, rows)
    half_at = pl.multiple_of(side * plan.part, plan.part)
    squares = jnp.zeros((8, w), F32)
    for t in range(plan.own):
        res = source[t] - energy * turned_in[t]
        squares = squares + jnp.sum((res * res).reshape(w // 8, 8, w), axis=0)
        source[t] = res
        u_rows = source[t, :, pl.ds(half_at, plan.part)].T
        total[t] = u_rows
        residual[t] = total[t, pl.ds(at, rows), :]
        high, low = halves(res * level)
        s_pair[t, :, :w], s_pair[t, :, w:] = high, low
    norm[...] = jnp.full(norm.shape, jnp.sum(squares), F32)
    copies[1].wait()
    prepare_left(plan, half_at, left_in, a_pair)
    copies[2].wait()
    prepare_right(plan, right_in, b_pair)
    apply_terms(plan, my_sec, coupling, inverse, a_pair, b_pair, s_pair, u_pair, total)
    hand_out(plan, total, left_sizes, right_sizes, keep, send)


def common_scratch(plan):
    w, h = plan.width, plan.part
    return [
        pltpu.VMEM((2 * plan.terms, h, 2 * w), BF16),
        pltpu.VMEM((plan.terms, w, 2 * w), BF16),
        pltpu.VMEM((plan.own, w, 2 * w), BF16),
        pltpu.VMEM((2 * plan.terms, plan.own * h, 2 * w), BF16),
        pltpu.VMEM((plan.sectors, h, w), F32),
        pltpu.SMEM((plan.terms, plan.sectors), jnp.int32),
        pltpu.SemaphoreType.DMA((3,)),
    ]


def sum_over_owners(plan, keep, send):
    both = keep + plan.across_cores(send)
    sums = [None] * plan.sec
    for sec_off in list(range(1, plan.sec)) + [0]:
        run = both[sec_off, plan.half - 1]
        for op_off in range(plan.half - 2, -1, -1):
            run = plan.next_in_half(run) + both[sec_off, op_off]
        sums[sec_off] = run
    run = sums[plan.sec - 1]
    for sec_off in range(plan.sec - 2, -1, -1):
        run = plan.next_sec(run) + sums[sec_off]
    return run


def powers(count):
    return [1 << i for i in range(count.bit_length() - 1)]


def total_of(plan, x):
    x = x + plan.across_cores(x)
    for bits in powers(plan.sec):
        x = x + plan.flip_sec(x, bits)
    for bits in powers(plan.op):
        x = x + plan.flip_op(x, bits)
    return x


def gather_along_op(plan, piece):
    if plan.op == 4:
        far = plan.flip_op(piece, 3)
        near = plan.flip_op(piece, 1)
        op = lax.axis_index("op")
        carried = jnp.where((op == 1) | (op == 2), far, piece)
        return [piece, near, plan.onward(carried), far]
    got = piece[None]
    for bits in powers(plan.op):
        got = jnp.concatenate([got, plan.flip_op(got, bits)])
    return [got[i] for i in range(plan.op)]


def on_device(mesh_shape, wavefunction, left_operators, right_operators, coupling, left_sizes, right_sizes):
    plan = Plan(mesh_shape, wavefunction, left_operators, coupling)
    own, w, rows = plan.own, plan.width, plan.rows
    smem = pl.BlockSpec(memory_space=pltpu.SMEM)
    vmem = pl.BlockSpec(memory_space=pltpu.VMEM)
    anywhere = pl.BlockSpec(memory_space=pl.ANY)
    spread = jax.ShapeDtypeStruct((plan.sec, plan.half, own, rows, w), F32)
    whole = jax.ShapeDtypeStruct((own, w, w), F32)
    chunk = jax.ShapeDtypeStruct((own, rows, w), F32)
    operators = pltpu.VMEM((plan.terms, w, w), F32)
    blocks = pltpu.VMEM((own, w, w), F32)
    flops = 3 * 2 * 2 * 2 * plan.terms * own * plan.part * w * w
    cost = pl.CostEstimate(flops=flops, bytes_accessed=8 << 20, transcendentals=0)
    params = pltpu.CompilerParams(vmem_limit_bytes=40 << 20)

    keep, send, turned, piece = pl.pallas_call(
        functools.partial(first_kernel, plan),
        out_shape=(spread, spread, whole, chunk),
        in_specs=[smem] * 3 + [anywhere] * 3,
        out_specs=(vmem,) * 4,
        scratch_shapes=[blocks, operators, operators] + common_scratch(plan),
        compiler_params=params,
        cost_estimate=cost,
    )(coupling, left_sizes, right_sizes, wavefunction, left_operators, right_operators)

    sigma = sum_over_owners(plan, keep, send)

    units = gather_along_op(plan, sigma)
    units = units + [plan.across_cores(unit) for unit in units]

    entries = plan.sectors * w * w
    tiny = 2.0 ** -32
    sums = [jnp.sum(piece * sigma), jnp.sum(piece * piece), jnp.sum((sigma * tiny) ** 2)]
    sums = total_of(plan, jnp.stack([jnp.full((8, 128), x) for x in sums]))[:, 0, 0]
    energy = sums[0] / sums[1]
    height = 1.0 + jnp.sqrt(sums[2] / entries) / tiny
    scalars = jnp.stack([energy, 1.0 / height])

    keep, send, residual, norm = pl.pallas_call(
        functools.partial(second_kernel, plan),
        out_shape=(spread, spread, chunk, jax.ShapeDtypeStruct((8, 128), F32)),
        in_specs=[smem] * 4 + [anywhere] * 3 + [vmem] * len(units),
        out_specs=(vmem,) * 4,
        scratch_shapes=[blocks, operators, operators, blocks] + common_scratch(plan),
        compiler_params=params,
        cost_estimate=cost,
    )(coupling, left_sizes, right_sizes, scalars, turned, left_operators, right_operators, *units)

    moving = norm
    for _ in range(1, plan.sec):
        moving = plan.next_sec(moving)
        norm = norm + moving
    factor = height / jnp.sqrt(norm[0, 0] / entries + 1e-06)
    sigma_next = sum_over_owners(plan, keep, send) * factor
    return (sigma_next, residual)


def solution(mesh):
    in_specs = (
        P(("grp", "sec"), None, None),
        P(("op", "rep"), None, None),
        P(("op", "rep"), None, None),
        P(("op", "rep"), None),
        P("grp"),
        P("grp"),
    )
    out_specs = (P(("grp", "sec"), ("op", "rep"), None), P(("grp", "sec"), ("op", "rep"), None))
    return jax.shard_map(
        functools.partial(on_device, dict(mesh.shape)),
        mesh=mesh, in_specs=in_specs, out_specs=out_specs, check_vma=False,
    )
```

time: 303 us -> 110 us (0.36)
  waiting for transfers between devices: 186 us -> 34.1 us
  matrix products: 53.7 us -> 0 us
  Pallas kernels: 0 us -> 33.2 us
  starting transfers between devices: 0.34 us -> 23.8 us
  local copies, waits for them, and re-layouts: 23.1 us -> 10.8 us
  between operations: 15.9 us -> 3.63 us
  blocking collectives: 11.1 us -> 0 us
  other arithmetic: 12.9 us -> 3.89 us
    all_gather x2 -> x0, waiting for transfers between devices: 90.9 us -> none  [local_terms(): gathered = lax.all_gather(field, 'sec', axis=0, tiled=True)]
    psum x1 -> x0, waiting for transfers between devices: 62 us -> none  [on_device(): sigma_first = lax.psum(partial_first, ('op', 'rep'))]
    dot_general x4 -> x0, matrix products: 53.7 us -> none  [the longest x2 31.5 us: local_terms(): jnp.einsum('kij,ksjl->ksil', left_operators, picked, precision=lax.Precis...]
    ppermute x0 -> x20, waiting for transfers between devices: none -> 34.1 us  [the longest x4 12.9 us: next_in_half(): return lax.ppermute(x, EVERYONE, self.perm(move))]
    pallas_call x0 -> x2, Pallas kernels: none -> 33.2 us  [the longest x1 17.4 us: on_device(): pl.pallas_call(functools.partial(second_kernel, plan), out_shape=(spread,...]
    reduce_scatter x1 -> x0, waiting for transfers between devices: 32.8 us -> none  [on_device(): lax.psum_scatter(partial_next, ('op', 'rep'), scatter_dimension=1, tiled=...]
    ppermute x0 -> x20, starting transfers between devices: none -> 23.8 us  [the longest x4 6.21 us: flip_op(): lax.ppermute(x, EVERYONE, self.perm(lambda o, s, r: (o ^ bits, s, r)))]
    gather x3 -> x0, local copies, waits for them, and re-layouts: 19.6 us -> none  [the longest x2 19.1 us: local_terms(): picked = gathered[sources]]
  transfers between devices with their start and end apart: 4 -> 20, of which waited for: 4 -> 10; matrix products, arithmetic and copies ran while one was open for 1% -> 1% of each run, Pallas kernels for 0% -> 0%
where the time goes in v1:
time: 110 us; the launch traced here: 109 us
  waiting for transfers between devices  34.1 us (31%)
  Pallas kernels  33.2 us (30%)
  starting transfers between devices  23.8 us (22%)
  local copies, waits for them, and re-layouts  10.8 us (10%)
  other arithmetic  3.89 us (4%)
  between operations  3.63 us (3%)
    pallas_call x1, Pallas kernels, on_device(): pl.pallas_call(functools.partial(second_kernel, plan), out_shape=(spread,...  17.4 us
    pallas_call x1, Pallas kernels, on_device(): pl.pallas_call(functools.partial(first_kernel, plan), out_shape=(spread,...  15.8 us
    ppermute x4, waiting for transfers between devices, next_in_half(): return lax.ppermute(x, EVERYONE, self.perm(move))  12.9 us
    ppermute x4, waiting for transfers between devices, flip_op(): lax.ppermute(x, EVERYONE, self.perm(lambda o, s, r: (o ^ bits, s, r)))  10.7 us
    unnamed x26, local copies, waits for them, and re-layouts  9.6 us
    ppermute x3, waiting for transfers between devices, next_sec(): lax.ppermute(x, EVERYONE, self.perm(lambda o, s, r: (o, (s + 1) % self.se...  6.67 us
    ppermute x4, starting transfers between devices, flip_op(): lax.ppermute(x, EVERYONE, self.perm(lambda o, s, r: (o ^ bits, s, r)))  6.21 us
    ppermute x4, starting transfers between devices, next_in_half(): return lax.ppermute(x, EVERYONE, self.perm(move))  5.69 us
  transfers between devices with their start and end apart: 20, of which 10 were waited for; matrix products, arithmetic and copies ran while one was open for 1% of the time, Pallas kernels for 0%

profile of v1, /device:TPU:0, one launch (start us, length us, event | category | flops | bytes accessed | tf_op | source)
XLA Modules:
  0.0 109.5 jit_solution(16592683008894775514)
XLA Ops:
  0.6 1.6 %copy-done = f32[8,256,256]{2,1,0:T(8,128)S(1)} copy-done((f32[8,256,256]{2,1,0:T(8,128)S(1)}, f32[8,256,256]{2,1,0:T(8,128)}, u32[]{:S(2)}) %copy-start) | copy-done | bytes 2097176
  2.2 1.6 %copy-done.2 = f32[8,256,256]{2,1,0:T(8,128)S(1)} copy-done((f32[8,256,256]{2,1,0:T(8,128)S(1)}, f32[8,256,256]{2,1,0:T(8,128)}, u32[]{:S(2)}) %copy-start.2) | copy-done | bytes 2097176
  3.8 1.4 %copy-done.4 = f32[6,256,256]{2,1,0:T(8,128)S(1)} copy-done((f32[6,256,256]{2,1,0:T(8,128)S(1)}, f32[6,256,256]{2,1,0:T(8,128)}, u32[]{:S(2)}) %copy-start.4) | copy-done | bytes 1572888
  5.2 0.7 copy-done.5
  5.9 0.7 copy-done.7
  6.6 0.7 copy-done.9
  7.2 15.8 %shard_map.77 = (f32[2,2,6,32,256]{4,3,2,1,0:T(8,128)S(1)}, f32[2,2,6,32,256]{4,3,2,1,0:T(8,128)S(1)}, f32[6,256,256]{2,1,0:T(8,128)S(1)}, f32[6,32,256]{2,1,0:T(8,128)S(1)}) custom-call(s32[8,12]{1,0:T(8,128)S(1)} %copy-done.5, s32[12]{0:T(128)S(1)} %copy-done.7, s32[12]{0:T(128)S(1)} %copy-done.9, f32[6,256,256]{2,1,0:T(8,128)S(1)} %copy-done.4, ...), custom_call_target="tpu_custom_call" | custom-call | flops 9663676416 | bytes 8388608 | tf_op jit(solution)/shard_map/pallas_call | solution.py:300
  23.5 1.9 %collective-permute-done = f32[2,2,6,32,256]{4,3,2,1,0:T(8,128)S(1)} collective-permute-done((f32[2,2,6,32,256]{4,3,2,1,0:T(8,128)S(1)}, f32[2,2,6,32,256]{4,3,2,1,0:T(8,128)S(1)}, u32[]{:S(2)}, u32[]{:S(2)}) %collective-permute-start) | collective-permute-done | bytes 786464 | tf_op jit(solution)/shard_map/ppermute | solution.py:58
  25.6 3.0 %collective-permute-start.1 = (f32[6,32,256]{2,1,0:T(8,128)S(1)}, f32[6,32,256]{2,1,0:T(8,128)S(1)}, u32[]{:S(2)}, u32[]{:S(2)}) collective-permute-start(f32[6,32,256]{2,1,0:T(8,128)S(1)} %get-tuple-element.25), channel_id=1, source_target_pairs={{0,4},{1,5},{2,6},{3,7},{4,0},{5,1},{6,2},{7,3},{8,12},{9,13},{10,... | collective-permute-start | bytes 589832 | tf_op jit(solution)/shard_map/ppermute | solution.py:68
  28.7 5.6 %collective-permute-done.1 = f32[6,32,256]{2,1,0:T(8,128)S(1)} collective-permute-done((f32[6,32,256]{2,1,0:T(8,128)S(1)}, f32[6,32,256]{2,1,0:T(8,128)S(1)}, u32[]{:S(2)}, u32[]{:S(2)}) %collective-permute-start.1) | collective-permute-done | bytes 196640 | tf_op jit(solution)/shard_map/ppermute | solution.py:68
  34.4 2.0 %collective-permute-start.2 = (f32[6,32,256]{2,1,0:T(8,128)S(1)}, f32[6,32,256]{2,1,0:T(8,128)S(1)}, u32[]{:S(2)}, u32[]{:S(2)}) collective-permute-start(f32[6,32,256]{2,1,0:T(8,128)S(1)} %fusion.6), channel_id=1, source_target_pairs={{0,2},{1,3},{2,0},{3,1},{4,6},{5,7},{6,4},{7,5},{8,10},{9,11},{10,... | collective-permute-start | bytes 589832 | tf_op jit(solution)/shard_map/ppermute | solution.py:61
  36.4 1.7 %collective-permute-done.3 = f32[6,32,256]{2,1,0:T(8,128)S(1)} collective-permute-done((f32[6,32,256]{2,1,0:T(8,128)S(1)}, f32[6,32,256]{2,1,0:T(8,128)S(1)}, u32[]{:S(2)}, u32[]{:S(2)}) %collective-permute-start.3) | collective-permute-done | bytes 196640 | tf_op jit(solution)/shard_map/ppermute | solution.py:68
  38.1 2.3 %collective-permute-done.2 = f32[6,32,256]{2,1,0:T(8,128)S(1)} collective-permute-done((f32[6,32,256]{2,1,0:T(8,128)S(1)}, f32[6,32,256]{2,1,0:T(8,128)S(1)}, u32[]{:S(2)}, u32[]{:S(2)}) %collective-permute-start.2) | collective-permute-done | bytes 196640 | tf_op jit(solution)/shard_map/ppermute | solution.py:61
  40.4 0.7 multiply_reduce_fusion.2
  41.1 1.9 %maximum_maximum_fusion = f32[3]{0:T(128)S(1)} fusion(f32[1]{0:T(128)} %bitcast.14, f32[1]{0:T(128)} %bitcast.13, f32[1]{0:T(128)} %bitcast.12), kind=kLoop, calls=%fused_computation.20 | loop fusion | flops 6 | bytes 24 | tf_op jit(solution)/shard_map/stack | solution.py:318
  43.1 3.8 %collective-permute-start.9 = (f32[6,32,256]{2,1,0:T(8,128)S(1)}, f32[6,32,256]{2,1,0:T(8,128)S(1)}, u32[]{:S(2)}, u32[]{:S(2)}) collective-permute-start(f32[6,32,256]{2,1,0:T(8,128)S(1)} %get-tuple-element.21.rest_0_), channel_id=1, source_target_pairs={{0,12},{1,13},{2,14},{3,15},{4,8},{5,9},{6,10},{7,11},{8,4},{9,5},... | collective-permute-start | bytes 589832 | tf_op jit(solution)/shard_map/ppermute | solution.py:71
  47.0 1.5 %collective-permute-start.5 = (f32[3,8,128]{2,1,0:T(8,128)S(1)}, f32[3,8,128]{2,1,0:T(8,128)S(1)}, u32[]{:S(2)}, u32[]{:S(2)}) collective-permute-start(f32[3,8,128]{2,1,0:T(8,128)S(1)} %broadcast_add_fusion), channel_id=1, source_target_pairs={{0,2},{1,3},{2,0},{3,1},{4,6},{5,7},{6,4},{7,5},{8,10},{9,11},{10,... | collective-permute-start | bytes 36872 | tf_op jit(solution)/shard_map/ppermute | solution.py:74
  48.5 4.3 %collective-permute-done.9.rest_3_ = f32[6,32,256]{2,1,0:T(8,128)S(1)} collective-permute-done((f32[6,32,256]{2,1,0:T(8,128)S(1)}, f32[6,32,256]{2,1,0:T(8,128)S(1)}, u32[]{:S(2)}, u32[]{:S(2)}) %collective-permute-start.9) | collective-permute-done | bytes 196640 | tf_op jit(solution)/shard_map/ppermute | solution.py:71
  52.8 4.7 %collective-permute-start.10 = (f32[6,32,256]{2,1,0:T(8,128)S(1)}, f32[6,32,256]{2,1,0:T(8,128)S(1)}, u32[]{:S(2)}, u32[]{:S(2)}) collective-permute-start(f32[6,32,256]{2,1,0:T(8,128)S(1)} %broadcast_select_fusion), channel_id=1, source_target_pairs={{0,8},{1,9},{2,10},{3,11},{4,0},{5,1},{6,2},{7,3},{8,12},{9,13},{1... | collective-permute-start | bytes 589832 | tf_op jit(solution)/shard_map/ppermute | solution.py:78
  57.6 4.2 %collective-permute-done.6 = f32[3,8,128]{2,1,0:T(8,128)S(1)} collective-permute-done((f32[3,8,128]{2,1,0:T(8,128)S(1)}, f32[3,8,128]{2,1,0:T(8,128)S(1)}, u32[]{:S(2)}, u32[]{:S(2)}) %collective-permute-start.6) | collective-permute-done | bytes 12320 | tf_op jit(solution)/shard_map/ppermute | solution.py:71
  61.8 2.4 %collective-permute-start.7 = (f32[3,8,128]{2,1,0:T(8,128)S(1)}, f32[3,8,128]{2,1,0:T(8,128)S(1)}, u32[]{:S(2)}, u32[]{:S(2)}) collective-permute-start(f32[3,8,128]{2,1,0:T(8,128)S(1)} %add.55), channel_id=1, source_target_pairs={{0,8},{1,9},{2,10},{3,11},{4,12},{5,13},{6,14},{7,15},{8,0},{9,1},... | collective-permute-start | bytes 36872 | tf_op jit(solution)/shard_map/ppermute | solution.py:71
  64.2 2.2 %collective-permute-done.7 = f32[3,8,128]{2,1,0:T(8,128)S(1)} collective-permute-done((f32[3,8,128]{2,1,0:T(8,128)S(1)}, f32[3,8,128]{2,1,0:T(8,128)S(1)}, u32[]{:S(2)}, u32[]{:S(2)}) %collective-permute-start.7) | collective-permute-done | bytes 12320 | tf_op jit(solution)/shard_map/ppermute | solution.py:71
  67.0 0.6 fusion.8
  69.8 1.6 %copy-done.3 = f32[8,256,256]{2,1,0:T(8,128)S(1)} copy-done((f32[8,256,256]{2,1,0:T(8,128)S(1)}, f32[8,256,256]{2,1,0:T(8,128)}, u32[]{:S(2)}) %copy-start.3) | copy-done | bytes 2097176
  71.4 1.4 %copy-done.12 = f32[6,256,256]{2,1,0:T(8,128)S(1)} copy-done((f32[6,256,256]{2,1,0:T(8,128)S(1)}, f32[6,256,256]{2,1,0:T(8,128)}, u32[]{:S(2)}) %copy-start.12) | copy-done | bytes 1572888
  72.8 17.4 %shard_map.78 = (f32[2,2,6,32,256]{4,3,2,1,0:T(8,128)S(1)}, f32[2,2,6,32,256]{4,3,2,1,0:T(8,128)S(1)}, f32[6,32,256]{2,1,0:T(8,128)}, f32[8,128]{1,0:T(8,128)S(1)}) custom-call(s32[8,12]{1,0:T(8,128)S(1)} %copy-done.6, s32[12]{0:T(128)S(1)} %copy-done.8, s32[12]{0:T(128)S(1)} %copy-done.10, f32[2]{0:T(128)S(1)} %pad_maximum_fusion.scalars, ...), custom_call_target="tpu_custom_call" | custom-call | flops 9663676416 | bytes 8388608 | tf_op jit(solution)/shard_map/pallas_call | solution.py:323
  90.7 1.9 %collective-permute-done.15 = f32[2,2,6,32,256]{4,3,2,1,0:T(8,128)S(1)} collective-permute-done((f32[2,2,6,32,256]{4,3,2,1,0:T(8,128)S(1)}, f32[2,2,6,32,256]{4,3,2,1,0:T(8,128)S(1)}, u32[]{:S(2)}, u32[]{:S(2)}) %collective-permute-start.15) | collective-permute-done | bytes 786464 | tf_op jit(solution)/shard_map/ppermute | solution.py:58
  92.8 2.5 %collective-permute-start.16 = (f32[6,32,256]{2,1,0:T(8,128)S(1)}, f32[6,32,256]{2,1,0:T(8,128)S(1)}, u32[]{:S(2)}, u32[]{:S(2)}) collective-permute-start(f32[6,32,256]{2,1,0:T(8,128)S(1)} %get-tuple-element.23), channel_id=1, source_target_pairs={{0,4},{1,5},{2,6},{3,7},{4,0},{5,1},{6,2},{7,3},{8,12},{9,13},{10,... | collective-permute-start | bytes 589832 | tf_op jit(solution)/shard_map/ppermute | solution.py:68
  95.4 5.7 %collective-permute-done.16 = f32[6,32,256]{2,1,0:T(8,128)S(1)} collective-permute-done((f32[6,32,256]{2,1,0:T(8,128)S(1)}, f32[6,32,256]{2,1,0:T(8,128)S(1)}, u32[]{:S(2)}, u32[]{:S(2)}) %collective-permute-start.16) | collective-permute-done | bytes 196640 | tf_op jit(solution)/shard_map/ppermute | solution.py:68
  101.1 1.6 %collective-permute-start.17 = (f32[6,32,256]{2,1,0:T(8,128)S(1)}, f32[6,32,256]{2,1,0:T(8,128)S(1)}, u32[]{:S(2)}, u32[]{:S(2)}) collective-permute-start(f32[6,32,256]{2,1,0:T(8,128)S(1)} %fusion.3), channel_id=1, source_target_pairs={{0,2},{1,3},{2,0},{3,1},{4,6},{5,7},{6,4},{7,5},{8,10},{9,11},{10,... | collective-permute-start | bytes 589832 | tf_op jit(solution)/shard_map/ppermute | solution.py:61
  103.2 4.4 %collective-permute-done.19 = f32[8,128]{1,0:T(8,128)S(1)} collective-permute-done((f32[8,128]{1,0:T(8,128)S(1)}, f32[8,128]{1,0:T(8,128)S(1)}, u32[]{:S(2)}, u32[]{:S(2)}) %collective-permute-start.19) | collective-permute-done | bytes 4128 | tf_op jit(solution)/shard_map/ppermute | solution.py:61
  108.8 0.7 fusion.2
  (55 shorter events, 3.5 us)
Async XLA Ops:
  0.6 1.6 %copy-start = (f32[8,256,256]{2,1,0:T(8,128)S(1)}, f32[8,256,256]{2,1,0:T(8,128)}, u32[]{:S(2)}) copy-start(f32[8,256,256]{2,1,0:T(8,128)} %left_ops.3) | copy-start | bytes 6291460
  2.2 1.6 %copy-start.2 = (f32[8,256,256]{2,1,0:T(8,128)S(1)}, f32[8,256,256]{2,1,0:T(8,128)}, u32[]{:S(2)}) copy-start(f32[8,256,256]{2,1,0:T(8,128)} %right_ops.3) | copy-start | bytes 6291460
  3.8 1.4 %copy-start.4 = (f32[6,256,256]{2,1,0:T(8,128)S(1)}, f32[6,256,256]{2,1,0:T(8,128)}, u32[]{:S(2)}) copy-start(f32[6,256,256]{2,1,0:T(8,128)} %wave.1) | copy-start | bytes 4718596
  5.2 0.7 copy-start.5
  5.9 0.7 copy-start.7
  23.0 18.1 %copy-start.11 = (f32[6,256,256]{2,1,0:T(8,128)}, f32[6,256,256]{2,1,0:T(8,128)S(1)}, u32[]{:S(2)}) copy-start(f32[6,256,256]{2,1,0:T(8,128)S(1)} %get-tuple-element.13.turned) | copy-start | bytes 4718596
  23.0 2.4 %collective-permute-start = (f32[2,2,6,32,256]{4,3,2,1,0:T(8,128)S(1)}, f32[2,2,6,32,256]{4,3,2,1,0:T(8,128)S(1)}, u32[]{:S(2)}, u32[]{:S(2)}) collective-permute-start(f32[2,2,6,32,256]{4,3,2,1,0:T(8,128)S(1)} %get-tuple-element.12), channel_id=1, source_target_pairs={{0,1},{1,0},{2,3},{3,2},{4,5},{5,4},{6,7},{7,6},{8,9},{9,8},{10,11... | collective-permute-start | bytes 2359304 | tf_op jit(solution)/shard_map/ppermute | solution.py:58
  25.6 44.2 %copy-start.1 = (f32[8,256,256]{2,1,0:T(8,128)S(1)}, f32[8,256,256]{2,1,0:T(8,128)}, u32[]{:S(2)}) copy-start(f32[8,256,256]{2,1,0:T(8,128)} %left_ops.3) | copy-start | bytes 6291460
  25.6 44.2 %copy-start.6 = (s32[8,12]{1,0:T(8,128)S(1)}, s32[8,12]{1,0:T(8,128)}, u32[]{:S(2)}) copy-start(s32[8,12]{1,0:T(8,128)} %coupling.3) | copy-start | bytes 1156
  25.6 44.2 %copy-start.8 = (s32[12]{0:T(128)S(1)}, s32[12]{0:T(128)}, u32[]{:S(2)}) copy-start(s32[12]{0:T(128)} %left_sizes.3) | copy-start | bytes 148
  25.6 44.2 %copy-start.10 = (s32[12]{0:T(128)S(1)}, s32[12]{0:T(128)}, u32[]{:S(2)}) copy-start(s32[12]{0:T(128)} %right_sizes.3) | copy-start | bytes 148
  25.6 8.7 %collective-permute-start.1 = (f32[6,32,256]{2,1,0:T(8,128)S(1)}, f32[6,32,256]{2,1,0:T(8,128)S(1)}, u32[]{:S(2)}, u32[]{:S(2)}) collective-permute-start(f32[6,32,256]{2,1,0:T(8,128)S(1)} %get-tuple-element.25), channel_id=1, source_target_pairs={{0,4},{1,5},{2,6},{3,7},{4,0},{5,1},{6,2},{7,3},{8,12},{9,13},{10,... | collective-permute-start | bytes 589832 | tf_op jit(solution)/shard_map/ppermute | solution.py:68
  28.7 9.4 %collective-permute-start.3 = (f32[6,32,256]{2,1,0:T(8,128)S(1)}, f32[6,32,256]{2,1,0:T(8,128)S(1)}, u32[]{:S(2)}, u32[]{:S(2)}) collective-permute-start(f32[6,32,256]{2,1,0:T(8,128)S(1)} %get-tuple-element.24), channel_id=1, source_target_pairs={{0,4},{1,5},{2,6},{3,7},{4,0},{5,1},{6,2},{7,3},{8,12},{9,13},{10,... | collective-permute-start | bytes 589832 | tf_op jit(solution)/shard_map/ppermute | solution.py:68
  34.4 6.0 %collective-permute-start.2 = (f32[6,32,256]{2,1,0:T(8,128)S(1)}, f32[6,32,256]{2,1,0:T(8,128)S(1)}, u32[]{:S(2)}, u32[]{:S(2)}) collective-permute-start(f32[6,32,256]{2,1,0:T(8,128)S(1)} %fusion.6), channel_id=1, source_target_pairs={{0,2},{1,3},{2,0},{3,1},{4,6},{5,7},{6,4},{7,5},{8,10},{9,11},{10,... | collective-permute-start | bytes 589832 | tf_op jit(solution)/shard_map/ppermute | solution.py:61
  43.1 3.9 %collective-permute-start.4 = (f32[3,8,128]{2,1,0:T(8,128)S(1)}, f32[3,8,128]{2,1,0:T(8,128)S(1)}, u32[]{:S(2)}, u32[]{:S(2)}) collective-permute-start(f32[3,8,128]{2,1,0:T(8,128)S(1)} %broadcast.4), channel_id=1, source_target_pairs={{0,1},{1,0},{2,3},{3,2},{4,5},{5,4},{6,7},{7,6},{8,9},{9,8},{10,11... | collective-permute-start | bytes 36872 | tf_op jit(solution)/shard_map/ppermute | solution.py:58
  43.1 9.7 %collective-permute-start.9 = (f32[6,32,256]{2,1,0:T(8,128)S(1)}, f32[6,32,256]{2,1,0:T(8,128)S(1)}, u32[]{:S(2)}, u32[]{:S(2)}) collective-permute-start(f32[6,32,256]{2,1,0:T(8,128)S(1)} %get-tuple-element.21.rest_0_), channel_id=1, source_target_pairs={{0,12},{1,13},{2,14},{3,15},{4,8},{5,9},{6,10},{7,11},{8,4},{9,5},... | collective-permute-start | bytes 589832 | tf_op jit(solution)/shard_map/ppermute | solution.py:71
  47.0 19.5 %collective-permute-start.8 = (f32[6,32,256]{2,1,0:T(8,128)S(1)}, f32[6,32,256]{2,1,0:T(8,128)S(1)}, u32[]{:S(2)}, u32[]{:S(2)}) collective-permute-start(f32[6,32,256]{2,1,0:T(8,128)S(1)} %get-tuple-element.21.rest_0_), channel_id=1, source_target_pairs={{0,4},{1,5},{2,6},{3,7},{4,0},{5,1},{6,2},{7,3},{8,12},{9,13},{10,... | collective-permute-start | bytes 589832 | tf_op jit(solution)/shard_map/ppermute | solution.py:71
  47.0 10.5 %collective-permute-start.5 = (f32[3,8,128]{2,1,0:T(8,128)S(1)}, f32[3,8,128]{2,1,0:T(8,128)S(1)}, u32[]{:S(2)}, u32[]{:S(2)}) collective-permute-start(f32[3,8,128]{2,1,0:T(8,128)S(1)} %broadcast_add_fusion), channel_id=1, source_target_pairs={{0,2},{1,3},{2,0},{3,1},{4,6},{5,7},{6,4},{7,5},{8,10},{9,11},{10,... | collective-permute-start | bytes 36872 | tf_op jit(solution)/shard_map/ppermute | solution.py:74
  52.8 14.1 %collective-permute-start.10 = (f32[6,32,256]{2,1,0:T(8,128)S(1)}, f32[6,32,256]{2,1,0:T(8,128)S(1)}, u32[]{:S(2)}, u32[]{:S(2)}) collective-permute-start(f32[6,32,256]{2,1,0:T(8,128)S(1)} %broadcast_select_fusion), channel_id=1, source_target_pairs={{0,8},{1,9},{2,10},{3,11},{4,0},{5,1},{6,2},{7,3},{8,12},{9,13},{1... | collective-permute-start | bytes 589832 | tf_op jit(solution)/shard_map/ppermute | solution.py:78
  57.6 4.2 %collective-permute-start.6 = (f32[3,8,128]{2,1,0:T(8,128)S(1)}, f32[3,8,128]{2,1,0:T(8,128)S(1)}, u32[]{:S(2)}, u32[]{:S(2)}) collective-permute-start(f32[3,8,128]{2,1,0:T(8,128)S(1)} %fusion.9), channel_id=1, source_target_pairs={{0,4},{1,5},{2,6},{3,7},{4,0},{5,1},{6,2},{7,3},{8,12},{9,13},{10,... | collective-permute-start | bytes 36872 | tf_op jit(solution)/shard_map/ppermute | solution.py:71
  61.8 4.6 %collective-permute-start.7 = (f32[3,8,128]{2,1,0:T(8,128)S(1)}, f32[3,8,128]{2,1,0:T(8,128)S(1)}, u32[]{:S(2)}, u32[]{:S(2)}) collective-permute-start(f32[3,8,128]{2,1,0:T(8,128)S(1)} %add.55), channel_id=1, source_target_pairs={{0,8},{1,9},{2,10},{3,11},{4,12},{5,13},{6,14},{7,15},{8,0},{9,1},... | collective-permute-start | bytes 36872 | tf_op jit(solution)/shard_map/ppermute | solution.py:71
  64.2 5.6 %collective-permute-start.11 = (f32[6,32,256]{2,1,0:T(8,128)S(1)}, f32[6,32,256]{2,1,0:T(8,128)S(1)}, u32[]{:S(2)}, u32[]{:S(2)}) collective-permute-start(f32[6,32,256]{2,1,0:T(8,128)S(1)} %get-tuple-element.21.rest_0_), channel_id=1, source_target_pairs={{0,1},{1,0},{2,3},{3,2},{4,5},{5,4},{6,7},{7,6},{8,9},{9,8},{10,11... | collective-permute-start | bytes 589832 | tf_op jit(solution)/shard_map/ppermute | solution.py:58
  66.4 3.4 %collective-permute-start.14 = (f32[6,32,256]{2,1,0:T(8,128)S(1)}, f32[6,32,256]{2,1,0:T(8,128)S(1)}, u32[]{:S(2)}, u32[]{:S(2)}) collective-permute-start(f32[6,32,256]{2,1,0:T(8,128)S(1)} %collective-permute-done.9.rest_3_), channel_id=1, source_target_pairs={{0,1},{1,0},{2,3},{3,2},{4,5},{5,4},{6,7},{7,6},{8,9},{9,8},{10,11... | collective-permute-start | bytes 589832 | tf_op jit(solution)/shard_map/ppermute | solution.py:58
  66.4 3.3 %collective-permute-start.12 = (f32[6,32,256]{2,1,0:T(8,128)S(1)}, f32[6,32,256]{2,1,0:T(8,128)S(1)}, u32[]{:S(2)}, u32[]{:S(2)}) collective-permute-start(f32[6,32,256]{2,1,0:T(8,128)S(1)} %collective-permute-done.8.rest_1_), channel_id=1, source_target_pairs={{0,1},{1,0},{2,3},{3,2},{4,5},{5,4},{6,7},{7,6},{8,9},{9,8},{10,11... | collective-permute-start | bytes 589832 | tf_op jit(solution)/shard_map/ppermute | solution.py:58
  66.9 2.8 %collective-permute-start.13 = (f32[6,32,256]{2,1,0:T(8,128)S(1)}, f32[6,32,256]{2,1,0:T(8,128)}, u32[]{:S(2)}, u32[]{:S(2)}) collective-permute-start(f32[6,32,256]{2,1,0:T(8,128)S(1)} %collective-permute-done.10.rest_2_), channel_id=1, source_target_pairs={{0,1},{1,0},{2,3},{3,2},{4,5},{5,4},{6,7},{7,6},{8,9},{9,8},{10,11... | collective-permute-start | bytes 589832 | tf_op jit(solution)/shard_map/ppermute | solution.py:58
  69.8 1.6 %copy-start.3 = (f32[8,256,256]{2,1,0:T(8,128)S(1)}, f32[8,256,256]{2,1,0:T(8,128)}, u32[]{:S(2)}) copy-start(f32[8,256,256]{2,1,0:T(8,128)} %right_ops.3) | copy-start | bytes 6291460
  71.4 1.4 %copy-start.12 = (f32[6,256,256]{2,1,0:T(8,128)S(1)}, f32[6,256,256]{2,1,0:T(8,128)}, u32[]{:S(2)}) copy-start(f32[6,256,256]{2,1,0:T(8,128)} %copy-done.11) | copy-start | bytes 4718596
  90.2 2.4 %collective-permute-start.15 = (f32[2,2,6,32,256]{4,3,2,1,0:T(8,128)S(1)}, f32[2,2,6,32,256]{4,3,2,1,0:T(8,128)S(1)}, u32[]{:S(2)}, u32[]{:S(2)}) collective-permute-start(f32[2,2,6,32,256]{4,3,2,1,0:T(8,128)S(1)} %get-tuple-element.15), channel_id=1, source_target_pairs={{0,1},{1,0},{2,3},{3,2},{4,5},{5,4},{6,7},{7,6},{8,9},{9,8},{10,11... | collective-permute-start | bytes 2359304 | tf_op jit(solution)/shard_map/ppermute | solution.py:58
  92.8 8.3 %collective-permute-start.16 = (f32[6,32,256]{2,1,0:T(8,128)S(1)}, f32[6,32,256]{2,1,0:T(8,128)S(1)}, u32[]{:S(2)}, u32[]{:S(2)}) collective-permute-start(f32[6,32,256]{2,1,0:T(8,128)S(1)} %get-tuple-element.23), channel_id=1, source_target_pairs={{0,4},{1,5},{2,6},{3,7},{4,0},{5,1},{6,2},{7,3},{8,12},{9,13},{10,... | collective-permute-start | bytes 589832 | tf_op jit(solution)/shard_map/ppermute | solution.py:68
  95.3 13.4 %collective-permute-start.18 = (f32[6,32,256]{2,1,0:T(8,128)S(1)}, f32[6,32,256]{2,1,0:T(8,128)S(1)}, u32[]{:S(2)}, u32[]{:S(2)}) collective-permute-start(f32[6,32,256]{2,1,0:T(8,128)S(1)} %get-tuple-element.22), channel_id=1, source_target_pairs={{0,4},{1,5},{2,6},{3,7},{4,0},{5,1},{6,2},{7,3},{8,12},{9,13},{10,... | collective-permute-start | bytes 589832 | tf_op jit(solution)/shard_map/ppermute | solution.py:68
  101.1 7.7 %collective-permute-start.17 = (f32[6,32,256]{2,1,0:T(8,128)S(1)}, f32[6,32,256]{2,1,0:T(8,128)S(1)}, u32[]{:S(2)}, u32[]{:S(2)}) collective-permute-start(f32[6,32,256]{2,1,0:T(8,128)S(1)} %fusion.3), channel_id=1, source_target_pairs={{0,2},{1,3},{2,0},{3,1},{4,6},{5,7},{6,4},{7,5},{8,10},{9,11},{10,... | collective-permute-start | bytes 589832 | tf_op jit(solution)/shard_map/ppermute | solution.py:61
  102.7 4.8 %collective-permute-start.19 = (f32[8,128]{1,0:T(8,128)S(1)}, f32[8,128]{1,0:T(8,128)S(1)}, u32[]{:S(2)}, u32[]{:S(2)}) collective-permute-start(f32[8,128]{1,0:T(8,128)S(1)} %get-tuple-element.16), channel_id=1, source_target_pairs={{0,2},{1,3},{2,0},{3,1},{4,6},{5,7},{6,4},{7,5},{8,10},{9,11},{10,... | collective-permute-start | bytes 12296 | tf_op jit(solution)/shard_map/ppermute | solution.py:61
  (1 other events, 0.7 us)

commit v2 on v0

v2 whole, which is shorter than its diff:
```python
import functools

import jax
import jax.numpy as jnp
from jax import lax
from jax.experimental import pallas as pl
from jax.experimental.pallas import tpu as pltpu
from jax.sharding import PartitionSpec as P

F32 = jnp.float32
BF16 = jnp.bfloat16
CONTRACT_LAST = (((1,), (1,)), ((), ()))
CONTRACT_FIRST = (((1,), (0,)), ((), ()))
EVERYONE = ("grp", "op", "sec", "rep")
TINY = 2.0 ** -32
TILE = 8


def halves(value):
    high = value.astype(BF16)
    low = (value - high.astype(F32)).astype(BF16)
    return high, low


def put_halves(goal, at, value):
    width = value.shape[-1]
    goal[at + (slice(0, width),)], goal[at + (slice(width, 2 * width),)] = halves(value)


def wide_left(pair, width):
    high, low = pair[:, :width], pair[:, width:]
    return jnp.concatenate([high, high, low], axis=1)


def wide_right(pair, width, axis):
    high, low = pair[:, :width], pair[:, width:]
    return jnp.concatenate([high, low, high], axis=axis)


def powers(count):
    return [1 << i for i in range(count.bit_length() - 1)]


class Plan:
    def __init__(self, mesh_shape, wavefunction, operators, coupling):
        self.grp, self.op, self.sec, self.rep = (mesh_shape[a] for a in EVERYONE)
        self.half = self.op // 2
        self.own, self.width = wavefunction.shape[0], wavefunction.shape[1]
        self.terms = operators.shape[0]
        self.sectors = coupling.shape[1]
        self.rows = self.width // (self.op * self.rep)
        self.block = self.rows * self.rep
        self.part = self.width // 2
        self.away = self.block * (self.half - 1)
        self.piece = self.own * self.rows

    def perm(self, move):
        def flat(g, o, s, r):
            return ((g * self.op + o) * self.sec + s) * self.rep + r

        pairs = []
        for g in range(self.grp):
            for o in range(self.op):
                for s in range(self.sec):
                    for r in range(self.rep):
                        pairs.append((flat(g, o, s, r), flat(g, *move(o, s, r))))
        return pairs

    def across_cores(self, x):
        return lax.ppermute(x, EVERYONE, self.perm(lambda o, s, r: (o, s, 1 - r)))

    def next_sec(self, x):
        return lax.ppermute(x, EVERYONE, self.perm(lambda o, s, r: (o, (s + 1) % self.sec, r)))

    def next_in_half(self, x):
        def move(o, s, r):
            base = o // self.half * self.half
            return (base + (o - base + 1) % self.half, s, r)

        return lax.ppermute(x, EVERYONE, self.perm(move))

    def flip_op(self, x, bits):
        return lax.ppermute(x, EVERYONE, self.perm(lambda o, s, r: (o ^ bits, s, r)))

    def flip_sec(self, x, bits):
        return lax.ppermute(x, EVERYONE, self.perm(lambda o, s, r: (o, s ^ bits, r)))

    def onward(self, x):
        to = {0: 2, 2: 3, 3: 1, 1: 0}
        return lax.ppermute(x, EVERYONE, self.perm(lambda o, s, r: (to[o], s, r)))


def places(plan):
    op = lax.axis_index("op")
    return lax.div(op, plan.half), lax.rem(op, plan.half), lax.axis_index("sec"), lax.axis_index("rep")


def prepare(plan, left_in, right_in, flipped, a_away, a_home, b_pair, ready):
    side, mine, _, _ = places(plan)
    half_at = pl.multiple_of(side * plan.part, plan.part)
    ready(0)
    for k in range(plan.terms):
        flipped[k] = left_in[k, :, pl.ds(half_at, plan.part)].T
    for off in range(plan.half):
        at = pl.multiple_of(lax.rem(mine + off, plan.half) * plan.block, plan.block)
        goal = a_away if off else a_home
        start = (off - 1) * plan.block if off else 0
        rows = slice(start, start + plan.block)
        for k in range(plan.terms):
            straight = left_in[k, pl.ds(pl.multiple_of(half_at + at, plan.block), plan.block), :]
            put_halves(goal, (k, rows), straight)
            put_halves(goal, (plan.terms + k, rows), flipped[k, pl.ds(at, plan.block), :])
    ready(1)
    for k in range(plan.terms):
        put_halves(b_pair, (k, slice(None)), right_in[k])


def apply_terms(plan, coupling, inverse, a_pair, b_pair, s_pair, u_pair, total):
    w, terms, own = plan.width, plan.terms, plan.own
    n = a_pair.shape[1]
    first_own = lax.axis_index("sec") * own
    for k in range(terms):
        for s in range(plan.sectors):
            inverse[k, coupling[k, s]] = s
    total[...] = jnp.zeros_like(total)
    left = wide_left(a_pair[...].reshape(2 * terms * n, 2 * w), w)
    for t in range(own):
        got = lax.dot_general(left, wide_right(s_pair[t], w, 1), CONTRACT_LAST, preferred_element_type=F32)
        high, low = halves(got)
        for k in range(2 * terms):
            u_pair[k, t * n:(t + 1) * n, :w] = high[k * n:(k + 1) * n]
            u_pair[k, t * n:(t + 1) * n, w:] = low[k * n:(k + 1) * n]

    unroll = 8 if terms % 8 == 0 else 1

    def second_stage(i, carry):
        for j in range(unroll):
            k = i * unroll + j
            got = lax.dot_general(wide_left(u_pair[k], w), wide_right(b_pair[k], w, 1), CONTRACT_LAST,
                                  preferred_element_type=F32)
            for t in range(own):
                total[inverse[k, first_own + t]] += got[t * n:(t + 1) * n]
            got = lax.dot_general(wide_left(u_pair[terms + k], w), wide_right(b_pair[k], w, 0), CONTRACT_FIRST,
                                  preferred_element_type=F32)
            for t in range(own):
                total[coupling[k, first_own + t]] += got[t * n:(t + 1) * n]
        return carry

    lax.fori_loop(0, terms // unroll, second_stage, 0)


def hand_out(plan, offsets, total, row_sizes, col_sizes, keep, send):
    side, mine, my_sec, my_rep = places(plan)
    rows = plan.rows
    row_id = lax.broadcasted_iota(jnp.int32, (rows, plan.width), 0)
    col_id = lax.broadcasted_iota(jnp.int32, (rows, plan.width), 1)
    for sec_off in range(plan.sec):
        for i, op_off in enumerate(offsets):
            for rep_off in range(plan.rep):
                inner = pl.multiple_of(lax.rem(my_rep + rep_off, plan.rep) * rows, rows)
                first_row = side * plan.part + lax.rem(mine + op_off, plan.half) * plan.block + inner
                goal = send if rep_off else keep
                for t in range(plan.own):
                    s = lax.rem(my_sec + sec_off, plan.sec) * plan.own + t
                    ok = (row_id + first_row < row_sizes[s]) & (col_id < col_sizes[s])
                    value = total[s, pl.ds(pl.multiple_of(i * plan.block + inner, rows), rows), :]
                    goal[sec_off, i, t * rows:(t + 1) * rows] = jnp.where(ok, value, 0.0)


def first_kernel(plan, coupling, left_sizes, right_sizes, wave, left_ops, right_ops,
                 keep, send, turned, piece, a_home, b_pair, s_pair,
                 wave_in, left_in, right_in, flipped, a_away, u_pair, total, inverse, sems):
    _, _, my_sec, my_rep = places(plan)
    w = plan.width
    loads = ((wave, wave_in), (right_ops, right_in), (left_ops, left_in))
    copies = [pltpu.make_async_copy(src, dst, sems.at[i]) for i, (src, dst) in enumerate(loads)]
    for copy in copies:
        copy.start()
    copies[0].wait()
    row_id = lax.broadcasted_iota(jnp.int32, (w, w), 0)
    col_id = lax.broadcasted_iota(jnp.int32, (w, w), 1)
    at = pl.multiple_of((lax.axis_index("op") * plan.rep + my_rep) * plan.rows, plan.rows)
    for t in range(plan.own):
        s = my_sec * plan.own + t
        ok = (row_id < left_sizes[s]) & (col_id < right_sizes[s])
        masked = jnp.where(ok, wave_in[t], 0.0)
        put_halves(s_pair, (t, slice(None)), masked)
        turned[t] = masked.T
        piece[t * plan.rows:(t + 1) * plan.rows] = turned[t, pl.ds(at, plan.rows), :]
    prepare(plan, right_in, left_in, flipped, a_away, a_home, b_pair, lambda i: copies[1 + i].wait())
    apply_terms(plan, coupling, inverse, a_away, b_pair, s_pair, u_pair, total)
    hand_out(plan, range(1, plan.half), total, right_sizes, left_sizes, keep, send)


def home_kernel(plan, coupling, row_sizes, col_sizes, a_home, b_pair, s_pair, keep, send, u_pair, total, inverse):
    apply_terms(plan, coupling, inverse, a_home, b_pair, s_pair, u_pair, total)
    hand_out(plan, range(1), total, row_sizes, col_sizes, keep, send)


def prepare_kernel(plan, left_ops, right_ops, a_away, a_home, b_pair, flipped):
    prepare(plan, left_ops, right_ops, flipped, a_away, a_home, b_pair, lambda i: None)


def second_kernel(plan, coupling, left_sizes, right_sizes, turned, a_away, b_pair, *rest):
    units, rest = rest[:2 * plan.op], rest[2 * plan.op:]
    (keep, send, s_pair, residual, norm, source, flipped, u_pair, total, inverse) = rest
    side, mine, _, my_rep = places(plan)
    my_op = lax.axis_index("op")
    w, rows = plan.width, plan.rows
    sums = jnp.zeros((TILE, w), F32)
    for whose in range(2):
        for bits in range(plan.op):
            unit = units[whose * plan.op + bits]
            r = my_rep if whose == 0 else 1 - my_rep
            at = pl.multiple_of(((my_op ^ bits) * plan.rep + r) * rows, rows)
            for t in range(plan.own):
                source[t, pl.ds(at, rows), :] = unit[t * rows:(t + 1) * rows]
            sums = sums + unit[plan.piece:]
    entries = plan.sectors * w * w
    sums = jnp.broadcast_to(jnp.sum(sums, axis=1, keepdims=True), sums.shape)
    energy = sums[0:1] / sums[1:2]
    height = 1.0 + jnp.sqrt(sums[2:3] / entries) / TINY
    level = 1.0 / height
    at = pl.multiple_of((mine * plan.rep + my_rep) * rows, rows)
    half_at = pl.multiple_of(side * plan.part, plan.part)
    squares = jnp.zeros((8, w), F32)
    for t in range(plan.own):
        res = source[t] - energy * turned[t]
        squares = squares + jnp.sum((res * res).reshape(w // 8, 8, w), axis=0)
        source[t] = res
        put_halves(s_pair, (t, slice(None)), res * level)
    for t in range(plan.own):
        flipped[t] = source[t, :, pl.ds(half_at, plan.part)].T
        residual[t] = flipped[t, pl.ds(at, rows), :]
    norm[0:4] = jnp.full((4, w), jnp.sum(squares), F32)
    norm[4:8] = jnp.broadcast_to(height, (4, w))
    apply_terms(plan, coupling, inverse, a_away, b_pair, s_pair, u_pair, total)
    hand_out(plan, range(1, plan.half), total, left_sizes, right_sizes, keep, send)


def sums_tile(products, squares, shares):
    rows = [sum(jnp.sum(x, axis=0, keepdims=True) for x in part) for part in (products, squares, shares)]
    return jnp.concatenate(rows + [jnp.zeros((TILE - 3,) + rows[0].shape[1:], F32)])


def gather_along_op(plan, piece, beside):
    if plan.op == 4:
        far = plan.flip_op(piece, 3)
        near = plan.flip_op(piece, 1)
        op = lax.axis_index("op")
        far, beside = lax.optimization_barrier((far, beside))
        carried = jnp.where((op == 1) | (op == 2), far, piece)
        return [piece, near, plan.onward(carried), far], beside
    got = piece[None]
    for bits in powers(plan.op):
        got = jnp.concatenate([got, plan.flip_op(got, bits)])
    return [got[i] for i in range(plan.op)], beside


def on_device(mesh_shape, wavefunction, left_operators, right_operators, coupling, left_sizes, right_sizes):
    plan = Plan(mesh_shape, wavefunction, left_operators, coupling)
    own, w, rows, terms = plan.own, plan.width, plan.rows, plan.terms
    smem = pl.BlockSpec(memory_space=pltpu.SMEM)
    vmem = pl.BlockSpec(memory_space=pltpu.VMEM)
    hbm = pl.BlockSpec(memory_space=pltpu.HBM)

    def spread(offsets):
        return jax.ShapeDtypeStruct((plan.sec, offsets, plan.piece, w), F32)

    def work(n):
        return [
            pltpu.VMEM((2 * terms, own * n, 2 * w), BF16),
            pltpu.VMEM((plan.sectors, n, w), F32),
            pltpu.SMEM((terms, plan.sectors), jnp.int32),
        ]

    def call(body, n, out_shape, in_specs, scratch, grant=36):
        flops = 3 * 2 * 2 * 2 * terms * own * n * w * w
        return pl.pallas_call(
            functools.partial(body, plan),
            out_shape=out_shape,
            in_specs=in_specs,
            out_specs=(vmem,) * len(out_shape),
            scratch_shapes=scratch,
            compiler_params=pltpu.CompilerParams(vmem_limit_bytes=grant << 20),
            cost_estimate=pl.CostEstimate(flops=flops, bytes_accessed=4 << 20, transcendentals=0),
        )

    blocks = jax.ShapeDtypeStruct((own, w, w), F32)
    block_pairs = jax.ShapeDtypeStruct((own, w, 2 * w), BF16)
    lefts_away = jax.ShapeDtypeStruct((2 * terms, plan.away, 2 * w), BF16)
    lefts_home = jax.ShapeDtypeStruct((2 * terms, plan.block, 2 * w), BF16)
    rights = jax.ShapeDtypeStruct((terms, w, 2 * w), BF16)
    chunk = jax.ShapeDtypeStruct((plan.piece, w), F32)
    operators = pltpu.VMEM((terms, w, w), F32)
    turned_operators = pltpu.VMEM((terms, plan.part, w), F32)
    home = call(home_kernel, plan.block, (spread(1),) * 2, [smem] * 3 + [vmem] * 3, work(plan.block))

    def along_half(keep, send, home_args, beside=()):
        away = keep + plan.across_cores(send)
        away, home_args = lax.optimization_barrier((away, home_args))
        run = away[:, plan.half - 2]
        for i in range(plan.half - 3, -1, -1):
            run = plan.next_in_half(run) + away[:, i]
        run = plan.next_in_half(run)
        home_keep, home_send = home(*home_args)
        home_send, beside = lax.optimization_barrier((home_send, beside))
        return run + (home_keep + plan.across_cores(home_send))[:, 0], beside

    def along_sec(sums, extra):
        run = sums[plan.sec - 1]
        if plan.sec == 2:
            return jnp.concatenate([sums[0], extra]) + plan.next_sec(jnp.concatenate([run, extra]))
        for i in range(plan.sec - 2, -1, -1):
            run = plan.next_sec(run) + sums[i]
        for bits in powers(plan.sec):
            extra = extra + plan.flip_sec(extra, bits)
        return jnp.concatenate([run, extra])

    keep, send, turned, piece, a_home, b_pair, s_pair = call(
        first_kernel, plan.away,
        (spread(plan.half - 1),) * 2 + (blocks, chunk, lefts_home, rights, block_pairs),
        [smem] * 3 + [hbm] * 3,
        [pltpu.VMEM(blocks.shape, F32), operators, operators, turned_operators,
         pltpu.VMEM(lefts_away.shape, BF16)] + work(plan.away) + [pltpu.SemaphoreType.DMA((3,))],
        grant=48,
    )(coupling, left_sizes, right_sizes, wavefunction, left_operators, right_operators)

    pieces = [piece]
    for _ in range(1, plan.sec):
        pieces.append(plan.next_sec(pieces[-1]))
    pieces = [pieces[-i % plan.sec] for i in range(plan.sec)]
    sums, pieces = along_half(keep, send, (coupling, right_sizes, left_sizes, a_home, b_pair, s_pair), pieces)
    extra = sums_tile(
        [pieces[i] * sums[i] for i in range(plan.sec)], [piece * piece],
        [(sums[i] * TINY) ** 2 for i in range(plan.sec)],
    )
    unit = along_sec(sums, extra)

    unit, left_again, right_again = lax.optimization_barrier((unit, left_operators, right_operators))
    prepared = call(
        prepare_kernel, 1, (lefts_away, lefts_home, rights), [vmem] * 2, [turned_operators],
    )(left_again, right_again)
    units, (a_away, a_home, b_pair) = gather_along_op(plan, unit, prepared)
    units = units + [plan.across_cores(x) for x in units]

    keep, send, s_pair, residual, norm = call(
        second_kernel, plan.away,
        (spread(plan.half - 1),) * 2 + (block_pairs, jax.ShapeDtypeStruct((own, rows, w), F32),
                                        jax.ShapeDtypeStruct((TILE, w), F32)),
        [smem] * 3 + [vmem] * (3 + len(units)),
        [pltpu.VMEM(blocks.shape, F32), pltpu.VMEM((own, plan.part, w), F32)] + work(plan.away),
    )(coupling, left_sizes, right_sizes, turned, a_away, b_pair, *units)

    sums, _ = along_half(keep, send, (coupling, left_sizes, right_sizes, a_home, b_pair, s_pair))
    done = along_sec(sums, norm)
    height = norm[4:5]
    entries = plan.sectors * w * w
    factor = height / jnp.sqrt(done[plan.piece:plan.piece + 1] / entries + 1e-06)
    sigma_next = (done[:plan.piece] * factor).reshape(own, rows, w)
    return (sigma_next, residual)


def solution(mesh):
    in_specs = (
        P(("grp", "sec"), None, None),
        P(("op", "rep"), None, None),
        P(("op", "rep"), None, None),
        P(("op", "rep"), None),
        P("grp"),
        P("grp"),
    )
    out_specs = (P(("grp", "sec"), ("op", "rep"), None), P(("grp", "sec"), ("op", "rep"), None))
    return jax.shard_map(
        functools.partial(on_device, dict(mesh.shape)),
        mesh=mesh, in_specs=in_specs, out_specs=out_specs, check_vma=False,
    )
```

time: 303 us -> 81 us (0.27)
  waiting for transfers between devices: 186 us -> 25.9 us
  matrix products: 53.7 us -> 0 us
  Pallas kernels: 0 us -> 30.1 us
  local copies, waits for them, and re-layouts: 23.1 us -> 5.33 us
  starting transfers between devices: 0.34 us -> 17.3 us
  between operations: 15.9 us -> 0.84 us
  other arithmetic: 12.9 us -> 1.21 us
  blocking collectives: 11.1 us -> 0 us
    all_gather x2 -> x0, waiting for transfers between devices: 90.9 us -> none  [local_terms(): gathered = lax.all_gather(field, 'sec', axis=0, tiled=True)]
    psum x1 -> x0, waiting for transfers between devices: 62 us -> none  [on_device(): sigma_first = lax.psum(partial_first, ('op', 'rep'))]
    dot_general x4 -> x0, matrix products: 53.7 us -> none  [the longest x2 31.5 us: local_terms(): jnp.einsum('kij,ksjl->ksil', left_operators, picked, precision=lax.Precis...]
    reduce_scatter x1 -> x0, waiting for transfers between devices: 32.8 us -> none  [on_device(): lax.psum_scatter(partial_next, ('op', 'rep'), scatter_dimension=1, tiled=...]
    pallas_call x0 -> x5, Pallas kernels: none -> 30.1 us  [the longest x2 12 us: along_half(): home_keep, home_send = home(*home_args)]
    ppermute x0 -> x16, waiting for transfers between devices: none -> 25.9 us  [the longest x3 10.2 us: next_sec(): lax.ppermute(x, EVERYONE, self.perm(lambda o, s, r: (o, (s + 1) % self.se...]
    gather x3 -> x0, local copies, waits for them, and re-layouts: 19.6 us -> none  [the longest x2 19.1 us: local_terms(): picked = gathered[sources]]
    ppermute x0 -> x16, starting transfers between devices: none -> 17.3 us  [the longest x3 5.8 us: next_sec(): lax.ppermute(x, EVERYONE, self.perm(lambda o, s, r: (o, (s + 1) % self.se...]
  transfers between devices with their start and end apart: 4 -> 16, of which waited for: 4 -> 8; matrix products, arithmetic and copies ran while one was open for 1% -> 0% of each run, Pallas kernels for 0% -> 16%
where the time goes in v2:
time: 81 us; the launch traced here: 80.7 us
  Pallas kernels  30.1 us (37%)
  waiting for transfers between devices  25.9 us (32%)
  starting transfers between devices  17.3 us (21%)
  local copies, waits for them, and re-layouts  5.33 us (7%)
  other arithmetic  1.21 us (1%)
  between operations  0.84 us (1%)
    pallas_call x2, Pallas kernels, along_half(): home_keep, home_send = home(*home_args)  12 us
    ppermute x3, waiting for transfers between devices, next_sec(): lax.ppermute(x, EVERYONE, self.perm(lambda o, s, r: (o, (s + 1) % self.se...  10.2 us
    pallas_call x1, Pallas kernels, on_device(): call(first_kernel, plan.away, (spread(plan.half - 1),) * 2 + (blocks, chu...  9.88 us
    pallas_call x1, Pallas kernels, on_device(): call(second_kernel, plan.away, (spread(plan.half - 1),) * 2 + (block_pair...  7.24 us
    ppermute x3, starting transfers between devices, next_sec(): lax.ppermute(x, EVERYONE, self.perm(lambda o, s, r: (o, (s + 1) % self.se...  5.8 us
    unnamed x22, local copies, waits for them, and re-layouts  5.2 us
    ppermute x2, waiting for transfers between devices, next_in_half(): return lax.ppermute(x, EVERYONE, self.perm(move))  5.13 us
    ppermute x2, waiting for transfers between devices, flip_op(): lax.ppermute(x, EVERYONE, self.perm(lambda o, s, r: (o ^ bits, s, r)))  4.1 us
  transfers between devices with their start and end apart: 16, of which 8 were waited for; matrix products, arithmetic and copies ran while one was open for 0% of the time, Pallas kernels for 16%

profile of v2, /device:TPU:0, one launch (start us, length us, event | category | flops | bytes accessed | tf_op | source)
XLA Modules:
  0.0 80.7 jit_solution(13520876473426608457)
XLA Ops:
  0.6 0.7 copy-done.2
  1.3 0.7 copy-done.4
  2.0 0.7 copy-done.6
  2.6 9.9 %shard_map.77 = (f32[2,1,192,256]{3,2,1,0:T(8,128)S(1)}, f32[2,1,192,256]{3,2,1,0:T(8,128)S(1)}, f32[6,256,256]{2,1,0:T(8,128)S(1)}, f32[192,256]{1,0:T(8,128)S(...) custom-call(s32[8,12]{1,0:T(8,128)S(1)} %copy-done.2, ...), custom_call_target="tpu_custom_call" | custom-call | flops 4831838208 | bytes 4194304 | tf_op jit(solution)/shard_map/pallas_call | solution.py:320
  12.5 0.5 collective-permute-start
  13.0 2.6 %collective-permute-start.2 = (f32[192,256]{1,0:T(8,128)S(1)}, f32[192,256]{1,0:T(8,128)S(1)}, u32[]{:S(2)}, u32[]{:S(2)}) collective-permute-start(f32[192,256]{1,0:T(8,128)S(1)} %get-tuple-element.62), channel_id=1, source_target_pairs={{0,2},{1,3},{2,0},{3,1},{4,6},{5,7},{6,4},{7,5},{8,10},{9,11},{10,... | collective-permute-start | bytes 589832 | tf_op jit(solution)/shard_map/ppermute | solution.py:73
  15.7 1.8 %collective-permute-start.1 = (f32[2,192,256]{2,1,0:T(8,128)S(1)}, f32[2,192,256]{2,1,0:T(8,128)S(1)}, u32[]{:S(2)}, u32[]{:S(2)}) collective-permute-start(f32[2,192,256]{2,1,0:T(8,128)S(1)} %bitcast.41), channel_id=1, source_target_pairs={{0,4},{1,5},{2,6},{3,7},{4,0},{5,1},{6,2},{7,3},{8,12},{9,13},{10,... | collective-permute-start | bytes 1179656 | tf_op jit(solution)/shard_map/ppermute | solution.py:80
  17.5 1.6 %copy-done.8 = bf16[8,256,512]{2,1,0:T(8,128)(2,1)S(1)} copy-done((bf16[8,256,512]{2,1,0:T(8,128)(2,1)S(1)}, bf16[8,256,512]{2,1,0:T(8,128)(2,1)}, u32[]{:S(2)}) %copy-start.8) | copy-done | bytes 2097176
  19.0 6.0 %shard_map.78 = (f32[2,1,192,256]{3,2,1,0:T(8,128)S(1)}, f32[2,1,192,256]{3,2,1,0:T(8,128)S(1)}) custom-call(s32[8,12]{1,0:T(8,128)S(1)} %copy-done.2, s32[12]{0:T(128)S(1)} %copy-done.6, s32[12]{0:T(128)S(1)} %copy-done.4, bf16[16,64,512]{2,1,0:T(8,128)(2,1)S(1)} %get-tuple-element.55.a_home, bf16[8,256,512]{2,1,0:T(8,128)(2,1)S(1)} %copy-done.8, ...), custom_call_target="tpu_custom_call" | custom-call | flops 4831838208 | bytes 4194304 | tf_op jit(solution)/shard_map/pallas_call | solution.py:306
  25.2 1.7 %collective-permute-done.1 = f32[2,192,256]{2,1,0:T(8,128)S(1)} collective-permute-done((f32[2,192,256]{2,1,0:T(8,128)S(1)}, f32[2,192,256]{2,1,0:T(8,128)S(1)}, u32[]{:S(2)}, u32[]{:S(2)}) %collective-permute-start.1) | collective-permute-done | bytes 393248 | tf_op jit(solution)/shard_map/ppermute | solution.py:80
  27.0 0.1 multiply_reduce_fusion
  27.2 1.7 %collective-permute-start.4 = (f32[200,256]{1,0:T(8,128)S(1)}, f32[200,256]{1,0:T(8,128)S(1)}, u32[]{:S(2)}, u32[]{:S(2)}) collective-permute-start(f32[200,256]{1,0:T(8,128)S(1)} %concatenate.16), channel_id=1, source_target_pairs={{0,2},{1,3},{2,0},{3,1},{4,6},{5,7},{6,4},{7,5},{8,10},{9,11},{10,... | collective-permute-start | bytes 614408 | tf_op jit(solution)/shard_map/ppermute | solution.py:73
  28.9 5.4 %collective-permute-done.4 = f32[200,256]{1,0:T(8,128)S(1)} collective-permute-done((f32[200,256]{1,0:T(8,128)S(1)}, f32[200,256]{1,0:T(8,128)S(1)}, u32[]{:S(2)}, u32[]{:S(2)}) %collective-permute-start.4) | collective-permute-done | bytes 204832 | tf_op jit(solution)/shard_map/ppermute | solution.py:73
  34.4 3.0 %collective-permute-start.5 = (f32[200,256]{1,0:T(8,128)S(1)}, f32[200,256]{1,0:T(8,128)S(1)}, u32[]{:S(2)}, u32[]{:S(2)}) collective-permute-start(f32[200,256]{1,0:T(8,128)S(1)} %add.65.rest_0_), channel_id=1, source_target_pairs={{0,12},{1,13},{2,14},{3,15},{4,8},{5,9},{6,10},{7,11},{8,4},{9,5},... | collective-permute-start | bytes 614408 | tf_op jit(solution)/shard_map/ppermute | solution.py:83
  37.4 0.2 collective-permute-start.6
  37.6 1.6 %copy-done.1 = f32[8,256,256]{2,1,0:T(8,128)S(1)} copy-done((f32[8,256,256]{2,1,0:T(8,128)S(1)}, f32[8,256,256]{2,1,0:T(8,128)}, u32[]{:S(2)}) %copy-start.1) | copy-done | bytes 2097176
  39.2 1.0 %shard_map.79 = (bf16[16,64,512]{2,1,0:T(8,128)(2,1)S(1)}, bf16[16,64,512]{2,1,0:T(8,128)(2,1)S(1)}, bf16[8,256,512]{2,1,0:T(8,128)(2,1)S(1)}) custom-call(f32[8,256,256]{2,1,0:T(8,128)S(1)} %copy-done, f32[8,256,256]{2,1,0:T(8,128)S(1)} %copy-done.1), custom_call_target="tpu_custom_call" | custom-call | flops 75497472 | bytes 4194304 | tf_op jit(solution)/shard_map/pallas_call | solution.py:341
  40.2 4.1 %collective-permute-done.5.rest_3_ = f32[200,256]{1,0:T(8,128)S(1)} collective-permute-done((f32[200,256]{1,0:T(8,128)S(1)}, f32[200,256]{1,0:T(8,128)S(1)}, u32[]{:S(2)}, u32[]{:S(2)}) %collective-permute-start.5) | collective-permute-done | bytes 204832 | tf_op jit(solution)/shard_map/ppermute | solution.py:83
  44.3 3.5 %collective-permute-start.7 = (f32[200,256]{1,0:T(8,128)S(1)}, f32[200,256]{1,0:T(8,128)S(1)}, u32[]{:S(2)}, u32[]{:S(2)}) collective-permute-start(f32[200,256]{1,0:T(8,128)S(1)} %broadcast_select_fusion), channel_id=1, source_target_pairs={{0,8},{1,9},{2,10},{3,11},{4,0},{5,1},{6,2},{7,3},{8,12},{9,13},{1... | collective-permute-start | bytes 614408 | tf_op jit(solution)/shard_map/ppermute | solution.py:90
  47.8 0.5 collective-permute-start.11
  48.3 3.4 %collective-permute-done.7.rest_2_ = f32[200,256]{1,0:T(8,128)S(1)} collective-permute-done((f32[200,256]{1,0:T(8,128)S(1)}, f32[200,256]{1,0:T(8,128)S(1)}, u32[]{:S(2)}, u32[]{:S(2)}) %collective-permute-start.7) | collective-permute-done | bytes 204832 | tf_op jit(solution)/shard_map/ppermute | solution.py:90
  51.8 1.4 %collective-permute-done.10.rest_6_ = f32[200,256]{1,0:T(8,128)S(1)} collective-permute-done((f32[200,256]{1,0:T(8,128)S(1)}, f32[200,256]{1,0:T(8,128)S(1)}, u32[]{:S(2)}, u32[]{:S(2)}) %collective-permute-start.10) | collective-permute-done | bytes 204832 | tf_op jit(solution)/shard_map/ppermute | solution.py:70
  53.2 7.2 %shard_map.80 = (f32[2,1,192,256]{3,2,1,0:T(8,128)S(1)}, f32[2,1,192,256]{3,2,1,0:T(8,128)S(1)}, bf16[6,256,512]{2,1,0:T(8,128)(2,1)S(1)}, f32[6,32,256]{2,1,0:T(8,128)}, f32[8,256]{1,0:T(8,128)S(1)}) custom-call(s32[8,12]{1,0:T(8,128)S(1)} %copy-done.3, s32[12]{0:T(128)S(1)} %copy-done.5, s32[12]{0:T(128)S(1)} %copy-done.7, f32[6,256,256]{2,1,0:T(8,128)S(1)} %copy-done.10, ...), custom_call_target="tpu_custom_call" | custom-call | flops 4831838208 | bytes 4194304 | tf_op jit(solution)/shard_map/pallas_call | solution.py:347
  60.5 0.1 collective-permute-start.12
  60.6 1.6 %collective-permute-done.12 = f32[2,1,192,256]{3,2,0,1:T(8,128)S(1)} collective-permute-done((f32[2,1,192,256]{3,2,0,1:T(8,128)S(1)}, f32[2,1,192,256]{3,2,0,1:T(8,128)S(1)}, u32[]{:S(2)}, u32[]{:S(2)}) %collective-permute-start.12) | collective-permute-done | bytes 393248 | tf_op jit(solution)/shard_map/ppermute | solution.py:70
  62.3 1.7 %collective-permute-start.13 = (f32[2,192,256]{2,1,0:T(8,128)S(1)}, f32[2,192,256]{2,1,0:T(8,128)S(1)}, u32[]{:S(2)}, u32[]{:S(2)}) collective-permute-start(f32[2,192,256]{2,1,0:T(8,128)S(1)} %bitcast.42), channel_id=1, source_target_pairs={{0,4},{1,5},{2,6},{3,7},{4,0},{5,1},{6,2},{7,3},{8,12},{9,13},{10,... | collective-permute-start | bytes 1179656 | tf_op jit(solution)/shard_map/ppermute | solution.py:80
  63.9 6.0 %shard_map.81 = (f32[2,1,192,256]{3,2,1,0:T(8,128)S(1)}, f32[2,1,192,256]{3,2,1,0:T(8,128)S(1)}) custom-call(s32[8,12]{1,0:T(8,128)S(1)} %copy-done.3, s32[12]{0:T(128)S(1)} %copy-done.5, s32[12]{0:T(128)S(1)} %copy-done.7, bf16[16,64,512]{2,1,0:T(8,128)(2,1)S(1)} %get-tuple-element.81.a_home, bf16[8,256,512]{2,1,0:T(8,128)(2,1)S(1)} %get-tuple-element.82.b_pair, ...), custom_call_target="tpu_custom_call" | custom-call | flops 4831838208 | bytes 4194304 | tf_op jit(solution)/shard_map/pallas_call | solution.py:306
  70.0 3.4 %collective-permute-done.13 = f32[2,192,256]{2,1,0:T(8,128)S(1)} collective-permute-done((f32[2,192,256]{2,1,0:T(8,128)S(1)}, f32[2,192,256]{2,1,0:T(8,128)S(1)}, u32[]{:S(2)}, u32[]{:S(2)}) %collective-permute-start.13) | collective-permute-done | bytes 393248 | tf_op jit(solution)/shard_map/ppermute | solution.py:80
  73.5 0.1 bitcast_add_fusion
  73.6 1.6 %collective-permute-start.15 = (f32[200,256]{1,0:T(8,128)S(1)}, f32[200,256]{1,0:T(8,128)S(1)}, u32[]{:S(2)}, u32[]{:S(2)}) collective-permute-start(f32[200,256]{1,0:T(8,128)S(1)} %pad_maximum_fusion), channel_id=1, source_target_pairs={{0,2},{1,3},{2,0},{3,1},{4,6},{5,7},{6,4},{7,5},{8,10},{9,11},{10,... | collective-permute-start | bytes 614408 | tf_op jit(solution)/shard_map/ppermute | solution.py:73
  75.2 4.8 %collective-permute-done.15 = f32[200,256]{1,0:T(8,128)S(1)} collective-permute-done((f32[200,256]{1,0:T(8,128)S(1)}, f32[200,256]{1,0:T(8,128)S(1)}, u32[]{:S(2)}, u32[]{:S(2)}) %collective-permute-start.15) | collective-permute-done | bytes 204832 | tf_op jit(solution)/shard_map/ppermute | solution.py:73
  80.0 0.7 slice_multiply_fusion
  (46 shorter events, 0.7 us)
Async XLA Ops:
  0.6 0.7 copy-start.2
  1.3 0.7 copy-start.4
  2.0 0.7 copy-start.6
  12.5 12.6 %copy-start.9 = (f32[6,256,256]{2,1,0:T(8,128)}, f32[6,256,256]{2,1,0:T(8,128)S(1)}, u32[]{:S(2)}) copy-start(f32[6,256,256]{2,1,0:T(8,128)S(1)} %get-tuple-element.45.turned) | copy-start | bytes 4718596
  12.5 3.1 %collective-permute-start = (f32[2,1,192,256]{3,2,0,1:T(8,128)S(1)}, f32[2,1,192,256]{3,2,0,1:T(8,128)S(1)}, u32[]{:S(2)}, u32[]{:S(2)}) collective-permute-start(f32[2,1,192,256]{3,2,0,1:T(8,128)S(1)} %bitcast.40), channel_id=1, source_target_pairs={{0,1},{1,0},{2,3},{3,2},{4,5},{5,4},{6,7},{7,6},{8,9},{9,8},{10,11... | collective-permute-start | bytes 1179656 | tf_op jit(solution)/shard_map/ppermute | solution.py:70
  13.0 12.0 %collective-permute-start.2 = (f32[192,256]{1,0:T(8,128)S(1)}, f32[192,256]{1,0:T(8,128)S(1)}, u32[]{:S(2)}, u32[]{:S(2)}) collective-permute-start(f32[192,256]{1,0:T(8,128)S(1)} %get-tuple-element.62), channel_id=1, source_target_pairs={{0,2},{1,3},{2,0},{3,1},{4,6},{5,7},{6,4},{7,5},{8,10},{9,11},{10,... | collective-permute-start | bytes 589832 | tf_op jit(solution)/shard_map/ppermute | solution.py:73
  15.7 11.3 %collective-permute-start.1 = (f32[2,192,256]{2,1,0:T(8,128)S(1)}, f32[2,192,256]{2,1,0:T(8,128)S(1)}, u32[]{:S(2)}, u32[]{:S(2)}) collective-permute-start(f32[2,192,256]{2,1,0:T(8,128)S(1)} %bitcast.41), channel_id=1, source_target_pairs={{0,4},{1,5},{2,6},{3,7},{4,0},{5,1},{6,2},{7,3},{8,12},{9,13},{10,... | collective-permute-start | bytes 1179656 | tf_op jit(solution)/shard_map/ppermute | solution.py:80
  17.5 1.6 %copy-start.8 = (bf16[8,256,512]{2,1,0:T(8,128)(2,1)S(1)}, bf16[8,256,512]{2,1,0:T(8,128)(2,1)}, u32[]{:S(2)}) copy-start(bf16[8,256,512]{2,1,0:T(8,128)(2,1)} %get-tuple-element.56.b_pair) | copy-start | bytes 6291460
  25.1 1.8 %collective-permute-start.3 = (f32[2,1,192,256]{3,2,0,1:T(8,128)S(1)}, f32[2,1,192,256]{3,2,0,1:T(8,128)S(1)}, u32[]{:S(2)}, u32[]{:S(2)}) collective-permute-start(f32[2,1,192,256]{3,2,0,1:T(8,128)S(1)} %bitcast.39), channel_id=1, source_target_pairs={{0,1},{1,0},{2,3},{3,2},{4,5},{5,4},{6,7},{7,6},{8,9},{9,8},{10,11... | collective-permute-start | bytes 1179656 | tf_op jit(solution)/shard_map/ppermute | solution.py:70
  26.9 10.7 %copy-start = (f32[8,256,256]{2,1,0:T(8,128)S(1)}, f32[8,256,256]{2,1,0:T(8,128)}, u32[]{:S(2)}) copy-start(f32[8,256,256]{2,1,0:T(8,128)} %left_ops.2) | copy-start | bytes 6291460
  27.2 7.1 %collective-permute-start.4 = (f32[200,256]{1,0:T(8,128)S(1)}, f32[200,256]{1,0:T(8,128)S(1)}, u32[]{:S(2)}, u32[]{:S(2)}) collective-permute-start(f32[200,256]{1,0:T(8,128)S(1)} %concatenate.16), channel_id=1, source_target_pairs={{0,2},{1,3},{2,0},{3,1},{4,6},{5,7},{6,4},{7,5},{8,10},{9,11},{10,... | collective-permute-start | bytes 614408 | tf_op jit(solution)/shard_map/ppermute | solution.py:73
  34.4 9.9 %collective-permute-start.5 = (f32[200,256]{1,0:T(8,128)S(1)}, f32[200,256]{1,0:T(8,128)S(1)}, u32[]{:S(2)}, u32[]{:S(2)}) collective-permute-start(f32[200,256]{1,0:T(8,128)S(1)} %add.65.rest_0_), channel_id=1, source_target_pairs={{0,12},{1,13},{2,14},{3,15},{4,8},{5,9},{6,10},{7,11},{8,4},{9,5},... | collective-permute-start | bytes 614408 | tf_op jit(solution)/shard_map/ppermute | solution.py:83
  37.4 10.9 %collective-permute-start.6 = (f32[200,256]{1,0:T(8,128)S(1)}, f32[200,256]{1,0:T(8,128)S(1)}, u32[]{:S(2)}, u32[]{:S(2)}) collective-permute-start(f32[200,256]{1,0:T(8,128)S(1)} %add.65.rest_0_), channel_id=1, source_target_pairs={{0,4},{1,5},{2,6},{3,7},{4,0},{5,1},{6,2},{7,3},{8,12},{9,13},{10,... | collective-permute-start | bytes 614408 | tf_op jit(solution)/shard_map/ppermute | solution.py:83
  37.6 1.6 %copy-start.1 = (f32[8,256,256]{2,1,0:T(8,128)S(1)}, f32[8,256,256]{2,1,0:T(8,128)}, u32[]{:S(2)}) copy-start(f32[8,256,256]{2,1,0:T(8,128)} %right_ops.2) | copy-start | bytes 6291460
  39.2 14.0 %copy-start.3 = (s32[8,12]{1,0:T(8,128)S(1)}, s32[8,12]{1,0:T(8,128)}, u32[]{:S(2)}) copy-start(s32[8,12]{1,0:T(8,128)} %coupling.5) | copy-start | bytes 1156
  39.2 14.0 %copy-start.5 = (s32[12]{0:T(128)S(1)}, s32[12]{0:T(128)}, u32[]{:S(2)}) copy-start(s32[12]{0:T(128)} %row_sizes.1) | copy-start | bytes 148
  39.2 14.0 %copy-start.7 = (s32[12]{0:T(128)S(1)}, s32[12]{0:T(128)}, u32[]{:S(2)}) copy-start(s32[12]{0:T(128)} %col_sizes.1) | copy-start | bytes 148
  39.2 14.0 %copy-start.10 = (f32[6,256,256]{2,1,0:T(8,128)S(1)}, f32[6,256,256]{2,1,0:T(8,128)}, u32[]{:S(2)}) copy-start(f32[6,256,256]{2,1,0:T(8,128)} %copy-done.9) | copy-start | bytes 4718596
  44.3 7.5 %collective-permute-start.7 = (f32[200,256]{1,0:T(8,128)S(1)}, f32[200,256]{1,0:T(8,128)S(1)}, u32[]{:S(2)}, u32[]{:S(2)}) collective-permute-start(f32[200,256]{1,0:T(8,128)S(1)} %broadcast_select_fusion), channel_id=1, source_target_pairs={{0,8},{1,9},{2,10},{3,11},{4,0},{5,1},{6,2},{7,3},{8,12},{9,13},{1... | collective-permute-start | bytes 614408 | tf_op jit(solution)/shard_map/ppermute | solution.py:90
  47.8 4.0 %collective-permute-start.8 = (f32[200,256]{1,0:T(8,128)S(1)}, f32[200,256]{1,0:T(8,128)S(1)}, u32[]{:S(2)}, u32[]{:S(2)}) collective-permute-start(f32[200,256]{1,0:T(8,128)S(1)} %add.65.rest_0_), channel_id=1, source_target_pairs={{0,1},{1,0},{2,3},{3,2},{4,5},{5,4},{6,7},{7,6},{8,9},{9,8},{10,11... | collective-permute-start | bytes 614408 | tf_op jit(solution)/shard_map/ppermute | solution.py:70
  47.8 4.0 %collective-permute-start.11 = (f32[200,256]{1,0:T(8,128)S(1)}, f32[200,256]{1,0:T(8,128)S(1)}, u32[]{:S(2)}, u32[]{:S(2)}) collective-permute-start(f32[200,256]{1,0:T(8,128)S(1)} %collective-permute-done.5.rest_3_), channel_id=1, source_target_pairs={{0,1},{1,0},{2,3},{3,2},{4,5},{5,4},{6,7},{7,6},{8,9},{9,8},{10,11... | collective-permute-start | bytes 614408 | tf_op jit(solution)/shard_map/ppermute | solution.py:70
  48.3 3.5 %collective-permute-start.9 = (f32[200,256]{1,0:T(8,128)S(1)}, f32[200,256]{1,0:T(8,128)S(1)}, u32[]{:S(2)}, u32[]{:S(2)}) collective-permute-start(f32[200,256]{1,0:T(8,128)S(1)} %collective-permute-done.6.rest_1_), channel_id=1, source_target_pairs={{0,1},{1,0},{2,3},{3,2},{4,5},{5,4},{6,7},{7,6},{8,9},{9,8},{10,11... | collective-permute-start | bytes 614408 | tf_op jit(solution)/shard_map/ppermute | solution.py:70
  51.8 1.5 %collective-permute-start.10 = (f32[200,256]{1,0:T(8,128)S(1)}, f32[200,256]{1,0:T(8,128)S(1)}, u32[]{:S(2)}, u32[]{:S(2)}) collective-permute-start(f32[200,256]{1,0:T(8,128)S(1)} %collective-permute-done.7.rest_2_), channel_id=1, source_target_pairs={{0,1},{1,0},{2,3},{3,2},{4,5},{5,4},{6,7},{7,6},{8,9},{9,8},{10,11... | collective-permute-start | bytes 614408 | tf_op jit(solution)/shard_map/ppermute | solution.py:70
  60.5 1.7 %collective-permute-start.12 = (f32[2,1,192,256]{3,2,0,1:T(8,128)S(1)}, f32[2,1,192,256]{3,2,0,1:T(8,128)S(1)}, u32[]{:S(2)}, u32[]{:S(2)}) collective-permute-start(f32[2,1,192,256]{3,2,0,1:T(8,128)S(1)} %bitcast.38), channel_id=1, source_target_pairs={{0,1},{1,0},{2,3},{3,2},{4,5},{5,4},{6,7},{7,6},{8,9},{9,8},{10,11... | collective-permute-start | bytes 1179656 | tf_op jit(solution)/shard_map/ppermute | solution.py:70
  62.3 11.2 %collective-permute-start.13 = (f32[2,192,256]{2,1,0:T(8,128)S(1)}, f32[2,192,256]{2,1,0:T(8,128)S(1)}, u32[]{:S(2)}, u32[]{:S(2)}) collective-permute-start(f32[2,192,256]{2,1,0:T(8,128)S(1)} %bitcast.42), channel_id=1, source_target_pairs={{0,4},{1,5},{2,6},{3,7},{4,0},{5,1},{6,2},{7,3},{8,12},{9,13},{10,... | collective-permute-start | bytes 1179656 | tf_op jit(solution)/shard_map/ppermute | solution.py:80
  70.0 3.5 %collective-permute-start.14 = (f32[2,1,192,256]{3,2,1,0:T(8,128)S(1)}, f32[2,1,192,256]{3,2,1,0:T(8,128)S(1)}, u32[]{:S(2)}, u32[]{:S(2)}) collective-permute-start(f32[2,1,192,256]{3,2,1,0:T(8,128)S(1)} %get-tuple-element.85), channel_id=1, source_target_pairs={{0,1},{1,0},{2,3},{3,2},{4,5},{5,4},{6,7},{7,6},{8,9},{9,8},{10,11... | collective-permute-start | bytes 1179656 | tf_op jit(solution)/shard_map/ppermute | solution.py:70
  73.6 6.4 %collective-permute-start.15 = (f32[200,256]{1,0:T(8,128)S(1)}, f32[200,256]{1,0:T(8,128)S(1)}, u32[]{:S(2)}, u32[]{:S(2)}) collective-permute-start(f32[200,256]{1,0:T(8,128)S(1)} %pad_maximum_fusion), channel_id=1, source_target_pairs={{0,2},{1,3},{2,0},{3,1},{4,6},{5,7},{6,4},{7,5},{8,10},{9,11},{10,... | collective-permute-start | bytes 614408 | tf_op jit(solution)/shard_map/ppermute | solution.py:73

commit v3 on v2

v3 whole, which is shorter than its diff:
```python
import functools

import jax
import jax.numpy as jnp
from jax import lax
from jax.experimental import pallas as pl
from jax.experimental.pallas import tpu as pltpu
from jax.sharding import PartitionSpec as P

F32 = jnp.float32
BF16 = jnp.bfloat16
CONTRACT_LAST = (((1,), (1,)), ((), ()))
CONTRACT_FIRST = (((1,), (0,)), ((), ()))
EVERYONE = ("grp", "op", "sec", "rep")
TINY = 2.0 ** -32
TILE = 8


def halves(value):
    high = value.astype(BF16)
    low = (value - high.astype(F32)).astype(BF16)
    return high, low


def wide_left(pair, width):
    high, low = pair[:, :width], pair[:, width:]
    return jnp.concatenate([high, high, low], axis=1)


def wide_right(pair, width, axis):
    high, low = pair[:, :width], pair[:, width:]
    return jnp.concatenate([high, low, high], axis=axis)


def powers(count):
    return [1 << i for i in range(count.bit_length() - 1)]


class Plan:
    def __init__(self, mesh_shape, wavefunction, operators, coupling):
        self.grp, self.op, self.sec, self.rep = (mesh_shape[a] for a in EVERYONE)
        self.half = self.op // 2
        self.own, self.width = wavefunction.shape[0], wavefunction.shape[1]
        self.terms = operators.shape[0]
        self.sectors = coupling.shape[1]
        self.rows = self.width // (self.op * self.rep)
        self.block = self.rows * self.rep
        self.part = self.width // 2
        self.away = self.block * (self.half - 1)
        self.piece = self.own * self.rows

    def perm(self, move):
        def flat(g, o, s, r):
            return ((g * self.op + o) * self.sec + s) * self.rep + r

        pairs = []
        for g in range(self.grp):
            for o in range(self.op):
                for s in range(self.sec):
                    for r in range(self.rep):
                        pairs.append((flat(g, o, s, r), flat(g, *move(o, s, r))))
        return pairs

    def across_cores(self, x):
        return lax.ppermute(x, EVERYONE, self.perm(lambda o, s, r: (o, s, 1 - r)))

    def next_sec(self, x):
        return lax.ppermute(x, EVERYONE, self.perm(lambda o, s, r: (o, (s + 1) % self.sec, r)))

    def next_in_half(self, x):
        def move(o, s, r):
            base = o // self.half * self.half
            return (base + (o - base + 1) % self.half, s, r)

        return lax.ppermute(x, EVERYONE, self.perm(move))

    def flip_op(self, x, bits):
        return lax.ppermute(x, EVERYONE, self.perm(lambda o, s, r: (o ^ bits, s, r)))

    def flip_sec(self, x, bits):
        return lax.ppermute(x, EVERYONE, self.perm(lambda o, s, r: (o, s ^ bits, r)))

    def onward(self, x):
        to = {0: 2, 2: 3, 3: 1, 1: 0}
        return lax.ppermute(x, EVERYONE, self.perm(lambda o, s, r: (to[o], s, r)))


def places(plan):
    op = lax.axis_index("op")
    return lax.div(op, plan.half), lax.rem(op, plan.half), lax.axis_index("sec"), lax.axis_index("rep")


class Stack:
    def __init__(self, ref, start, count, height):
        self.ref, self.start, self.count, self.height = ref, start, count, height

    def span(self, block, rows=None):
        first, last = (0, self.height) if rows is None else rows
        return slice(self.start + block * self.height + first, self.start + block * self.height + last)

    def put(self, block, value, rows=None):
        width = value.shape[-1]
        at = self.span(block, rows)
        self.ref[at, :width], self.ref[at, width:] = halves(value)

    def get(self, block):
        if isinstance(block, int):
            return self.ref[self.span(block)]
        return self.ref[pl.ds(pl.multiple_of(self.start + block * self.height, 16), self.height)]

    def all(self):
        return self.ref[self.start:self.start + self.count * self.height]


def stacks(plan, ref, *names):
    sizes = dict(
        away=(2 * plan.terms, plan.away), home=(2 * plan.terms, plan.block),
        right=(plan.terms, plan.width), source=(plan.own, plan.width),
    )
    found, start = [], 0
    for name in names:
        count, height = sizes[name]
        found.append(Stack(ref, start, count, height))
        start += count * height
    return found


def stack_shape(plan, *names):
    end = stacks(plan, None, *names)[-1]
    return (end.start + end.count * end.height, 2 * plan.width)


def prepare_left(plan, left_in, flipped, away, home):
    side, mine, _, _ = places(plan)
    half_at = pl.multiple_of(side * plan.part, plan.part)
    for k in range(plan.terms):
        flipped[k] = left_in[k, :, pl.ds(half_at, plan.part)].T
    for off in range(plan.half):
        at = pl.multiple_of(lax.rem(mine + off, plan.half) * plan.block, plan.block)
        goal = away if off else home
        start = (off - 1) * plan.block if off else 0
        rows = (start, start + plan.block)
        for k in range(plan.terms):
            goal.put(k, left_in[k, pl.ds(pl.multiple_of(half_at + at, plan.block), plan.block), :], rows)
            goal.put(plan.terms + k, flipped[k, pl.ds(at, plan.block), :], rows)


def prepare_right(plan, right_in, right):
    for k in range(plan.terms):
        right.put(k, right_in[k])


def apply_terms(plan, tables, inverse, lefts, right, source, u_pair, total):
    w, terms, own = plan.width, plan.terms, plan.own
    n = lefts.height
    first_own = lax.axis_index("sec") * own
    for k in range(terms):
        for s in range(plan.sectors):
            inverse[k, tables[k, s]] = s
    total[...] = jnp.zeros_like(total)
    left = wide_left(lefts.all(), w)
    for t in range(own):
        got = lax.dot_general(left, wide_right(source.get(t), w, 1), CONTRACT_LAST, preferred_element_type=F32)
        high, low = halves(got)
        for k in range(2 * terms):
            u_pair[k, t * n:(t + 1) * n, :w] = high[k * n:(k + 1) * n]
            u_pair[k, t * n:(t + 1) * n, w:] = low[k * n:(k + 1) * n]

    unroll = 8 if terms % 8 == 0 else 1

    def second_stage(i, carry):
        for j in range(unroll):
            k = i * unroll + j
            got = lax.dot_general(wide_left(u_pair[k], w), wide_right(right.get(k), w, 1), CONTRACT_LAST,
                                  preferred_element_type=F32)
            for t in range(own):
                total[inverse[k, first_own + t]] += got[t * n:(t + 1) * n]
            got = lax.dot_general(wide_left(u_pair[terms + k], w), wide_right(right.get(k), w, 0), CONTRACT_FIRST,
                                  preferred_element_type=F32)
            for t in range(own):
                total[tables[k, first_own + t]] += got[t * n:(t + 1) * n]
        return carry

    lax.fori_loop(0, terms // unroll, second_stage, 0)


def hand_out(plan, offsets, total, tables, rows_are, keep, send):
    side, mine, my_sec, my_rep = places(plan)
    rows = plan.rows
    row_id = lax.broadcasted_iota(jnp.int32, (rows, plan.width), 0)
    col_id = lax.broadcasted_iota(jnp.int32, (rows, plan.width), 1)
    for sec_off in range(plan.sec):
        for i, op_off in enumerate(offsets):
            for rep_off in range(plan.rep):
                inner = pl.multiple_of(lax.rem(my_rep + rep_off, plan.rep) * rows, rows)
                first_row = side * plan.part + lax.rem(mine + op_off, plan.half) * plan.block + inner
                goal = send if rep_off else keep
                for t in range(plan.own):
                    s = lax.rem(my_sec + sec_off, plan.sec) * plan.own + t
                    ok = row_id + first_row < tables[plan.terms + rows_are, s]
                    ok = ok & (col_id < tables[plan.terms + 1 - rows_are, s])
                    value = total[s, pl.ds(pl.multiple_of(i * plan.block + inner, rows), rows), :]
                    goal[sec_off, i, t * rows:(t + 1) * rows] = jnp.where(ok, value, 0.0)


def masked_wave(plan, tables, wave, t):
    rows, cols = lax.axis_index("sec") * plan.own + t, plan.terms
    row_id = lax.broadcasted_iota(jnp.int32, wave.shape[1:], 0)
    col_id = lax.broadcasted_iota(jnp.int32, wave.shape[1:], 1)
    ok = (row_id < tables[cols, rows]) & (col_id < tables[cols + 1, rows])
    return jnp.where(ok, wave[t], 0.0)


def first_kernel(plan, tables, wave, left_ops, right_ops,
                 keep, send, pieces, packed,
                 wave_in, left_in, right_in, flipped, a_away, u_pair, total, inverse, sems):
    side, mine, _, my_rep = places(plan)
    loads = ((wave, wave_in), (right_ops, right_in), (left_ops, left_in))
    copies = [pltpu.make_async_copy(src, dst, sems.at[i]) for i, (src, dst) in enumerate(loads)]
    for copy in copies:
        copy.start()
    home, right, source = stacks(plan, packed, "home", "right", "source")
    away, = stacks(plan, a_away, "away")
    half_at = pl.multiple_of(side * plan.part, plan.part)
    copies[0].wait()
    for t in range(plan.own):
        masked = masked_wave(plan, tables, wave_in, t)
        source.put(t, masked)
        wave_in[t] = masked
    for t in range(plan.own):
        flipped[t] = wave_in[t, :, pl.ds(half_at, plan.part)].T
        for off in range(plan.half):
            at = (lax.rem(mine + off, plan.half) * plan.rep + my_rep) * plan.rows
            value = flipped[t, pl.ds(pl.multiple_of(at, plan.rows), plan.rows), :]
            pieces[off, t * plan.rows:(t + 1) * plan.rows] = value
    copies[1].wait()
    prepare_left(plan, right_in, flipped.at[pl.ds(plan.own, plan.terms)], away, home)
    copies[2].wait()
    prepare_right(plan, left_in, right)
    apply_terms(plan, tables, inverse, away, right, source, u_pair, total)
    hand_out(plan, range(1, plan.half), total, tables, 1, keep, send)


def home_kernel(rows_are, names, plan, tables, *refs):
    packs, (keep, send, u_pair, total, inverse) = refs[:len(names)], refs[len(names):]
    home, right, source = [found for pack, part in zip(packs, names) for found in stacks(plan, pack, *part)]
    apply_terms(plan, tables, inverse, home, right, source, u_pair, total)
    hand_out(plan, range(1), total, tables, rows_are, keep, send)


def prepare_kernel(plan, tables, wave, left_ops, right_ops, a_away, packed, turned, flipped):
    home, right = stacks(plan, packed, "home", "right")
    away, = stacks(plan, a_away, "away")
    for t in range(plan.own):
        turned[t] = masked_wave(plan, tables, wave, t).T
    prepare_left(plan, left_ops, flipped, away, home)
    prepare_right(plan, right_ops, right)


def second_kernel(plan, tables, turned, a_away, packed, *rest):
    units, rest = rest[:2 * plan.op], rest[2 * plan.op:]
    (keep, send, s_pair, residual, norm, full, flipped, u_pair, total, inverse) = rest
    _, right = stacks(plan, packed, "home", "right")
    away, = stacks(plan, a_away, "away")
    source, = stacks(plan, s_pair, "source")
    side, mine, _, my_rep = places(plan)
    my_op = lax.axis_index("op")
    w, rows = plan.width, plan.rows
    sums = jnp.zeros((TILE, w), F32)
    for whose in range(2):
        for bits in range(plan.op):
            unit = units[whose * plan.op + bits]
            r = my_rep if whose == 0 else 1 - my_rep
            at = pl.multiple_of(((my_op ^ bits) * plan.rep + r) * rows, rows)
            for t in range(plan.own):
                full[t, pl.ds(at, rows), :] = unit[t * rows:(t + 1) * rows]
            sums = sums + unit[plan.piece:]
    entries = plan.sectors * w * w
    sums = jnp.broadcast_to(jnp.sum(sums, axis=1, keepdims=True), sums.shape)
    energy = sums[0:1] / sums[1:2]
    height = 1.0 + jnp.sqrt(sums[2:3] / entries) / TINY
    level = 1.0 / height
    at = pl.multiple_of((mine * plan.rep + my_rep) * rows, rows)
    half_at = pl.multiple_of(side * plan.part, plan.part)
    squares = jnp.zeros((8, w), F32)
    for t in range(plan.own):
        res = full[t] - energy * turned[t]
        squares = squares + jnp.sum((res * res).reshape(w // 8, 8, w), axis=0)
        full[t] = res
        source.put(t, res * level)
    for t in range(plan.own):
        flipped[t] = full[t, :, pl.ds(half_at, plan.part)].T
        residual[t] = flipped[t, pl.ds(at, rows), :]
    norm[0:4] = jnp.full((4, w), jnp.sum(squares), F32)
    norm[4:8] = jnp.broadcast_to(height, (4, w))
    apply_terms(plan, tables, inverse, away, right, source, u_pair, total)
    hand_out(plan, range(1, plan.half), total, tables, 0, keep, send)


def join_kernel(plan, sigma, extra, cross, unit):
    unit[:plan.piece] = sigma[...]
    row = lax.broadcasted_iota(jnp.int32, extra.shape, 0)
    unit[plan.piece:] = extra[...] + jnp.where(row == 0, cross[...], 0.0)


def sums_tile(products, squares, shares):
    rows = [sum(jnp.sum(x, axis=0, keepdims=True) for x in part) for part in (products, squares, shares)]
    return jnp.concatenate(rows + [jnp.zeros((TILE - 3,) + rows[0].shape[1:], F32)])


def gather_along_op(plan, piece, beside):
    if plan.op == 4:
        far = plan.flip_op(piece, 3)
        near = plan.flip_op(piece, 1)
        op = lax.axis_index("op")
        far, beside = lax.optimization_barrier((far, beside))
        carried = jnp.where((op == 1) | (op == 2), far, piece)
        return [piece, near, plan.onward(carried), far], beside
    got = piece[None]
    for bits in powers(plan.op):
        got = jnp.concatenate([got, plan.flip_op(got, bits)])
    return [got[i] for i in range(plan.op)], beside


def on_device(mesh_shape, wavefunction, left_operators, right_operators, coupling, left_sizes, right_sizes):
    plan = Plan(mesh_shape, wavefunction, left_operators, coupling)
    own, w, rows, terms = plan.own, plan.width, plan.rows, plan.terms
    smem = pl.BlockSpec(memory_space=pltpu.SMEM)
    vmem = pl.BlockSpec(memory_space=pltpu.VMEM)
    hbm = pl.BlockSpec(memory_space=pltpu.HBM)

    def spread(offsets):
        return jax.ShapeDtypeStruct((plan.sec, offsets, plan.piece, w), F32)

    def work(n):
        return [
            pltpu.VMEM((2 * terms, own * n, 2 * w), BF16),
            pltpu.VMEM((plan.sectors, n, w), F32),
            pltpu.SMEM((terms, plan.sectors), jnp.int32),
        ]

    def call(body, n, out_shape, in_specs, scratch, grant=28):
        flops = 3 * 2 * 2 * 2 * terms * own * n * w * w
        return pl.pallas_call(
            functools.partial(body, plan),
            out_shape=out_shape,
            in_specs=in_specs,
            out_specs=(vmem,) * len(out_shape),
            scratch_shapes=scratch,
            compiler_params=pltpu.CompilerParams(vmem_limit_bytes=grant << 20),
            cost_estimate=pl.CostEstimate(flops=flops, bytes_accessed=4 << 20, transcendentals=0),
        )

    blocks = jax.ShapeDtypeStruct((own, w, w), F32)
    def packed(*names):
        return jax.ShapeDtypeStruct(stack_shape(plan, *names), BF16)

    chunks = jax.ShapeDtypeStruct((plan.half, plan.piece, w), F32)
    operators = pltpu.VMEM((terms, w, w), F32)
    turned_operators = pltpu.VMEM((terms, plan.part, w), F32)
    tables = jnp.concatenate([coupling, left_sizes[None], right_sizes[None]])

    def ring_in_half(parts, at):
        run = parts[at(plan.half - 2)]
        for i in range(plan.half - 3, -1, -1):
            run = plan.next_in_half(run) + parts[at(i)]
        return plan.next_in_half(run)

    def along_half(keep, send, rows_are, names, home_args):
        away = keep + plan.across_cores(send)
        away, home_args = lax.optimization_barrier((away, home_args))
        others = ring_in_half(away[1:], lambda i: (slice(None), i))
        kept = call(
            functools.partial(home_kernel, rows_are, names), plan.block, (spread(1),) * 2,
            [smem] + [vmem] * len(names), work(plan.block),
        )(tables, *home_args)
        sent, others, kept = lax.optimization_barrier((away[0], others, kept))
        home = (kept[0] + plan.across_cores(kept[1]))[:, 0]
        return others + home[1:], home[0], ring_in_half(sent, lambda i: i), sent

    def along_sec(others, ours, extra):
        if plan.sec == 2:
            got = plan.next_sec(jnp.concatenate([others[0], extra]))
            return ours + got[:plan.piece], extra + got[plan.piece:], got[:plan.piece]
        run = others[plan.sec - 2]
        for i in range(plan.sec - 3, -1, -1):
            run = plan.next_sec(run) + others[i]
        run = plan.next_sec(run)
        for bits in powers(plan.sec):
            extra = extra + plan.flip_sec(extra, bits)
        return ours + run, extra, run

    keep, send, pieces, packs = call(
        first_kernel, plan.away,
        (spread(plan.half - 1),) * 2 + (chunks, packed("home", "right", "source")),
        [smem] + [hbm] * 3,
        [pltpu.VMEM(blocks.shape, F32), operators, operators, pltpu.VMEM((own + terms, plan.part, w), F32),
         pltpu.VMEM(packed("away").shape, BF16)] + work(plan.away) + [pltpu.SemaphoreType.DMA((3,))],
    )(tables, *[pltpu.with_memory_space_constraint(x, pltpu.HBM)
                for x in (wavefunction, left_operators, right_operators)])

    others, home, got, sent = along_half(keep, send, 1, (("home", "right", "source"),), (packs,))
    extra = sums_tile(
        [home * pieces[0]] + [sent[i] * pieces[1 + i] for i in range(plan.half - 1)], [pieces[0] ** 2],
        [(x * TINY) ** 2 for x in [home, *sent, *others]],
    )
    sigma, extra, crossed = along_sec(others, home + got, extra)
    cross = jnp.sum(crossed * pieces[0], axis=0, keepdims=True)
    if plan.sec == 2:
        cross = 2.0 * cross
    else:
        for bits in powers(plan.sec):
            cross = cross + plan.flip_sec(cross, bits)
    unit, = call(join_kernel, 1, (jax.ShapeDtypeStruct((plan.piece + TILE, w), F32),), [vmem] * 3, [])(
        sigma, extra, cross)

    unit, *again = lax.optimization_barrier((unit, wavefunction, left_operators, right_operators))
    prepared = call(
        prepare_kernel, 1, (packed("away"), packed("home", "right"), blocks), [smem] + [vmem] * 3, [turned_operators],
    )(tables, *again)
    units, (a_away, packs, turned) = gather_along_op(plan, unit, prepared)
    units = units + [plan.across_cores(x) for x in units]

    keep, send, s_pair, residual, norm = call(
        second_kernel, plan.away,
        (spread(plan.half - 1),) * 2 + (packed("source"), jax.ShapeDtypeStruct((own, rows, w), F32),
                                        jax.ShapeDtypeStruct((TILE, w), F32)),
        [smem] + [vmem] * (3 + len(units)),
        [pltpu.VMEM(blocks.shape, F32), pltpu.VMEM((own, plan.part, w), F32)] + work(plan.away),
    )(tables, turned, a_away, packs, *units)

    others, home, got, _ = along_half(keep, send, 0, (("home", "right"), ("source",)), (packs, s_pair))
    sigma, total, _ = along_sec(others, home + got, norm)
    entries = plan.sectors * w * w
    factor = norm[4:5] / jnp.sqrt(total[0:1] / entries + 1e-06)
    sigma_next = (sigma * factor).reshape(own, rows, w)
    return (sigma_next, residual)


def solution(mesh):
    in_specs = (
        P(("grp", "sec"), None, None),
        P(("op", "rep"), None, None),
        P(("op", "rep"), None, None),
        P(("op", "rep"), None),
        P("grp"),
        P("grp"),
    )
    out_specs = (P(("grp", "sec"), ("op", "rep"), None), P(("grp", "sec"), ("op", "rep"), None))
    return jax.shard_map(
        functools.partial(on_device, dict(mesh.shape)),
        mesh=mesh, in_specs=in_specs, out_specs=out_specs, check_vma=False,
    )
```

time: 81 us -> 77.3 us (0.954)
  local copies, waits for them, and re-layouts: 5.33 us -> 3.1 us
  waiting for transfers between devices: 25.9 us -> 23.8 us
    ppermute x3 -> x2, waiting for transfers between devices: 10.2 us -> 5.45 us  [next_sec(): lax.ppermute(x, EVERYONE, self.perm(lambda o, s, r: (o, (s + 1) % self.se...]
    ppermute x8, waiting for transfers between devices: 3.04 us -> 7.79 us  [across_cores(): return lax.ppermute(x, EVERYONE, self.perm(lambda o, s, r: (o, s, 1 - r)))]
    ppermute x2 -> x4, starting transfers between devices: 3.47 us -> 7.11 us  [next_in_half(): return lax.ppermute(x, EVERYONE, self.perm(move))]
    ppermute x3 -> x2, starting transfers between devices: 5.8 us -> 2.4 us  [next_sec(): lax.ppermute(x, EVERYONE, self.perm(lambda o, s, r: (o, (s + 1) % self.se...]
    ppermute x2, waiting for transfers between devices: 4.1 us -> 1.58 us  [flip_op(): lax.ppermute(x, EVERYONE, self.perm(lambda o, s, r: (o ^ bits, s, r)))]
    unnamed x22 -> x6, local copies, waits for them, and re-layouts: 5.2 us -> 3 us
    ppermute x2 -> x4, waiting for transfers between devices: 5.13 us -> 6.09 us  [next_in_half(): return lax.ppermute(x, EVERYONE, self.perm(move))]
    pallas_call x5 -> x6, Pallas kernels: 30.1 us -> 29.9 us  [the longest x2 11.9 us: along_half(): call(functools.partial(home_kernel, rows_are, names), plan.block, (spread...]
  transfers between devices with their start and end apart: 16 -> 17, of which waited for: 8 -> 10; matrix products, arithmetic and copies ran while one was open for 0% -> 0% of each run, Pallas kernels for 16% -> 18%
where the time goes in v3:
time: 77.3 us; the launch traced here: 77.1 us
  Pallas kernels  29.9 us (39%)
  waiting for transfers between devices  23.8 us (31%)
  starting transfers between devices  17.4 us (23%)
  local copies, waits for them, and re-layouts  3.1 us (4%)
  other arithmetic  1.99 us (3%)
  between operations  0.82 us (1%)
    pallas_call x2, Pallas kernels, along_half(): call(functools.partial(home_kernel, rows_are, names), plan.block, (spread...  11.9 us
    pallas_call x1, Pallas kernels, on_device(): call(first_kernel, plan.away, (spread(plan.half - 1),) * 2 + (chunks, pac...  8.7 us
    ppermute x8, waiting for transfers between devices, across_cores(): return lax.ppermute(x, EVERYONE, self.perm(lambda o, s, r: (o, s, 1 - r)))  7.79 us
    pallas_call x1, Pallas kernels, on_device(): call(second_kernel, plan.away, (spread(plan.half - 1),) * 2 + (packed('so...  7.19 us
    ppermute x4, starting transfers between devices, next_in_half(): return lax.ppermute(x, EVERYONE, self.perm(move))  7.11 us
    ppermute x4, waiting for transfers between devices, next_in_half(): return lax.ppermute(x, EVERYONE, self.perm(move))  6.09 us
    ppermute x2, waiting for transfers between devices, next_sec(): lax.ppermute(x, EVERYONE, self.perm(lambda o, s, r: (o, (s + 1) % self.se...  5.45 us
    ppermute x1, starting transfers between devices, onward(): return lax.ppermute(x, EVERYONE, self.perm(lambda o, s, r: (to[o], s, r)))  3.36 us
  transfers between devices with their start and end apart: 17, of which 10 were waited for; matrix products, arithmetic and copies ran while one was open for 0% of the time, Pallas kernels for 18%

profile of v3, /device:TPU:0, one launch (start us, length us, event | category | flops | bytes accessed | tf_op | source)
XLA Modules:
  0.0 77.1 jit_solution(18236807744912866768)
XLA Ops:
  0.6 0.7 pad_add_fusion.tables
  1.4 8.7 %shard_map.77 = (f32[2,1,192,256]{3,2,1,0:T(8,128)S(1)}, f32[2,1,192,256]{3,2,1,0:T(8,128)S(1)}, f32[2,192,256]{2,1,0:T(8,128)S(1)}, bf16[4608,512]{1,0:T(8,128)(2,1)S(1)}) custom-call(s32[10,12]{1,0:T(8,128)S(1)} %pad_add_fusion.tables, f32[6,256,256]{2,1,0:T(8,128)} %wave.2, f32[8,256,256]{2,1,0:T(8,128)} %left_ops.2, f32[8,256,256]{2,1,0:T(8,128)} %right_ops.2), custom_call_target="tpu_custom_call" | custom-call | flops 4831838208 | bytes 4194304 | tf_op jit(solution)/shard_map/pallas_call | solution.py:393
  10.1 0.5 collective-permute-start
  10.6 1.3 %collective-permute-done = f32[2,1,192,256]{3,2,1,0:T(8,128)S(1)} collective-permute-done((f32[2,1,192,256]{3,2,1,0:T(8,128)S(1)}, f32[2,1,192,256]{3,2,1,0:T(8,128)S(1)}, u32[]{:S(2)}, u32[]{:S(2)}) %collective-permute-start) | collective-permute-done | bytes 393248 | tf_op jit(solution)/shard_map/ppermute | solution.py:65
  12.0 3.0 %collective-permute-start.1 = (f32[1,192,256]{2,1,0:T(8,128)S(1)}, f32[1,192,256]{2,1,0:T(8,128)S(1)}, u32[]{:S(2)}, u32[]{:S(2)}) collective-permute-start(f32[1,192,256]{2,1,0:T(8,128)S(1)} %get-tuple-element.87), channel_id=1, source_target_pairs={{0,4},{1,5},{2,6},{3,7},{4,0},{5,1},{6,2},{7,3},{8,12},{9,13},{10,... | collective-permute-start | bytes 589832 | tf_op jit(solution)/shard_map/ppermute | solution.py:75
  15.0 6.0 %shard_map.78 = (f32[2,1,192,256]{3,2,1,0:T(8,128)S(1)}, f32[2,1,192,256]{3,2,1,0:T(8,128)S(1)}) custom-call(s32[10,12]{1,0:T(8,128)S(1)} %pad_add_fusion.tables, bf16[4608,512]{1,0:T(8,128)(2,1)S(1)} %get-tuple-element.43.refs_0_), custom_call_target="tpu_custom_call" | custom-call | flops 4831838208 | bytes 4194304 | tf_op jit(solution)/shard_map/pallas_call | solution.py:373
  21.1 1.7 %collective-permute-done.2 = f32[2,1,192,256]{3,2,1,0:T(8,128)S(1)} collective-permute-done((f32[2,1,192,256]{3,2,1,0:T(8,128)S(1)}, f32[2,1,192,256]{3,2,1,0:T(8,128)S(1)}, u32[]{:S(2)}, u32[]{:S(2)}) %collective-permute-start.2) | collective-permute-done | bytes 393248 | tf_op jit(solution)/shard_map/ppermute | solution.py:65
  22.9 0.2 multiply_reduce_fusion.2
  23.1 1.6 %collective-permute-start.4 = (f32[200,256]{1,0:T(8,128)S(1)}, f32[200,256]{1,0:T(8,128)S(1)}, u32[]{:S(2)}, u32[]{:S(2)}) collective-permute-start(f32[200,256]{1,0:T(8,128)S(1)} %concatenate.14), channel_id=1, source_target_pairs={{0,2},{1,3},{2,0},{3,1},{4,6},{5,7},{6,4},{7,5},{8,10},{9,11},{10,... | collective-permute-start | bytes 614408 | tf_op jit(solution)/shard_map/ppermute | solution.py:68
  24.7 0.9 %collective-permute-start.3 = (f32[192,256]{1,0:T(8,128)S(1)}, f32[192,256]{1,0:T(8,128)S(1)}, u32[]{:S(2)}, u32[]{:S(2)}) collective-permute-start(f32[192,256]{1,0:T(8,128)S(1)} %bitcast.67), channel_id=1, source_target_pairs={{0,4},{1,5},{2,6},{3,7},{4,0},{5,1},{6,2},{7,3},{8,12},{9,13},{10,... | collective-permute-start | bytes 589832 | tf_op jit(solution)/shard_map/ppermute | solution.py:75
  25.5 5.8 %collective-permute-done.3 = f32[192,256]{1,0:T(8,128)S(1)} collective-permute-done((f32[192,256]{1,0:T(8,128)S(1)}, f32[192,256]{1,0:T(8,128)S(1)}, u32[]{:S(2)}, u32[]{:S(2)}) %collective-permute-start.3) | collective-permute-done | bytes 196640 | tf_op jit(solution)/shard_map/ppermute | solution.py:75
  31.4 3.0 %collective-permute-start.5 = (f32[200,256]{1,0:T(8,128)S(1)}, f32[200,256]{1,0:T(8,128)S(1)}, u32[]{:S(2)}, u32[]{:S(2)}) collective-permute-start(f32[200,256]{1,0:T(8,128)S(1)} %shard_map.79.rest_0_), channel_id=1, source_target_pairs={{0,12},{1,13},{2,14},{3,15},{4,8},{5,9},{6,10},{7,11},{8,4},{9,5},... | collective-permute-start | bytes 614408 | tf_op jit(solution)/shard_map/ppermute | solution.py:78
  34.4 0.2 collective-permute-start.6
  34.7 1.6 %copy-done.1 = f32[8,256,256]{2,1,0:T(8,128)S(1)} copy-done((f32[8,256,256]{2,1,0:T(8,128)S(1)}, f32[8,256,256]{2,1,0:T(8,128)}, u32[]{:S(2)}) %copy-start.1) | copy-done | bytes 2097176
  36.3 1.4 %copy-done.2 = f32[6,256,256]{2,1,0:T(8,128)S(1)} copy-done((f32[6,256,256]{2,1,0:T(8,128)S(1)}, f32[6,256,256]{2,1,0:T(8,128)}, u32[]{:S(2)}) %copy-start.2) | copy-done | bytes 1572888
  37.7 2.1 %shard_map.80 = (bf16[1024,512]{1,0:T(8,128)(2,1)S(1)}, bf16[3072,512]{1,0:T(8,128)(2,1)S(1)}, f32[6,256,256]{2,1,0:T(8,128)S(1)}) custom-call(s32[10,12]{1,0:T(8,128)S(1)} %pad_add_fusion.tables, f32[6,256,256]{2,1,0:T(8,128)S(1)} %copy-done.2, f32[8,256,256]{2,1,0:T(8,128)S(1)} %copy-done, f32[8,256,256]{2,1,0:T(8,128)S(1)} %copy-done.1), custom_call_target="tpu_custom_call" | custom-call | flops 75497472 | bytes 4194304 | tf_op jit(solution)/shard_map/pallas_call | solution.py:418
  39.7 1.6 %collective-permute-done.5.rest_3_ = f32[200,256]{1,0:T(8,128)S(1)} collective-permute-done((f32[200,256]{1,0:T(8,128)S(1)}, f32[200,256]{1,0:T(8,128)S(1)}, u32[]{:S(2)}, u32[]{:S(2)}) %collective-permute-start.5) | collective-permute-done | bytes 204832 | tf_op jit(solution)/shard_map/ppermute | solution.py:78
  41.4 3.4 %collective-permute-start.7 = (f32[200,256]{1,0:T(8,128)S(1)}, f32[200,256]{1,0:T(8,128)S(1)}, u32[]{:S(2)}, u32[]{:S(2)}) collective-permute-start(f32[200,256]{1,0:T(8,128)S(1)} %broadcast_select_fusion), channel_id=1, source_target_pairs={{0,8},{1,9},{2,10},{3,11},{4,0},{5,1},{6,2},{7,3},{8,12},{9,13},{1... | collective-permute-start | bytes 614408 | tf_op jit(solution)/shard_map/ppermute | solution.py:85
  44.7 0.5 collective-permute-start.11
  45.2 2.9 %collective-permute-done.7.rest_2_ = f32[200,256]{1,0:T(8,128)S(1)} collective-permute-done((f32[200,256]{1,0:T(8,128)S(1)}, f32[200,256]{1,0:T(8,128)S(1)}, u32[]{:S(2)}, u32[]{:S(2)}) %collective-permute-start.7) | collective-permute-done | bytes 204832 | tf_op jit(solution)/shard_map/ppermute | solution.py:85
  48.2 1.4 %collective-permute-done.10.rest_6_ = f32[200,256]{1,0:T(8,128)S(1)} collective-permute-done((f32[200,256]{1,0:T(8,128)S(1)}, f32[200,256]{1,0:T(8,128)S(1)}, u32[]{:S(2)}, u32[]{:S(2)}) %collective-permute-start.10) | collective-permute-done | bytes 204832 | tf_op jit(solution)/shard_map/ppermute | solution.py:65
  49.6 7.2 %shard_map.81 = (f32[2,1,192,256]{3,2,1,0:T(8,128)S(1)}, f32[2,1,192,256]{3,2,1,0:T(8,128)S(1)}, bf16[1536,512]{1,0:T(8,128)(2,1)S(1)}, f32[6,32,256]{2,1,0:T(8,128)}, f32[8,256]{1,0:T(8,128)S(1)}) custom-call(s32[10,12]{1,0:T(8,128)S(1)} %pad_add_fusion.tables, f32[6,256,256]{2,1,0:T(8,128)S(1)} %get-tuple-element.58.turned, ...), custom_call_target="tpu_custom_call" | custom-call | flops 4831838208 | bytes 4194304 | tf_op jit(solution)/shard_map/pallas_call | solution.py:424
  56.8 0.1 collective-permute-start.12
  56.9 1.6 %collective-permute-done.12 = f32[2,1,192,256]{3,2,1,0:T(8,128)S(1)} collective-permute-done((f32[2,1,192,256]{3,2,1,0:T(8,128)S(1)}, f32[2,1,192,256]{3,2,1,0:T(8,128)S(1)}, u32[]{:S(2)}, u32[]{:S(2)}) %collective-permute-start.12) | collective-permute-done | bytes 393248 | tf_op jit(solution)/shard_map/ppermute | solution.py:65
  58.6 2.3 %collective-permute-start.13 = (f32[1,192,256]{2,1,0:T(8,128)S(1)}, f32[1,192,256]{2,1,0:T(8,128)S(1)}, u32[]{:S(2)}, u32[]{:S(2)}) collective-permute-start(f32[1,192,256]{2,1,0:T(8,128)S(1)} %get-tuple-element.83), channel_id=1, source_target_pairs={{0,4},{1,5},{2,6},{3,7},{4,0},{5,1},{6,2},{7,3},{8,12},{9,13},{10,... | collective-permute-start | bytes 589832 | tf_op jit(solution)/shard_map/ppermute | solution.py:75
  60.9 6.0 %shard_map.82 = (f32[2,1,192,256]{3,2,1,0:T(8,128)S(1)}, f32[2,1,192,256]{3,2,1,0:T(8,128)S(1)}) custom-call(s32[10,12]{1,0:T(8,128)S(1)} %pad_add_fusion.tables, bf16[3072,512]{1,0:T(8,128)(2,1)S(1)} %get-tuple-element.66.packed.refs_0_, bf16[1536,512]{1,0:T(8,128)(2,1)S(1)} %get-tuple-element.67.refs_1_), custom_call_target="tpu_custom_call" | custom-call | flops 4831838208 | bytes 4194304 | tf_op jit(solution)/shard_map/pallas_call | solution.py:373
  67.0 1.7 %collective-permute-done.14 = f32[2,1,192,256]{3,2,1,0:T(8,128)S(1)} collective-permute-done((f32[2,1,192,256]{3,2,1,0:T(8,128)S(1)}, f32[2,1,192,256]{3,2,1,0:T(8,128)S(1)}, u32[]{:S(2)}, u32[]{:S(2)}) %collective-permute-start.14) | collective-permute-done | bytes 393248 | tf_op jit(solution)/shard_map/ppermute | solution.py:65
  68.8 0.8 %collective-permute-start.16 = (f32[200,256]{1,0:T(8,128)S(1)}, f32[200,256]{1,0:T(8,128)S(1)}, u32[]{:S(2)}, u32[]{:S(2)}) collective-permute-start(f32[200,256]{1,0:T(8,128)S(1)} %pad_maximum_fusion), channel_id=1, source_target_pairs={{0,2},{1,3},{2,0},{3,1},{4,6},{5,7},{6,4},{7,5},{8,10},{9,11},{10,... | collective-permute-start | bytes 614408 | tf_op jit(solution)/shard_map/ppermute | solution.py:68
  69.7 0.9 %collective-permute-start.15 = (f32[192,256]{1,0:T(8,128)S(1)}, f32[192,256]{1,0:T(8,128)S(1)}, u32[]{:S(2)}, u32[]{:S(2)}) collective-permute-start(f32[192,256]{1,0:T(8,128)S(1)} %bitcast.68), channel_id=1, source_target_pairs={{0,4},{1,5},{2,6},{3,7},{4,0},{5,1},{6,2},{7,3},{8,12},{9,13},{10,... | collective-permute-start | bytes 589832 | tf_op jit(solution)/shard_map/ppermute | solution.py:75
  70.6 5.5 %collective-permute-done.16 = f32[200,256]{1,0:T(8,128)S(1)} collective-permute-done((f32[200,256]{1,0:T(8,128)S(1)}, f32[200,256]{1,0:T(8,128)S(1)}, u32[]{:S(2)}, u32[]{:S(2)}) %collective-permute-start.16) | collective-permute-done | bytes 204832 | tf_op jit(solution)/shard_map/ppermute | solution.py:68
  76.0 0.3 collective-permute-done.15
  76.3 0.7 fusion
  (35 shorter events, 0.7 us)
Async XLA Ops:
  10.1 1.9 %collective-permute-start = (f32[2,1,192,256]{3,2,1,0:T(8,128)S(1)}, f32[2,1,192,256]{3,2,1,0:T(8,128)S(1)}, u32[]{:S(2)}, u32[]{:S(2)}) collective-permute-start(f32[2,1,192,256]{3,2,1,0:T(8,128)S(1)} %get-tuple-element.40), channel_id=1, source_target_pairs={{0,1},{1,0},{2,3},{3,2},{4,5},{5,4},{6,7},{7,6},{8,9},{9,8},{10,11... | collective-permute-start | bytes 1179656 | tf_op jit(solution)/shard_map/ppermute | solution.py:65
  12.0 9.0 %collective-permute-start.1 = (f32[1,192,256]{2,1,0:T(8,128)S(1)}, f32[1,192,256]{2,1,0:T(8,128)S(1)}, u32[]{:S(2)}, u32[]{:S(2)}) collective-permute-start(f32[1,192,256]{2,1,0:T(8,128)S(1)} %get-tuple-element.87), channel_id=1, source_target_pairs={{0,4},{1,5},{2,6},{3,7},{4,0},{5,1},{6,2},{7,3},{8,12},{9,13},{10,... | collective-permute-start | bytes 589832 | tf_op jit(solution)/shard_map/ppermute | solution.py:75
  21.0 13.6 %copy-start = (f32[8,256,256]{2,1,0:T(8,128)S(1)}, f32[8,256,256]{2,1,0:T(8,128)}, u32[]{:S(2)}) copy-start(f32[8,256,256]{2,1,0:T(8,128)} %left_ops.2) | copy-start | bytes 6291460
  21.0 1.8 %collective-permute-start.2 = (f32[2,1,192,256]{3,2,1,0:T(8,128)S(1)}, f32[2,1,192,256]{3,2,1,0:T(8,128)S(1)}, u32[]{:S(2)}, u32[]{:S(2)}) collective-permute-start(f32[2,1,192,256]{3,2,1,0:T(8,128)S(1)} %get-tuple-element.47), channel_id=1, source_target_pairs={{0,1},{1,0},{2,3},{3,2},{4,5},{5,4},{6,7},{7,6},{8,9},{9,8},{10,11... | collective-permute-start | bytes 1179656 | tf_op jit(solution)/shard_map/ppermute | solution.py:65
  23.1 8.2 %collective-permute-start.4 = (f32[200,256]{1,0:T(8,128)S(1)}, f32[200,256]{1,0:T(8,128)S(1)}, u32[]{:S(2)}, u32[]{:S(2)}) collective-permute-start(f32[200,256]{1,0:T(8,128)S(1)} %concatenate.14), channel_id=1, source_target_pairs={{0,2},{1,3},{2,0},{3,1},{4,6},{5,7},{6,4},{7,5},{8,10},{9,11},{10,... | collective-permute-start | bytes 614408 | tf_op jit(solution)/shard_map/ppermute | solution.py:68
  24.7 6.7 %collective-permute-start.3 = (f32[192,256]{1,0:T(8,128)S(1)}, f32[192,256]{1,0:T(8,128)S(1)}, u32[]{:S(2)}, u32[]{:S(2)}) collective-permute-start(f32[192,256]{1,0:T(8,128)S(1)} %bitcast.67), channel_id=1, source_target_pairs={{0,4},{1,5},{2,6},{3,7},{4,0},{5,1},{6,2},{7,3},{8,12},{9,13},{10,... | collective-permute-start | bytes 589832 | tf_op jit(solution)/shard_map/ppermute | solution.py:75
  31.4 9.9 %collective-permute-start.5 = (f32[200,256]{1,0:T(8,128)S(1)}, f32[200,256]{1,0:T(8,128)S(1)}, u32[]{:S(2)}, u32[]{:S(2)}) collective-permute-start(f32[200,256]{1,0:T(8,128)S(1)} %shard_map.79.rest_0_), channel_id=1, source_target_pairs={{0,12},{1,13},{2,14},{3,15},{4,8},{5,9},{6,10},{7,11},{8,4},{9,5},... | collective-permute-start | bytes 614408 | tf_op jit(solution)/shard_map/ppermute | solution.py:78
  34.4 10.8 %collective-permute-start.6 = (f32[200,256]{1,0:T(8,128)S(1)}, f32[200,256]{1,0:T(8,128)S(1)}, u32[]{:S(2)}, u32[]{:S(2)}) collective-permute-start(f32[200,256]{1,0:T(8,128)S(1)} %shard_map.79.rest_0_), channel_id=1, source_target_pairs={{0,4},{1,5},{2,6},{3,7},{4,0},{5,1},{6,2},{7,3},{8,12},{9,13},{10,... | collective-permute-start | bytes 614408 | tf_op jit(solution)/shard_map/ppermute | solution.py:78
  34.7 1.6 %copy-start.1 = (f32[8,256,256]{2,1,0:T(8,128)S(1)}, f32[8,256,256]{2,1,0:T(8,128)}, u32[]{:S(2)}) copy-start(f32[8,256,256]{2,1,0:T(8,128)} %right_ops.2) | copy-start | bytes 6291460
  36.3 1.4 %copy-start.2 = (f32[6,256,256]{2,1,0:T(8,128)S(1)}, f32[6,256,256]{2,1,0:T(8,128)}, u32[]{:S(2)}) copy-start(f32[6,256,256]{2,1,0:T(8,128)} %wave.2) | copy-start | bytes 4718596
  41.4 6.8 %collective-permute-start.7 = (f32[200,256]{1,0:T(8,128)S(1)}, f32[200,256]{1,0:T(8,128)S(1)}, u32[]{:S(2)}, u32[]{:S(2)}) collective-permute-start(f32[200,256]{1,0:T(8,128)S(1)} %broadcast_select_fusion), channel_id=1, source_target_pairs={{0,8},{1,9},{2,10},{3,11},{4,0},{5,1},{6,2},{7,3},{8,12},{9,13},{1... | collective-permute-start | bytes 614408 | tf_op jit(solution)/shard_map/ppermute | solution.py:85
  44.7 3.4 %collective-permute-start.8 = (f32[200,256]{1,0:T(8,128)S(1)}, f32[200,256]{1,0:T(8,128)S(1)}, u32[]{:S(2)}, u32[]{:S(2)}) collective-permute-start(f32[200,256]{1,0:T(8,128)S(1)} %shard_map.79.rest_0_), channel_id=1, source_target_pairs={{0,1},{1,0},{2,3},{3,2},{4,5},{5,4},{6,7},{7,6},{8,9},{9,8},{10,11... | collective-permute-start | bytes 614408 | tf_op jit(solution)/shard_map/ppermute | solution.py:65
  44.7 3.4 %collective-permute-start.11 = (f32[200,256]{1,0:T(8,128)S(1)}, f32[200,256]{1,0:T(8,128)S(1)}, u32[]{:S(2)}, u32[]{:S(2)}) collective-permute-start(f32[200,256]{1,0:T(8,128)S(1)} %collective-permute-done.5.rest_3_), channel_id=1, source_target_pairs={{0,1},{1,0},{2,3},{3,2},{4,5},{5,4},{6,7},{7,6},{8,9},{9,8},{10,11... | collective-permute-start | bytes 614408 | tf_op jit(solution)/shard_map/ppermute | solution.py:65
  45.2 2.9 %collective-permute-start.9 = (f32[200,256]{1,0:T(8,128)S(1)}, f32[200,256]{1,0:T(8,128)S(1)}, u32[]{:S(2)}, u32[]{:S(2)}) collective-permute-start(f32[200,256]{1,0:T(8,128)S(1)} %collective-permute-done.6.rest_1_), channel_id=1, source_target_pairs={{0,1},{1,0},{2,3},{3,2},{4,5},{5,4},{6,7},{7,6},{8,9},{9,8},{10,11... | collective-permute-start | bytes 614408 | tf_op jit(solution)/shard_map/ppermute | solution.py:65
  48.1 1.5 %collective-permute-start.10 = (f32[200,256]{1,0:T(8,128)S(1)}, f32[200,256]{1,0:T(8,128)S(1)}, u32[]{:S(2)}, u32[]{:S(2)}) collective-permute-start(f32[200,256]{1,0:T(8,128)S(1)} %collective-permute-done.7.rest_2_), channel_id=1, source_target_pairs={{0,1},{1,0},{2,3},{3,2},{4,5},{5,4},{6,7},{7,6},{8,9},{9,8},{10,11... | collective-permute-start | bytes 614408 | tf_op jit(solution)/shard_map/ppermute | solution.py:65
  56.8 1.7 %collective-permute-start.12 = (f32[2,1,192,256]{3,2,1,0:T(8,128)S(1)}, f32[2,1,192,256]{3,2,1,0:T(8,128)S(1)}, u32[]{:S(2)}, u32[]{:S(2)}) collective-permute-start(f32[2,1,192,256]{3,2,1,0:T(8,128)S(1)} %get-tuple-element.63), channel_id=1, source_target_pairs={{0,1},{1,0},{2,3},{3,2},{4,5},{5,4},{6,7},{7,6},{8,9},{9,8},{10,11... | collective-permute-start | bytes 1179656 | tf_op jit(solution)/shard_map/ppermute | solution.py:65
  58.6 8.3 %collective-permute-start.13 = (f32[1,192,256]{2,1,0:T(8,128)S(1)}, f32[1,192,256]{2,1,0:T(8,128)S(1)}, u32[]{:S(2)}, u32[]{:S(2)}) collective-permute-start(f32[1,192,256]{2,1,0:T(8,128)S(1)} %get-tuple-element.83), channel_id=1, source_target_pairs={{0,4},{1,5},{2,6},{3,7},{4,0},{5,1},{6,2},{7,3},{8,12},{9,13},{10,... | collective-permute-start | bytes 589832 | tf_op jit(solution)/shard_map/ppermute | solution.py:75
  66.9 1.8 %collective-permute-start.14 = (f32[2,1,192,256]{3,2,1,0:T(8,128)S(1)}, f32[2,1,192,256]{3,2,1,0:T(8,128)S(1)}, u32[]{:S(2)}, u32[]{:S(2)}) collective-permute-start(f32[2,1,192,256]{3,2,1,0:T(8,128)S(1)} %get-tuple-element.71), channel_id=1, source_target_pairs={{0,1},{1,0},{2,3},{3,2},{4,5},{5,4},{6,7},{7,6},{8,9},{9,8},{10,11... | collective-permute-start | bytes 1179656 | tf_op jit(solution)/shard_map/ppermute | solution.py:65
  68.8 7.2 %collective-permute-start.16 = (f32[200,256]{1,0:T(8,128)S(1)}, f32[200,256]{1,0:T(8,128)S(1)}, u32[]{:S(2)}, u32[]{:S(2)}) collective-permute-start(f32[200,256]{1,0:T(8,128)S(1)} %pad_maximum_fusion), channel_id=1, source_target_pairs={{0,2},{1,3},{2,0},{3,1},{4,6},{5,7},{6,4},{7,5},{8,10},{9,11},{10,... | collective-permute-start | bytes 614408 | tf_op jit(solution)/shard_map/ppermute | solution.py:68
  69.7 6.7 %collective-permute-start.15 = (f32[192,256]{1,0:T(8,128)S(1)}, f32[192,256]{1,0:T(8,128)S(1)}, u32[]{:S(2)}, u32[]{:S(2)}) collective-permute-start(f32[192,256]{1,0:T(8,128)S(1)} %bitcast.68), channel_id=1, source_target_pairs={{0,4},{1,5},{2,6},{3,7},{4,0},{5,1},{6,2},{7,3},{8,12},{9,13},{10,... | collective-permute-start | bytes 589832 | tf_op jit(solution)/shard_map/ppermute | solution.py:75

commit v4 on v3

--- a/solution.py
+++ b/solution.py
@@ -150,38 +150,46 @@
         right.put(k, right_in[k])
 
 
-def apply_terms(plan, tables, inverse, lefts, right, source, u_pair, total):
-    w, terms, own = plan.width, plan.terms, plan.own
-    n = lefts.height
+def first_products(plan, lefts, source, u_pair):
+    w, n = plan.width, lefts.height
+    left = wide_left(lefts.all(), w)
+    for t in range(plan.own):
+        got = lax.dot_general(left, wide_right(source.get(t), w, 1), CONTRACT_LAST, preferred_element_type=F32)
+        high, low = halves(got)
+        for k in range(lefts.count):
+            u_pair[k, t * n:(t + 1) * n, :w] = high[k * n:(k + 1) * n]
+            u_pair[k, t * n:(t + 1) * n, w:] = low[k * n:(k + 1) * n]
+
+
+def second_products(plan, tables, inverse, right, u_pair, total):
+    w, terms, own, n = plan.width, plan.terms, plan.own, total.shape[1]
     first_own = lax.axis_index("sec") * own
     for k in range(terms):
         for s in range(plan.sectors):
             inverse[k, tables[k, s]] = s
     total[...] = jnp.zeros_like(total)
-    left = wide_left(lefts.all(), w)
-    for t in range(own):
-        got = lax.dot_general(left, wide_right(source.get(t), w, 1), CONTRACT_LAST, preferred_element_type=F32)
-        high, low = halves(got)
-        for k in range(2 * terms):
-            u_pair[k, t * n:(t + 1) * n, :w] = high[k * n:(k + 1) * n]
-            u_pair[k, t * n:(t + 1) * n, w:] = low[k * n:(k + 1) * n]
-
-    unroll = 8 if terms % 8 == 0 else 1
-
-    def second_stage(i, carry):
-        for j in range(unroll):
-            k = i * unroll + j
-            got = lax.dot_general(wide_left(u_pair[k], w), wide_right(right.get(k), w, 1), CONTRACT_LAST,
-                                  preferred_element_type=F32)
-            for t in range(own):
-                total[inverse[k, first_own + t]] += got[t * n:(t + 1) * n]
-            got = lax.dot_general(wide_left(u_pair[terms + k], w), wide_right(right.get(k), w, 0), CONTRACT_FIRST,
-                                  preferred_element_type=F32)
-            for t in range(own):
-                total[tables[k, first_own + t]] += got[t * n:(t + 1) * n]
+
+    def one_term(k, carry):
+        got = lax.dot_general(wide_left(u_pair[k], w), wide_right(right.get(k), w, 1), CONTRACT_LAST,
+                              preferred_element_type=F32)
+        for t in range(own):
+            total[inverse[k, first_own + t]] += got[t * n:(t + 1) * n]
+        got = lax.dot_general(wide_left(u_pair[terms + k], w), wide_right(right.get(k), w, 0), CONTRACT_FIRST,
+                              preferred_element_type=F32)
+        for t in range(own):
+            total[tables[k, first_own + t]] += got[t * n:(t + 1) * n]
         return carry
 
-    lax.fori_loop(0, terms // unroll, second_stage, 0)
+    if terms <= 8:
+        for k in range(terms):
+            one_term(k, 0)
+    else:
+        lax.fori_loop(0, terms, one_term, 0)
+
+
+def apply_terms(plan, tables, inverse, lefts, right, source, u_pair, total):
+    first_products(plan, lefts, source, u_pair)
+    second_products(plan, tables, inverse, right, u_pair, total)
 
 
 def hand_out(plan, offsets, total, tables, rows_are, keep, send):
@@ -211,10 +219,22 @@
     return jnp.where(ok, wave[t], 0.0)
 
 
-def first_kernel(plan, tables, wave, left_ops, right_ops,
+class Tables:
+    def __init__(self, coupling, *sizes):
+        self.coupling, self.sizes, self.terms = coupling, sizes, coupling.shape[0]
+
+    def __getitem__(self, at):
+        row, sector = at
+        if isinstance(row, int) and row >= self.terms:
+            return self.sizes[row - self.terms][sector]
+        return self.coupling[row, sector]
+
+
+def first_kernel(plan, coupling, left_sizes, right_sizes, wave, left_ops, right_ops,
                  keep, send, pieces, packed,
                  wave_in, left_in, right_in, flipped, a_away, u_pair, total, inverse, sems):
     side, mine, _, my_rep = places(plan)
+    tables = Tables(coupling, left_sizes, right_sizes)
     loads = ((wave, wave_in), (right_ops, right_in), (left_ops, left_in))
     copies = [pltpu.make_async_copy(src, dst, sems.at[i]) for i, (src, dst) in enumerate(loads)]
     for copy in copies:
@@ -235,9 +255,10 @@
             pieces[off, t * plan.rows:(t + 1) * plan.rows] = value
     copies[1].wait()
     prepare_left(plan, right_in, flipped.at[pl.ds(plan.own, plan.terms)], away, home)
+    first_products(plan, away, source, u_pair)
     copies[2].wait()
     prepare_right(plan, left_in, right)
-    apply_terms(plan, tables, inverse, away, right, source, u_pair, total)
+    second_products(plan, tables, inverse, right, u_pair, total)
     hand_out(plan, range(1, plan.half), total, tables, 1, keep, send)
 
 
@@ -358,7 +379,6 @@
     chunks = jax.ShapeDtypeStruct((plan.half, plan.piece, w), F32)
     operators = pltpu.VMEM((terms, w, w), F32)
     turned_operators = pltpu.VMEM((terms, plan.part, w), F32)
-    tables = jnp.concatenate([coupling, left_sizes[None], right_sizes[None]])
 
     def ring_in_half(parts, at):
         run = parts[at(plan.half - 2)]
@@ -366,7 +386,7 @@
             run = plan.next_in_half(run) + parts[at(i)]
         return plan.next_in_half(run)
 
-    def along_half(keep, send, rows_are, names, home_args):
+    def along_half(keep, send, rows_are, names, home_args, tables):
         away = keep + plan.across_cores(send)
         away, home_args = lax.optimization_barrier((away, home_args))
         others = ring_in_half(away[1:], lambda i: (slice(None), i))
@@ -393,13 +413,15 @@
     keep, send, pieces, packs = call(
         first_kernel, plan.away,
         (spread(plan.half - 1),) * 2 + (chunks, packed("home", "right", "source")),
-        [smem] + [hbm] * 3,
+        [smem] * 3 + [hbm] * 3,
         [pltpu.VMEM(blocks.shape, F32), operators, operators, pltpu.VMEM((own + terms, plan.part, w), F32),
          pltpu.VMEM(packed("away").shape, BF16)] + work(plan.away) + [pltpu.SemaphoreType.DMA((3,))],
-    )(tables, *[pltpu.with_memory_space_constraint(x, pltpu.HBM)
-                for x in (wavefunction, left_operators, right_operators)])
-
-    others, home, got, sent = along_half(keep, send, 1, (("home", "right", "source"),), (packs,))
+    )(*[pltpu.with_memory_space_constraint(x, pltpu.HBM)
+        for x in (coupling, left_sizes, right_sizes, wavefunction, left_operators, right_operators)])
+    keep, *again = lax.optimization_barrier((keep, coupling, left_sizes, right_sizes))
+    tables = jnp.concatenate([again[0], again[1][None], again[2][None]])
+
+    others, home, got, sent = along_half(keep, send, 1, (("home", "right", "source"),), (packs,), tables)
     extra = sums_tile(
         [home * pieces[0]] + [sent[i] * pieces[1 + i] for i in range(plan.half - 1)], [pieces[0] ** 2],
         [(x * TINY) ** 2 for x in [home, *sent, *others]],
@@ -429,7 +451,7 @@
         [pltpu.VMEM(blocks.shape, F32), pltpu.VMEM((own, plan.part, w), F32)] + work(plan.away),
     )(tables, turned, a_away, packs, *units)
 
-    others, home, got, _ = along_half(keep, send, 0, (("home", "right"), ("source",)), (packs, s_pair))
+    others, home, got, _ = along_half(keep, send, 0, (("home", "right"), ("source",)), (packs, s_pair), tables)
     sigma, total, _ = along_sec(others, home + got, norm)
     entries = plan.sectors * w * w
     factor = norm[4:5] / jnp.sqrt(total[0:1] / entries + 1e-06)

time: 77.3 us -> 76.5 us (0.990)
    unnamed x6 -> x12, local copies, waits for them, and re-layouts: 3 us -> 3.02 us
  transfers between devices with their start and end apart: 17 -> 17, of which waited for: 10 -> 10; matrix products, arithmetic and copies ran while one was open for 0% -> 0% of each run, Pallas kernels for 18% -> 19%
where the time goes in v4:
time: 76.5 us; the launch traced here: 76.3 us
  Pallas kernels  30.2 us (39%)
  waiting for transfers between devices  23.8 us (31%)
  starting transfers between devices  17.1 us (22%)
  local copies, waits for them, and re-layouts  3.12 us (4%)
  other arithmetic  1.27 us (2%)
  between operations  0.84 us (1%)
    pallas_call x2, Pallas kernels, along_half(): call(functools.partial(home_kernel, rows_are, names), plan.block, (spread...  11.9 us
    pallas_call x1, Pallas kernels, on_device(): call(first_kernel, plan.away, (spread(plan.half - 1),) * 2 + (chunks, pac...  8.74 us
    ppermute x8, waiting for transfers between devices, across_cores(): return lax.ppermute(x, EVERYONE, self.perm(lambda o, s, r: (o, s, 1 - r)))  7.77 us
    pallas_call x1, Pallas kernels, on_device(): call(second_kernel, plan.away, (spread(plan.half - 1),) * 2 + (packed('so...  7.19 us
    ppermute x4, starting transfers between devices, next_in_half(): return lax.ppermute(x, EVERYONE, self.perm(move))  6.97 us
    ppermute x4, waiting for transfers between devices, next_in_half(): return lax.ppermute(x, EVERYONE, self.perm(move))  6.1 us
    ppermute x2, waiting for transfers between devices, next_sec(): lax.ppermute(x, EVERYONE, self.perm(lambda o, s, r: (o, (s + 1) % self.se...  5.45 us
    ppermute x2, starting transfers between devices, flip_op(): lax.ppermute(x, EVERYONE, self.perm(lambda o, s, r: (o ^ bits, s, r)))  3.24 us
  transfers between devices with their start and end apart: 17, of which 10 were waited for; matrix products, arithmetic and copies ran while one was open for 0% of the time, Pallas kernels for 19%

profile of v4, /device:TPU:0, one launch (start us, length us, event | category | flops | bytes accessed | tf_op | source)
XLA Modules:
  0.0 76.3 jit_solution(7392126534361715220)
XLA Ops:
  0.7 8.7 %shard_map.77 = (f32[2,1,192,256]{3,2,1,0:T(8,128)S(1)}, f32[2,1,192,256]{3,2,1,0:T(8,128)S(1)}, f32[2,192,256]{2,1,0:T(8,128)S(1)}, bf16[4608,512]{1,0:T(8,128)(2,1)S(1)}) custom-call(s32[8,12]{1,0:T(8,128)} %coupling.1, s32[12]{0:T(128)} %left_sizes.1, s32[12]{0:T(128)} %right_sizes.1, f32[6,256,256]{2,1,0:T(8,128)} %wave.2, f32[8,256,256]{2,1,0:T(8,128)} %left_ops.2, ...), custom_call_target="tpu_custom_call" | custom-call | flops 4831838208 | bytes 4194304 | tf_op jit(solution)/shard_map/pallas_call | solution.py:413
  9.4 0.5 collective-permute-start
  10.0 1.3 %collective-permute-done = f32[2,1,192,256]{3,2,1,0:T(8,128)S(1)} collective-permute-done((f32[2,1,192,256]{3,2,1,0:T(8,128)S(1)}, f32[2,1,192,256]{3,2,1,0:T(8,128)S(1)}, u32[]{:S(2)}, u32[]{:S(2)}) %collective-permute-start) | collective-permute-done | bytes 393248 | tf_op jit(solution)/shard_map/ppermute | solution.py:65
  11.4 3.0 %collective-permute-start.1 = (f32[1,192,256]{2,1,0:T(8,128)S(1)}, f32[1,192,256]{2,1,0:T(8,128)S(1)}, u32[]{:S(2)}, u32[]{:S(2)}) collective-permute-start(f32[1,192,256]{2,1,0:T(8,128)S(1)} %get-tuple-element.95), channel_id=1, source_target_pairs={{0,4},{1,5},{2,6},{3,7},{4,0},{5,1},{6,2},{7,3},{8,12},{9,13},{10,... | collective-permute-start | bytes 589832 | tf_op jit(solution)/shard_map/ppermute | solution.py:75
  14.4 6.0 %shard_map.78 = (f32[2,1,192,256]{3,2,1,0:T(8,128)S(1)}, f32[2,1,192,256]{3,2,1,0:T(8,128)S(1)}) custom-call(s32[10,12]{1,0:T(8,128)S(1)} %pad_add_fusion.tables, bf16[4608,512]{1,0:T(8,128)(2,1)S(1)} %get-tuple-element.51.refs_0_), custom_call_target="tpu_custom_call" | custom-call | flops 4831838208 | bytes 4194304 | tf_op jit(solution)/shard_map/pallas_call | solution.py:393
  20.4 0.1 collective-permute-start.2
  20.5 1.7 %collective-permute-done.2 = f32[2,1,192,256]{3,2,1,0:T(8,128)S(1)} collective-permute-done((f32[2,1,192,256]{3,2,1,0:T(8,128)S(1)}, f32[2,1,192,256]{3,2,1,0:T(8,128)S(1)}, u32[]{:S(2)}, u32[]{:S(2)}) %collective-permute-start.2) | collective-permute-done | bytes 393248 | tf_op jit(solution)/shard_map/ppermute | solution.py:65
  22.2 0.2 multiply_reduce_fusion.2
  22.4 1.6 %collective-permute-start.4 = (f32[200,256]{1,0:T(8,128)S(1)}, f32[200,256]{1,0:T(8,128)S(1)}, u32[]{:S(2)}, u32[]{:S(2)}) collective-permute-start(f32[200,256]{1,0:T(8,128)S(1)} %concatenate.14), channel_id=1, source_target_pairs={{0,2},{1,3},{2,0},{3,1},{4,6},{5,7},{6,4},{7,5},{8,10},{9,11},{10,... | collective-permute-start | bytes 614408 | tf_op jit(solution)/shard_map/ppermute | solution.py:68
  24.0 0.9 %collective-permute-start.3 = (f32[192,256]{1,0:T(8,128)S(1)}, f32[192,256]{1,0:T(8,128)S(1)}, u32[]{:S(2)}, u32[]{:S(2)}) collective-permute-start(f32[192,256]{1,0:T(8,128)S(1)} %bitcast.67), channel_id=1, source_target_pairs={{0,4},{1,5},{2,6},{3,7},{4,0},{5,1},{6,2},{7,3},{8,12},{9,13},{10,... | collective-permute-start | bytes 589832 | tf_op jit(solution)/shard_map/ppermute | solution.py:75
  24.9 5.8 %collective-permute-done.3 = f32[192,256]{1,0:T(8,128)S(1)} collective-permute-done((f32[192,256]{1,0:T(8,128)S(1)}, f32[192,256]{1,0:T(8,128)S(1)}, u32[]{:S(2)}, u32[]{:S(2)}) %collective-permute-start.3) | collective-permute-done | bytes 196640 | tf_op jit(solution)/shard_map/ppermute | solution.py:75
  30.8 3.0 %collective-permute-start.5 = (f32[200,256]{1,0:T(8,128)S(1)}, f32[200,256]{1,0:T(8,128)S(1)}, u32[]{:S(2)}, u32[]{:S(2)}) collective-permute-start(f32[200,256]{1,0:T(8,128)S(1)} %shard_map.79.rest_0_), channel_id=1, source_target_pairs={{0,12},{1,13},{2,14},{3,15},{4,8},{5,9},{6,10},{7,11},{8,4},{9,5},... | collective-permute-start | bytes 614408 | tf_op jit(solution)/shard_map/ppermute | solution.py:78
  33.8 0.2 collective-permute-start.6
  34.0 1.6 %copy-done.1 = f32[8,256,256]{2,1,0:T(8,128)S(1)} copy-done((f32[8,256,256]{2,1,0:T(8,128)S(1)}, f32[8,256,256]{2,1,0:T(8,128)}, u32[]{:S(2)}) %copy-start.1) | copy-done | bytes 2097176
  35.6 1.4 %copy-done.2 = f32[6,256,256]{2,1,0:T(8,128)S(1)} copy-done((f32[6,256,256]{2,1,0:T(8,128)S(1)}, f32[6,256,256]{2,1,0:T(8,128)}, u32[]{:S(2)}) %copy-start.2) | copy-done | bytes 1572888
  37.0 2.3 %shard_map.80 = (bf16[1024,512]{1,0:T(8,128)(2,1)S(1)}, bf16[3072,512]{1,0:T(8,128)(2,1)S(1)}, f32[6,256,256]{2,1,0:T(8,128)S(1)}) custom-call(s32[10,12]{1,0:T(8,128)S(1)} %pad_add_fusion.tables, f32[6,256,256]{2,1,0:T(8,128)S(1)} %copy-done.2, f32[8,256,256]{2,1,0:T(8,128)S(1)} %copy-done, f32[8,256,256]{2,1,0:T(8,128)S(1)} %copy-done.1), custom_call_target="tpu_custom_call" | custom-call | flops 75497472 | bytes 4194304 | tf_op jit(solution)/shard_map/pallas_call | solution.py:440
  39.3 1.4 %collective-permute-done.5.rest_3_ = f32[200,256]{1,0:T(8,128)S(1)} collective-permute-done((f32[200,256]{1,0:T(8,128)S(1)}, f32[200,256]{1,0:T(8,128)S(1)}, u32[]{:S(2)}, u32[]{:S(2)}) %collective-permute-start.5) | collective-permute-done | bytes 204832 | tf_op jit(solution)/shard_map/ppermute | solution.py:78
  40.7 3.2 %collective-permute-start.7 = (f32[200,256]{1,0:T(8,128)S(1)}, f32[200,256]{1,0:T(8,128)S(1)}, u32[]{:S(2)}, u32[]{:S(2)}) collective-permute-start(f32[200,256]{1,0:T(8,128)S(1)} %broadcast_select_fusion), channel_id=1, source_target_pairs={{0,8},{1,9},{2,10},{3,11},{4,0},{5,1},{6,2},{7,3},{8,12},{9,13},{1... | collective-permute-start | bytes 614408 | tf_op jit(solution)/shard_map/ppermute | solution.py:85
  43.9 0.5 collective-permute-start.11
  44.4 3.1 %collective-permute-done.7.rest_2_ = f32[200,256]{1,0:T(8,128)S(1)} collective-permute-done((f32[200,256]{1,0:T(8,128)S(1)}, f32[200,256]{1,0:T(8,128)S(1)}, u32[]{:S(2)}, u32[]{:S(2)}) %collective-permute-start.7) | collective-permute-done | bytes 204832 | tf_op jit(solution)/shard_map/ppermute | solution.py:85
  47.5 1.4 %collective-permute-done.10.rest_6_ = f32[200,256]{1,0:T(8,128)S(1)} collective-permute-done((f32[200,256]{1,0:T(8,128)S(1)}, f32[200,256]{1,0:T(8,128)S(1)}, u32[]{:S(2)}, u32[]{:S(2)}) %collective-permute-start.10) | collective-permute-done | bytes 204832 | tf_op jit(solution)/shard_map/ppermute | solution.py:65
  49.0 7.2 %shard_map.81 = (f32[2,1,192,256]{3,2,1,0:T(8,128)S(1)}, f32[2,1,192,256]{3,2,1,0:T(8,128)S(1)}, bf16[1536,512]{1,0:T(8,128)(2,1)S(1)}, f32[6,32,256]{2,1,0:T(8,128)}, f32[8,256]{1,0:T(8,128)S(1)}) custom-call(s32[10,12]{1,0:T(8,128)S(1)} %pad_add_fusion.tables, f32[6,256,256]{2,1,0:T(8,128)S(1)} %get-tuple-element.66.turned, ...), custom_call_target="tpu_custom_call" | custom-call | flops 4831838208 | bytes 4194304 | tf_op jit(solution)/shard_map/pallas_call | solution.py:446
  56.2 0.1 collective-permute-start.12
  56.3 1.6 %collective-permute-done.12 = f32[2,1,192,256]{3,2,1,0:T(8,128)S(1)} collective-permute-done((f32[2,1,192,256]{3,2,1,0:T(8,128)S(1)}, f32[2,1,192,256]{3,2,1,0:T(8,128)S(1)}, u32[]{:S(2)}, u32[]{:S(2)}) %collective-permute-start.12) | collective-permute-done | bytes 393248 | tf_op jit(solution)/shard_map/ppermute | solution.py:65
  58.0 2.2 %collective-permute-start.13 = (f32[1,192,256]{2,1,0:T(8,128)S(1)}, f32[1,192,256]{2,1,0:T(8,128)S(1)}, u32[]{:S(2)}, u32[]{:S(2)}) collective-permute-start(f32[1,192,256]{2,1,0:T(8,128)S(1)} %get-tuple-element.91), channel_id=1, source_target_pairs={{0,4},{1,5},{2,6},{3,7},{4,0},{5,1},{6,2},{7,3},{8,12},{9,13},{10,... | collective-permute-start | bytes 589832 | tf_op jit(solution)/shard_map/ppermute | solution.py:75
  60.2 6.0 %shard_map.82 = (f32[2,1,192,256]{3,2,1,0:T(8,128)S(1)}, f32[2,1,192,256]{3,2,1,0:T(8,128)S(1)}) custom-call(s32[10,12]{1,0:T(8,128)S(1)} %pad_add_fusion.tables, bf16[3072,512]{1,0:T(8,128)(2,1)S(1)} %get-tuple-element.74.packed.refs_0_, bf16[1536,512]{1,0:T(8,128)(2,1)S(1)} %get-tuple-element.75.refs_1_), custom_call_target="tpu_custom_call" | custom-call | flops 4831838208 | bytes 4194304 | tf_op jit(solution)/shard_map/pallas_call | solution.py:393
  66.2 1.7 %collective-permute-done.14 = f32[2,1,192,256]{3,2,1,0:T(8,128)S(1)} collective-permute-done((f32[2,1,192,256]{3,2,1,0:T(8,128)S(1)}, f32[2,1,192,256]{3,2,1,0:T(8,128)S(1)}, u32[]{:S(2)}, u32[]{:S(2)}) %collective-permute-start.14) | collective-permute-done | bytes 393248 | tf_op jit(solution)/shard_map/ppermute | solution.py:65
  68.0 0.8 %collective-permute-start.16 = (f32[200,256]{1,0:T(8,128)S(1)}, f32[200,256]{1,0:T(8,128)S(1)}, u32[]{:S(2)}, u32[]{:S(2)}) collective-permute-start(f32[200,256]{1,0:T(8,128)S(1)} %pad_maximum_fusion), channel_id=1, source_target_pairs={{0,2},{1,3},{2,0},{3,1},{4,6},{5,7},{6,4},{7,5},{8,10},{9,11},{10,... | collective-permute-start | bytes 614408 | tf_op jit(solution)/shard_map/ppermute | solution.py:68
  68.9 0.9 %collective-permute-start.15 = (f32[192,256]{1,0:T(8,128)S(1)}, f32[192,256]{1,0:T(8,128)S(1)}, u32[]{:S(2)}, u32[]{:S(2)}) collective-permute-start(f32[192,256]{1,0:T(8,128)S(1)} %bitcast.68), channel_id=1, source_target_pairs={{0,4},{1,5},{2,6},{3,7},{4,0},{5,1},{6,2},{7,3},{8,12},{9,13},{10,... | collective-permute-start | bytes 589832 | tf_op jit(solution)/shard_map/ppermute | solution.py:75
  69.8 5.4 %collective-permute-done.16 = f32[200,256]{1,0:T(8,128)S(1)} collective-permute-done((f32[200,256]{1,0:T(8,128)S(1)}, f32[200,256]{1,0:T(8,128)S(1)}, u32[]{:S(2)}, u32[]{:S(2)}) %collective-permute-start.16) | collective-permute-done | bytes 204832 | tf_op jit(solution)/shard_map/ppermute | solution.py:68
  75.2 0.3 collective-permute-done.15
  75.6 0.7 fusion
  (41 shorter events, 0.6 us)
Async XLA Ops:
  0.6 9.3 %copy-start.4 = (s32[12]{0:T(128)S(1)}, s32[12]{0:T(128)}, u32[]{:S(2)}) copy-start(s32[12]{0:T(128)} %right_sizes.1) | copy-start | bytes 148
  0.6 9.3 %copy-start.5 = (s32[12]{0:T(128)S(1)}, s32[12]{0:T(128)}, u32[]{:S(2)}) copy-start(s32[12]{0:T(128)} %left_sizes.1) | copy-start | bytes 148
  0.7 9.3 %copy-start.3 = (s32[8,12]{1,0:T(8,128)S(1)}, s32[8,12]{1,0:T(8,128)}, u32[]{:S(2)}) copy-start(s32[8,12]{1,0:T(8,128)} %coupling.1) | copy-start | bytes 1156
  9.4 1.9 %collective-permute-start = (f32[2,1,192,256]{3,2,1,0:T(8,128)S(1)}, f32[2,1,192,256]{3,2,1,0:T(8,128)S(1)}, u32[]{:S(2)}, u32[]{:S(2)}) collective-permute-start(f32[2,1,192,256]{3,2,1,0:T(8,128)S(1)} %get-tuple-element.48), channel_id=1, source_target_pairs={{0,1},{1,0},{2,3},{3,2},{4,5},{5,4},{6,7},{7,6},{8,9},{9,8},{10,11... | collective-permute-start | bytes 1179656 | tf_op jit(solution)/shard_map/ppermute | solution.py:65
  11.4 9.0 %collective-permute-start.1 = (f32[1,192,256]{2,1,0:T(8,128)S(1)}, f32[1,192,256]{2,1,0:T(8,128)S(1)}, u32[]{:S(2)}, u32[]{:S(2)}) collective-permute-start(f32[1,192,256]{2,1,0:T(8,128)S(1)} %get-tuple-element.95), channel_id=1, source_target_pairs={{0,4},{1,5},{2,6},{3,7},{4,0},{5,1},{6,2},{7,3},{8,12},{9,13},{10,... | collective-permute-start | bytes 589832 | tf_op jit(solution)/shard_map/ppermute | solution.py:75
  20.4 13.7 %copy-start = (f32[8,256,256]{2,1,0:T(8,128)S(1)}, f32[8,256,256]{2,1,0:T(8,128)}, u32[]{:S(2)}) copy-start(f32[8,256,256]{2,1,0:T(8,128)} %left_ops.2) | copy-start | bytes 6291460
  20.4 1.8 %collective-permute-start.2 = (f32[2,1,192,256]{3,2,1,0:T(8,128)S(1)}, f32[2,1,192,256]{3,2,1,0:T(8,128)S(1)}, u32[]{:S(2)}, u32[]{:S(2)}) collective-permute-start(f32[2,1,192,256]{3,2,1,0:T(8,128)S(1)} %get-tuple-element.55), channel_id=1, source_target_pairs={{0,1},{1,0},{2,3},{3,2},{4,5},{5,4},{6,7},{7,6},{8,9},{9,8},{10,11... | collective-permute-start | bytes 1179656 | tf_op jit(solution)/shard_map/ppermute | solution.py:65
  22.4 8.2 %collective-permute-start.4 = (f32[200,256]{1,0:T(8,128)S(1)}, f32[200,256]{1,0:T(8,128)S(1)}, u32[]{:S(2)}, u32[]{:S(2)}) collective-permute-start(f32[200,256]{1,0:T(8,128)S(1)} %concatenate.14), channel_id=1, source_target_pairs={{0,2},{1,3},{2,0},{3,1},{4,6},{5,7},{6,4},{7,5},{8,10},{9,11},{10,... | collective-permute-start | bytes 614408 | tf_op jit(solution)/shard_map/ppermute | solution.py:68
  24.0 6.7 %collective-permute-start.3 = (f32[192,256]{1,0:T(8,128)S(1)}, f32[192,256]{1,0:T(8,128)S(1)}, u32[]{:S(2)}, u32[]{:S(2)}) collective-permute-start(f32[192,256]{1,0:T(8,128)S(1)} %bitcast.67), channel_id=1, source_target_pairs={{0,4},{1,5},{2,6},{3,7},{4,0},{5,1},{6,2},{7,3},{8,12},{9,13},{10,... | collective-permute-start | bytes 589832 | tf_op jit(solution)/shard_map/ppermute | solution.py:75
  30.8 9.9 %collective-permute-start.5 = (f32[200,256]{1,0:T(8,128)S(1)}, f32[200,256]{1,0:T(8,128)S(1)}, u32[]{:S(2)}, u32[]{:S(2)}) collective-permute-start(f32[200,256]{1,0:T(8,128)S(1)} %shard_map.79.rest_0_), channel_id=1, source_target_pairs={{0,12},{1,13},{2,14},{3,15},{4,8},{5,9},{6,10},{7,11},{8,4},{9,5},... | collective-permute-start | bytes 614408 | tf_op jit(solution)/shard_map/ppermute | solution.py:78
  33.8 10.6 %collective-permute-start.6 = (f32[200,256]{1,0:T(8,128)S(1)}, f32[200,256]{1,0:T(8,128)S(1)}, u32[]{:S(2)}, u32[]{:S(2)}) collective-permute-start(f32[200,256]{1,0:T(8,128)S(1)} %shard_map.79.rest_0_), channel_id=1, source_target_pairs={{0,4},{1,5},{2,6},{3,7},{4,0},{5,1},{6,2},{7,3},{8,12},{9,13},{10,... | collective-permute-start | bytes 614408 | tf_op jit(solution)/shard_map/ppermute | solution.py:78
  34.0 1.6 %copy-start.1 = (f32[8,256,256]{2,1,0:T(8,128)S(1)}, f32[8,256,256]{2,1,0:T(8,128)}, u32[]{:S(2)}) copy-start(f32[8,256,256]{2,1,0:T(8,128)} %right_ops.2) | copy-start | bytes 6291460
  35.6 1.4 %copy-start.2 = (f32[6,256,256]{2,1,0:T(8,128)S(1)}, f32[6,256,256]{2,1,0:T(8,128)}, u32[]{:S(2)}) copy-start(f32[6,256,256]{2,1,0:T(8,128)} %wave.2) | copy-start | bytes 4718596
  40.7 6.8 %collective-permute-start.7 = (f32[200,256]{1,0:T(8,128)S(1)}, f32[200,256]{1,0:T(8,128)S(1)}, u32[]{:S(2)}, u32[]{:S(2)}) collective-permute-start(f32[200,256]{1,0:T(8,128)S(1)} %broadcast_select_fusion), channel_id=1, source_target_pairs={{0,8},{1,9},{2,10},{3,11},{4,0},{5,1},{6,2},{7,3},{8,12},{9,13},{1... | collective-permute-start | bytes 614408 | tf_op jit(solution)/shard_map/ppermute | solution.py:85
  43.9 3.6 %collective-permute-start.8 = (f32[200,256]{1,0:T(8,128)S(1)}, f32[200,256]{1,0:T(8,128)S(1)}, u32[]{:S(2)}, u32[]{:S(2)}) collective-permute-start(f32[200,256]{1,0:T(8,128)S(1)} %shard_map.79.rest_0_), channel_id=1, source_target_pairs={{0,1},{1,0},{2,3},{3,2},{4,5},{5,4},{6,7},{7,6},{8,9},{9,8},{10,11... | collective-permute-start | bytes 614408 | tf_op jit(solution)/shard_map/ppermute | solution.py:65
  43.9 3.6 %collective-permute-start.11 = (f32[200,256]{1,0:T(8,128)S(1)}, f32[200,256]{1,0:T(8,128)S(1)}, u32[]{:S(2)}, u32[]{:S(2)}) collective-permute-start(f32[200,256]{1,0:T(8,128)S(1)} %collective-permute-done.5.rest_3_), channel_id=1, source_target_pairs={{0,1},{1,0},{2,3},{3,2},{4,5},{5,4},{6,7},{7,6},{8,9},{9,8},{10,11... | collective-permute-start | bytes 614408 | tf_op jit(solution)/shard_map/ppermute | solution.py:65
  44.4 3.1 %collective-permute-start.9 = (f32[200,256]{1,0:T(8,128)S(1)}, f32[200,256]{1,0:T(8,128)S(1)}, u32[]{:S(2)}, u32[]{:S(2)}) collective-permute-start(f32[200,256]{1,0:T(8,128)S(1)} %collective-permute-done.6.rest_1_), channel_id=1, source_target_pairs={{0,1},{1,0},{2,3},{3,2},{4,5},{5,4},{6,7},{7,6},{8,9},{9,8},{10,11... | collective-permute-start | bytes 614408 | tf_op jit(solution)/shard_map/ppermute | solution.py:65
  47.5 1.5 %collective-permute-start.10 = (f32[200,256]{1,0:T(8,128)S(1)}, f32[200,256]{1,0:T(8,128)S(1)}, u32[]{:S(2)}, u32[]{:S(2)}) collective-permute-start(f32[200,256]{1,0:T(8,128)S(1)} %collective-permute-done.7.rest_2_), channel_id=1, source_target_pairs={{0,1},{1,0},{2,3},{3,2},{4,5},{5,4},{6,7},{7,6},{8,9},{9,8},{10,11... | collective-permute-start | bytes 614408 | tf_op jit(solution)/shard_map/ppermute | solution.py:65
  56.2 1.7 %collective-permute-start.12 = (f32[2,1,192,256]{3,2,1,0:T(8,128)S(1)}, f32[2,1,192,256]{3,2,1,0:T(8,128)S(1)}, u32[]{:S(2)}, u32[]{:S(2)}) collective-permute-start(f32[2,1,192,256]{3,2,1,0:T(8,128)S(1)} %get-tuple-element.71), channel_id=1, source_target_pairs={{0,1},{1,0},{2,3},{3,2},{4,5},{5,4},{6,7},{7,6},{8,9},{9,8},{10,11... | collective-permute-start | bytes 1179656 | tf_op jit(solution)/shard_map/ppermute | solution.py:65
  58.0 8.2 %collective-permute-start.13 = (f32[1,192,256]{2,1,0:T(8,128)S(1)}, f32[1,192,256]{2,1,0:T(8,128)S(1)}, u32[]{:S(2)}, u32[]{:S(2)}) collective-permute-start(f32[1,192,256]{2,1,0:T(8,128)S(1)} %get-tuple-element.91), channel_id=1, source_target_pairs={{0,4},{1,5},{2,6},{3,7},{4,0},{5,1},{6,2},{7,3},{8,12},{9,13},{10,... | collective-permute-start | bytes 589832 | tf_op jit(solution)/shard_map/ppermute | solution.py:75
  66.1 1.8 %collective-permute-start.14 = (f32[2,1,192,256]{3,2,1,0:T(8,128)S(1)}, f32[2,1,192,256]{3,2,1,0:T(8,128)S(1)}, u32[]{:S(2)}, u32[]{:S(2)}) collective-permute-start(f32[2,1,192,256]{3,2,1,0:T(8,128)S(1)} %get-tuple-element.79), channel_id=1, source_target_pairs={{0,1},{1,0},{2,3},{3,2},{4,5},{5,4},{6,7},{7,6},{8,9},{9,8},{10,11... | collective-permute-start | bytes 1179656 | tf_op jit(solution)/shard_map/ppermute | solution.py:65
  68.0 7.2 %collective-permute-start.16 = (f32[200,256]{1,0:T(8,128)S(1)}, f32[200,256]{1,0:T(8,128)S(1)}, u32[]{:S(2)}, u32[]{:S(2)}) collective-permute-start(f32[200,256]{1,0:T(8,128)S(1)} %pad_maximum_fusion), channel_id=1, source_target_pairs={{0,2},{1,3},{2,0},{3,1},{4,6},{5,7},{6,4},{7,5},{8,10},{9,11},{10,... | collective-permute-start | bytes 614408 | tf_op jit(solution)/shard_map/ppermute | solution.py:68
  68.9 6.7 %collective-permute-start.15 = (f32[192,256]{1,0:T(8,128)S(1)}, f32[192,256]{1,0:T(8,128)S(1)}, u32[]{:S(2)}, u32[]{:S(2)}) collective-permute-start(f32[192,256]{1,0:T(8,128)S(1)} %bitcast.68), channel_id=1, source_target_pairs={{0,4},{1,5},{2,6},{3,7},{4,0},{5,1},{6,2},{7,3},{8,12},{9,13},{10,... | collective-permute-start | bytes 589832 | tf_op jit(solution)/shard_map/ppermute | solution.py:75

commit v5 on v4

--- a/solution.py
+++ b/solution.py
@@ -192,7 +192,7 @@
     second_products(plan, tables, inverse, right, u_pair, total)
 
 
-def hand_out(plan, offsets, total, tables, rows_are, keep, send):
+def hand_out(plan, offsets, total, tables, rows_are, keep, send_others, send_ours):
     side, mine, my_sec, my_rep = places(plan)
     rows = plan.rows
     row_id = lax.broadcasted_iota(jnp.int32, (rows, plan.width), 0)
@@ -202,13 +202,16 @@
             for rep_off in range(plan.rep):
                 inner = pl.multiple_of(lax.rem(my_rep + rep_off, plan.rep) * rows, rows)
                 first_row = side * plan.part + lax.rem(mine + op_off, plan.half) * plan.block + inner
-                goal = send if rep_off else keep
+                if rep_off == 0:
+                    goal = keep.at[sec_off, i]
+                else:
+                    goal = send_others.at[sec_off - 1, i] if sec_off else send_ours.at[i]
                 for t in range(plan.own):
                     s = lax.rem(my_sec + sec_off, plan.sec) * plan.own + t
                     ok = row_id + first_row < tables[plan.terms + rows_are, s]
                     ok = ok & (col_id < tables[plan.terms + 1 - rows_are, s])
                     value = total[s, pl.ds(pl.multiple_of(i * plan.block + inner, rows), rows), :]
-                    goal[sec_off, i, t * rows:(t + 1) * rows] = jnp.where(ok, value, 0.0)
+                    goal[t * rows:(t + 1) * rows] = jnp.where(ok, value, 0.0)
 
 
 def masked_wave(plan, tables, wave, t):
@@ -230,19 +233,22 @@
         return self.coupling[row, sector]
 
 
-def first_kernel(plan, coupling, left_sizes, right_sizes, wave, left_ops, right_ops,
-                 keep, send, pieces, packed,
-                 wave_in, left_in, right_in, flipped, a_away, u_pair, total, inverse, sems):
+def first_kernel(plan, coupling_at, left_sizes_at, right_sizes_at, wave, left_ops, right_ops,
+                 keep, send_others, send_ours, pieces, packed,
+                 coupling, left_sizes, right_sizes, wave_in, left_in, right_in, flipped, a_away,
+                 u_pair, total, inverse, sems):
     side, mine, _, my_rep = places(plan)
     tables = Tables(coupling, left_sizes, right_sizes)
-    loads = ((wave, wave_in), (right_ops, right_in), (left_ops, left_in))
+    loads = ((wave, wave_in), (right_ops, right_in), (left_ops, left_in), (coupling_at, coupling),
+             (left_sizes_at, left_sizes), (right_sizes_at, right_sizes))
     copies = [pltpu.make_async_copy(src, dst, sems.at[i]) for i, (src, dst) in enumerate(loads)]
     for copy in copies:
         copy.start()
     home, right, source = stacks(plan, packed, "home", "right", "source")
     away, = stacks(plan, a_away, "away")
     half_at = pl.multiple_of(side * plan.part, plan.part)
-    copies[0].wait()
+    for i in (3, 4, 5, 0):
+        copies[i].wait()
     for t in range(plan.own):
         masked = masked_wave(plan, tables, wave_in, t)
         source.put(t, masked)
@@ -259,14 +265,15 @@
     copies[2].wait()
     prepare_right(plan, left_in, right)
     second_products(plan, tables, inverse, right, u_pair, total)
-    hand_out(plan, range(1, plan.half), total, tables, 1, keep, send)
+    hand_out(plan, range(1, plan.half), total, tables, 1, keep, send_others, send_ours)
 
 
 def home_kernel(rows_are, names, plan, tables, *refs):
-    packs, (keep, send, u_pair, total, inverse) = refs[:len(names)], refs[len(names):]
+    packs, refs = refs[:len(names)], refs[len(names):]
+    keep, send_others, send_ours, u_pair, total, inverse = refs
     home, right, source = [found for pack, part in zip(packs, names) for found in stacks(plan, pack, *part)]
     apply_terms(plan, tables, inverse, home, right, source, u_pair, total)
-    hand_out(plan, range(1), total, tables, rows_are, keep, send)
+    hand_out(plan, range(1), total, tables, rows_are, keep, send_others, send_ours)
 
 
 def prepare_kernel(plan, tables, wave, left_ops, right_ops, a_away, packed, turned, flipped):
@@ -280,42 +287,42 @@
 
 def second_kernel(plan, tables, turned, a_away, packed, *rest):
     units, rest = rest[:2 * plan.op], rest[2 * plan.op:]
-    (keep, send, s_pair, residual, norm, full, flipped, u_pair, total, inverse) = rest
+    (keep, send_others, send_ours, s_pair, full, norm, u_pair, total, inverse) = rest
     _, right = stacks(plan, packed, "home", "right")
     away, = stacks(plan, a_away, "away")
     source, = stacks(plan, s_pair, "source")
-    side, mine, _, my_rep = places(plan)
-    my_op = lax.axis_index("op")
+    my_op, my_rep = lax.axis_index("op"), lax.axis_index("rep")
     w, rows = plan.width, plan.rows
-    sums = jnp.zeros((TILE, w), F32)
-    for whose in range(2):
-        for bits in range(plan.op):
-            unit = units[whose * plan.op + bits]
-            r = my_rep if whose == 0 else 1 - my_rep
-            at = pl.multiple_of(((my_op ^ bits) * plan.rep + r) * rows, rows)
-            for t in range(plan.own):
-                full[t, pl.ds(at, rows), :] = unit[t * rows:(t + 1) * rows]
-            sums = sums + unit[plan.piece:]
+    sums = sum(unit[plan.piece:] for unit in units)
     entries = plan.sectors * w * w
     sums = jnp.broadcast_to(jnp.sum(sums, axis=1, keepdims=True), sums.shape)
     energy = sums[0:1] / sums[1:2]
     height = 1.0 + jnp.sqrt(sums[2:3] / entries) / TINY
     level = 1.0 / height
-    at = pl.multiple_of((mine * plan.rep + my_rep) * rows, rows)
-    half_at = pl.multiple_of(side * plan.part, plan.part)
-    squares = jnp.zeros((8, w), F32)
-    for t in range(plan.own):
-        res = full[t] - energy * turned[t]
-        squares = squares + jnp.sum((res * res).reshape(w // 8, 8, w), axis=0)
-        full[t] = res
-        source.put(t, res * level)
-    for t in range(plan.own):
-        flipped[t] = full[t, :, pl.ds(half_at, plan.part)].T
-        residual[t] = flipped[t, pl.ds(at, rows), :]
+    squares = jnp.zeros((TILE, w), F32)
+    for whose in range(2):
+        r = my_rep if whose == 0 else 1 - my_rep
+        for bits in range(plan.op):
+            unit = units[whose * plan.op + bits]
+            at = pl.multiple_of(((my_op ^ bits) * plan.rep + r) * rows, rows)
+            for t in range(plan.own):
+                res = unit[t * rows:(t + 1) * rows] - energy * turned[t, pl.ds(at, rows), :]
+                squares = squares + jnp.sum(res.reshape(rows // TILE, TILE, w) ** 2, axis=0)
+                full[t, pl.ds(at, rows), :] = res
+    for t in range(plan.own):
+        source.put(t, full[t] * level)
     norm[0:4] = jnp.full((4, w), jnp.sum(squares), F32)
     norm[4:8] = jnp.broadcast_to(height, (4, w))
     apply_terms(plan, tables, inverse, away, right, source, u_pair, total)
-    hand_out(plan, range(1, plan.half), total, tables, 0, keep, send)
+    hand_out(plan, range(1, plan.half), total, tables, 0, keep, send_others, send_ours)
+
+
+def residual_kernel(plan, full, residual, flipped):
+    side, mine, _, my_rep = places(plan)
+    at = pl.multiple_of((mine * plan.rep + my_rep) * plan.rows, plan.rows)
+    for t in range(plan.own):
+        flipped[t] = full[t, :, pl.ds(pl.multiple_of(side * plan.part, plan.part), plan.part)].T
+        residual[t] = flipped[t, pl.ds(at, plan.rows), :]
 
 
 def join_kernel(plan, sigma, extra, cross, unit):
@@ -351,7 +358,8 @@
     hbm = pl.BlockSpec(memory_space=pltpu.HBM)
 
     def spread(offsets):
-        return jax.ShapeDtypeStruct((plan.sec, offsets, plan.piece, w), F32)
+        shapes = ((plan.sec, offsets), (plan.sec - 1, offsets), (offsets,))
+        return tuple(jax.ShapeDtypeStruct(x + (plan.piece, w), F32) for x in shapes)
 
     def work(n):
         return [
@@ -386,17 +394,22 @@
             run = plan.next_in_half(run) + parts[at(i)]
         return plan.next_in_half(run)
 
-    def along_half(keep, send, rows_are, names, home_args, tables):
-        away = keep + plan.across_cores(send)
+    def along_half(sums, rows_are, names, home_args, tables):
+        keep, send_others, send_ours = sums
+        away = keep[1:] + plan.across_cores(send_others)
         away, home_args = lax.optimization_barrier((away, home_args))
-        others = ring_in_half(away[1:], lambda i: (slice(None), i))
+        sent = keep[0] + plan.across_cores(send_ours)
+        others = ring_in_half(away, lambda i: (slice(None), i))
         kept = call(
-            functools.partial(home_kernel, rows_are, names), plan.block, (spread(1),) * 2,
+            functools.partial(home_kernel, rows_are, names), plan.block, spread(1),
             [smem] + [vmem] * len(names), work(plan.block),
         )(tables, *home_args)
-        sent, others, kept = lax.optimization_barrier((away[0], others, kept))
-        home = (kept[0] + plan.across_cores(kept[1]))[:, 0]
-        return others + home[1:], home[0], ring_in_half(sent, lambda i: i), sent
+        others, kept = lax.optimization_barrier((others, kept))
+        keep, send_others, send_ours = kept
+        others = others + (keep[1:] + plan.across_cores(send_others))[:, 0]
+        home = (keep[0] + plan.across_cores(send_ours))[0]
+        going, _ = lax.optimization_barrier((sent, keep))
+        return others, home, ring_in_half(going, lambda i: i), sent
 
     def along_sec(others, ours, extra):
         if plan.sec == 2:
@@ -410,18 +423,19 @@
             extra = extra + plan.flip_sec(extra, bits)
         return ours + run, extra, run
 
-    keep, send, pieces, packs = call(
+    *sums, pieces, packs = call(
         first_kernel, plan.away,
-        (spread(plan.half - 1),) * 2 + (chunks, packed("home", "right", "source")),
-        [smem] * 3 + [hbm] * 3,
-        [pltpu.VMEM(blocks.shape, F32), operators, operators, pltpu.VMEM((own + terms, plan.part, w), F32),
-         pltpu.VMEM(packed("away").shape, BF16)] + work(plan.away) + [pltpu.SemaphoreType.DMA((3,))],
+        spread(plan.half - 1) + (chunks, packed("home", "right", "source")),
+        [hbm] * 6,
+        [pltpu.SMEM(x.shape, x.dtype) for x in (coupling, left_sizes, right_sizes)]
+        + [pltpu.VMEM(blocks.shape, F32), operators, operators, pltpu.VMEM((own + terms, plan.part, w), F32),
+         pltpu.VMEM(packed("away").shape, BF16)] + work(plan.away) + [pltpu.SemaphoreType.DMA((6,))],
     )(*[pltpu.with_memory_space_constraint(x, pltpu.HBM)
         for x in (coupling, left_sizes, right_sizes, wavefunction, left_operators, right_operators)])
-    keep, *again = lax.optimization_barrier((keep, coupling, left_sizes, right_sizes))
+    sums, *again = lax.optimization_barrier((sums, coupling, left_sizes, right_sizes))
     tables = jnp.concatenate([again[0], again[1][None], again[2][None]])
 
-    others, home, got, sent = along_half(keep, send, 1, (("home", "right", "source"),), (packs,), tables)
+    others, home, got, sent = along_half(sums, 1, (("home", "right", "source"),), (packs,), tables)
     extra = sums_tile(
         [home * pieces[0]] + [sent[i] * pieces[1 + i] for i in range(plan.half - 1)], [pieces[0] ** 2],
         [(x * TINY) ** 2 for x in [home, *sent, *others]],
@@ -443,16 +457,18 @@
     units, (a_away, packs, turned) = gather_along_op(plan, unit, prepared)
     units = units + [plan.across_cores(x) for x in units]
 
-    keep, send, s_pair, residual, norm = call(
+    *sums, s_pair, full, norm = call(
         second_kernel, plan.away,
-        (spread(plan.half - 1),) * 2 + (packed("source"), jax.ShapeDtypeStruct((own, rows, w), F32),
-                                        jax.ShapeDtypeStruct((TILE, w), F32)),
+        spread(plan.half - 1) + (packed("source"), blocks, jax.ShapeDtypeStruct((TILE, w), F32)),
         [smem] + [vmem] * (3 + len(units)),
-        [pltpu.VMEM(blocks.shape, F32), pltpu.VMEM((own, plan.part, w), F32)] + work(plan.away),
+        work(plan.away),
     )(tables, turned, a_away, packs, *units)
 
-    others, home, got, _ = along_half(keep, send, 0, (("home", "right"), ("source",)), (packs, s_pair), tables)
+    others, home, got, _ = along_half(sums, 0, (("home", "right"), ("source",)), (packs, s_pair), tables)
+    residual, = call(residual_kernel, 1, (jax.ShapeDtypeStruct((own, rows, w), F32),), [vmem],
+                     [pltpu.VMEM((own, plan.part, w), F32)])(full)
     sigma, total, _ = along_sec(others, home + got, norm)
+    sigma, residual = lax.optimization_barrier((sigma, residual))
     entries = plan.sectors * w * w
     factor = norm[4:5] / jnp.sqrt(total[0:1] / entries + 1e-06)
     sigma_next = (sigma * factor).reshape(own, rows, w)

time: 76.5 us -> 74.3 us (0.971)
  waiting for transfers between devices: 23.8 us -> 20.6 us
  starting transfers between devices: 17.1 us -> 18.1 us
    ppermute x8 -> x12, waiting for transfers between devices: 7.77 us -> 4.22 us  [across_cores(): return lax.ppermute(x, EVERYONE, self.perm(lambda o, s, r: (o, s, 1 - r)))]
    ppermute x8 -> x12, starting transfers between devices: 1.32 us -> 2.45 us  [across_cores(): return lax.ppermute(x, EVERYONE, self.perm(lambda o, s, r: (o, s, 1 - r)))]
    pallas_call x4 -> x5, Pallas kernels: 27.9 us -> 27.4 us  [the longest x2 12 us: along_half(): call(functools.partial(home_kernel, rows_are, names), plan.block, spread(...]
  transfers between devices with their start and end apart: 17 -> 21, of which waited for: 10 -> 10; matrix products, arithmetic and copies ran while one was open for 0% -> 1% of each run, Pallas kernels for 19% -> 21%
where the time goes in v5:
time: 74.3 us; the launch traced here: 74.2 us
  Pallas kernels  29.7 us (40%)
  waiting for transfers between devices  20.6 us (28%)
  starting transfers between devices  18.1 us (24%)
  local copies, waits for them, and re-layouts  3.06 us (4%)
  other arithmetic  1.85 us (2%)
  between operations  0.83 us (1%)
    pallas_call x2, Pallas kernels, along_half(): call(functools.partial(home_kernel, rows_are, names), plan.block, spread(...  12 us
    pallas_call x1, Pallas kernels, on_device(): call(first_kernel, plan.away, spread(plan.half - 1) + (chunks, packed('ho...  7.93 us
    ppermute x4, starting transfers between devices, next_in_half(): return lax.ppermute(x, EVERYONE, self.perm(move))  6.97 us
    pallas_call x1, Pallas kernels, on_device(): call(second_kernel, plan.away, spread(plan.half - 1) + (packed('source'),...  6.54 us
    ppermute x4, waiting for transfers between devices, next_in_half(): return lax.ppermute(x, EVERYONE, self.perm(move))  6.31 us
    ppermute x2, waiting for transfers between devices, next_sec(): lax.ppermute(x, EVERYONE, self.perm(lambda o, s, r: (o, (s + 1) % self.se...  5.58 us
    ppermute x12, waiting for transfers between devices, across_cores(): return lax.ppermute(x, EVERYONE, self.perm(lambda o, s, r: (o, s, 1 - r)))  4.22 us
    ppermute x1, starting transfers between devices, onward(): return lax.ppermute(x, EVERYONE, self.perm(lambda o, s, r: (to[o], s, r)))  3.31 us
  transfers between devices with their start and end apart: 21, of which 10 were waited for; matrix products, arithmetic and copies ran while one was open for 1% of the time, Pallas kernels for 21%

profile of v5, /device:TPU:0, one launch (start us, length us, event | category | flops | bytes accessed | tf_op | source)
XLA Modules:
  0.0 74.2 jit_solution(8306306039107870176)
XLA Ops:
  0.7 7.9 %shard_map.77 = (f32[2,1,192,256]{3,2,1,0:T(8,128)S(1)}, f32[1,1,192,256]{3,2,1,0:T(8,128)S(1)}, f32[1,192,256]{2,1,0:T(8,128)S(1)}, f32[2,192,256]{2,1,0:T(8,128)S(1)}, bf16[4608,512]{1,0:T(8,128)(2,1)S(1)}) custom-call(s32[8,12]{1,0:T(8,128)} %coupling_at.1, s32[12]{0:T(128)} %left_sizes_at.1, s32[12]{0:T(128)} %right_sizes_at.1, f32[6,256,256]{2,1,0:T(8,128)} %wave.2, ...), custom_call_target="tpu_custom_call" | custom-call | flops 4831838208 | bytes 4194304 | tf_op jit(solution)/shard_map/pallas_call | solution.py:426
  8.6 0.5 collective-permute-start
  9.2 1.0 %collective-permute-done = f32[1,1,192,256]{3,2,1,0:T(8,128)S(1)} collective-permute-done((f32[1,1,192,256]{3,2,1,0:T(8,128)S(1)}, f32[1,1,192,256]{3,2,1,0:T(8,128)S(1)}, u32[]{:S(2)}, u32[]{:S(2)}) %collective-permute-start) | collective-permute-done | bytes 196640 | tf_op jit(solution)/shard_map/ppermute | solution.py:65
  10.2 3.0 %collective-permute-start.1 = (f32[1,192,256]{2,1,0:T(8,128)S(1)}, f32[1,192,256]{2,1,0:T(8,128)S(1)}, u32[]{:S(2)}, u32[]{:S(2)}) collective-permute-start(f32[1,192,256]{2,1,0:T(8,128)S(1)} %bitcast.72), channel_id=1, source_target_pairs={{0,4},{1,5},{2,6},{3,7},{4,0},{5,1},{6,2},{7,3},{8,12},{9,13},{10,... | collective-permute-start | bytes 589832 | tf_op jit(solution)/shard_map/ppermute | solution.py:75
  13.2 6.0 %shard_map.78 = (f32[2,1,192,256]{3,2,1,0:T(8,128)S(1)}, f32[1,1,192,256]{3,2,1,0:T(8,128)S(1)}, f32[1,192,256]{2,1,0:T(8,128)S(1)}) custom-call(s32[10,12]{1,0:T(8,128)S(1)} %pad_add_fusion.tables, bf16[4608,512]{1,0:T(8,128)(2,1)S(1)} %get-tuple-element.63.refs_0_), custom_call_target="tpu_custom_call" | custom-call | flops 4831838208 | bytes 4194304 | tf_op jit(solution)/shard_map/pallas_call | solution.py:403
  19.3 0.5 collective-permute-start.5
  19.8 0.7 multiply_reduce_fusion.1
  20.6 0.2 collective-permute-done.2
  20.8 0.3 collective-permute-done.5
  21.2 1.5 %collective-permute-start.6 = (f32[200,256]{1,0:T(8,128)S(1)}, f32[200,256]{1,0:T(8,128)S(1)}, u32[]{:S(2)}, u32[]{:S(2)}) collective-permute-start(f32[200,256]{1,0:T(8,128)S(1)} %concatenate.14), channel_id=1, source_target_pairs={{0,2},{1,3},{2,0},{3,1},{4,6},{5,7},{6,4},{7,5},{8,10},{9,11},{10,... | collective-permute-start | bytes 614408 | tf_op jit(solution)/shard_map/ppermute | solution.py:68
  22.8 0.9 %collective-permute-start.4 = (f32[192,256]{1,0:T(8,128)}, f32[192,256]{1,0:T(8,128)S(1)}, u32[]{:S(2)}, u32[]{:S(2)}) collective-permute-start(f32[192,256]{1,0:T(8,128)} %bitcast.69), channel_id=1, source_target_pairs={{0,4},{1,5},{2,6},{3,7},{4,0},{5,1},{6,2},{7,3},{8,12},{9,13},{10,... | collective-permute-start | bytes 589832 | tf_op jit(solution)/shard_map/ppermute | solution.py:75
  23.6 6.1 %collective-permute-done.4 = f32[192,256]{1,0:T(8,128)S(1)} collective-permute-done((f32[192,256]{1,0:T(8,128)}, f32[192,256]{1,0:T(8,128)S(1)}, u32[]{:S(2)}, u32[]{:S(2)}) %collective-permute-start.4) | collective-permute-done | bytes 196640 | tf_op jit(solution)/shard_map/ppermute | solution.py:75
  29.9 3.0 %collective-permute-start.7 = (f32[200,256]{1,0:T(8,128)S(1)}, f32[200,256]{1,0:T(8,128)S(1)}, u32[]{:S(2)}, u32[]{:S(2)}) collective-permute-start(f32[200,256]{1,0:T(8,128)S(1)} %shard_map.79.rest_0_), channel_id=1, source_target_pairs={{0,12},{1,13},{2,14},{3,15},{4,8},{5,9},{6,10},{7,11},{8,4},{9,5},... | collective-permute-start | bytes 614408 | tf_op jit(solution)/shard_map/ppermute | solution.py:78
  32.8 0.3 collective-permute-start.8
  33.1 1.6 %copy-done.1 = f32[8,256,256]{2,1,0:T(8,128)S(1)} copy-done((f32[8,256,256]{2,1,0:T(8,128)S(1)}, f32[8,256,256]{2,1,0:T(8,128)}, u32[]{:S(2)}) %copy-start.1) | copy-done | bytes 2097176
  34.7 1.4 %copy-done.2 = f32[6,256,256]{2,1,0:T(8,128)S(1)} copy-done((f32[6,256,256]{2,1,0:T(8,128)S(1)}, f32[6,256,256]{2,1,0:T(8,128)}, u32[]{:S(2)}) %copy-start.2) | copy-done | bytes 1572888
  36.1 2.3 %shard_map.80 = (bf16[1024,512]{1,0:T(8,128)(2,1)S(1)}, bf16[3072,512]{1,0:T(8,128)(2,1)S(1)}, f32[6,256,256]{2,1,0:T(8,128)S(1)}) custom-call(s32[10,12]{1,0:T(8,128)S(1)} %pad_add_fusion.tables, f32[6,256,256]{2,1,0:T(8,128)S(1)} %copy-done.2, f32[8,256,256]{2,1,0:T(8,128)S(1)} %copy-done, f32[8,256,256]{2,1,0:T(8,128)S(1)} %copy-done.1), custom_call_target="tpu_custom_call" | custom-call | flops 75497472 | bytes 4194304 | tf_op jit(solution)/shard_map/pallas_call | solution.py:454
  38.4 1.4 %collective-permute-done.7.rest_3_ = f32[200,256]{1,0:T(8,128)S(1)} collective-permute-done((f32[200,256]{1,0:T(8,128)S(1)}, f32[200,256]{1,0:T(8,128)S(1)}, u32[]{:S(2)}, u32[]{:S(2)}) %collective-permute-start.7) | collective-permute-done | bytes 204832 | tf_op jit(solution)/shard_map/ppermute | solution.py:78
  39.8 3.3 %collective-permute-start.9 = (f32[200,256]{1,0:T(8,128)S(1)}, f32[200,256]{1,0:T(8,128)S(1)}, u32[]{:S(2)}, u32[]{:S(2)}) collective-permute-start(f32[200,256]{1,0:T(8,128)S(1)} %broadcast_select_fusion), channel_id=1, source_target_pairs={{0,8},{1,9},{2,10},{3,11},{4,0},{5,1},{6,2},{7,3},{8,12},{9,13},{1... | collective-permute-start | bytes 614408 | tf_op jit(solution)/shard_map/ppermute | solution.py:85
  43.1 0.5 collective-permute-start.13
  43.6 3.1 %collective-permute-done.9.rest_2_ = f32[200,256]{1,0:T(8,128)S(1)} collective-permute-done((f32[200,256]{1,0:T(8,128)S(1)}, f32[200,256]{1,0:T(8,128)S(1)}, u32[]{:S(2)}, u32[]{:S(2)}) %collective-permute-start.9) | collective-permute-done | bytes 204832 | tf_op jit(solution)/shard_map/ppermute | solution.py:85
  46.7 1.4 %collective-permute-done.12.rest_6_ = f32[200,256]{1,0:T(8,128)S(1)} collective-permute-done((f32[200,256]{1,0:T(8,128)S(1)}, f32[200,256]{1,0:T(8,128)S(1)}, u32[]{:S(2)}, u32[]{:S(2)}) %collective-permute-start.12) | collective-permute-done | bytes 204832 | tf_op jit(solution)/shard_map/ppermute | solution.py:65
  48.1 6.5 %shard_map.81 = (f32[2,1,192,256]{3,2,1,0:T(8,128)S(1)}, f32[1,1,192,256]{3,2,1,0:T(8,128)S(1)}, f32[1,192,256]{2,1,0:T(8,128)S(1)}, bf16[1536,512]{1,0:T(8,128)...) custom-call(s32[10,12]{1,0:T(8,128)S(1)} %pad_add_fusion.tables, ...), custom_call_target="tpu_custom_call" | custom-call | flops 4831838208 | bytes 4194304 | tf_op jit(solution)/shard_map/pallas_call | solution.py:460
  54.9 1.3 %collective-permute-done.14 = f32[1,1,192,256]{3,2,1,0:T(8,128)S(1)} collective-permute-done((f32[1,1,192,256]{3,2,1,0:T(8,128)S(1)}, f32[1,1,192,256]{3,2,1,0:T(8,128)S(1)}, u32[]{:S(2)}, u32[]{:S(2)}) %collective-permute-start.14) | collective-permute-done | bytes 196640 | tf_op jit(solution)/shard_map/ppermute | solution.py:65
  56.2 2.2 %collective-permute-start.15 = (f32[1,192,256]{2,1,0:T(8,128)S(1)}, f32[1,192,256]{2,1,0:T(8,128)S(1)}, u32[]{:S(2)}, u32[]{:S(2)}) collective-permute-start(f32[1,192,256]{2,1,0:T(8,128)S(1)} %bitcast.71), channel_id=1, source_target_pairs={{0,4},{1,5},{2,6},{3,7},{4,0},{5,1},{6,2},{7,3},{8,12},{9,13},{10,... | collective-permute-start | bytes 589832 | tf_op jit(solution)/shard_map/ppermute | solution.py:75
  58.4 6.0 %shard_map.82 = (f32[2,1,192,256]{3,2,1,0:T(8,128)S(1)}, f32[1,1,192,256]{3,2,1,0:T(8,128)S(1)}, f32[1,192,256]{2,1,0:T(8,128)S(1)}) custom-call(s32[10,12]{1,0:T(8,128)S(1)} %pad_add_fusion.tables, bf16[3072,512]{1,0:T(8,128)(2,1)S(1)} %get-tuple-element.89.packed.refs_0_, bf16[1536,512]{1,0:T(8,128)(2,1)S(1)} %get-tuple-element.90.refs_1_), custom_call_target="tpu_custom_call" | custom-call | flops 4831838208 | bytes 4194304 | tf_op jit(solution)/shard_map/pallas_call | solution.py:403
  64.5 0.5 collective-permute-start.17
  65.0 1.0 %shard_map.83 = f32[6,32,256]{2,1,0:T(8,128)} custom-call(f32[6,256,256]{2,1,0:T(8,128)S(1)} %get-tuple-element.101.full), custom_call_target="tpu_custom_call" | custom-call | flops 75497472 | bytes 4194304 | tf_op jit(solution)/shard_map/pallas_call | solution.py:468
  66.0 0.6 collective-permute-start.20
  66.7 0.9 %collective-permute-start.18 = (f32[192,256]{1,0:T(8,128)S(1)}, f32[192,256]{1,0:T(8,128)S(1)}, u32[]{:S(2)}, u32[]{:S(2)}) collective-permute-start(f32[192,256]{1,0:T(8,128)S(1)} %bitcast.70), channel_id=1, source_target_pairs={{0,4},{1,5},{2,6},{3,7},{4,0},{5,1},{6,2},{7,3},{8,12},{9,13},{10,... | collective-permute-start | bytes 589832 | tf_op jit(solution)/shard_map/ppermute | solution.py:75
  67.6 5.6 %collective-permute-done.20 = f32[200,256]{1,0:T(8,128)S(1)} collective-permute-done((f32[200,256]{1,0:T(8,128)S(1)}, f32[200,256]{1,0:T(8,128)S(1)}, u32[]{:S(2)}, u32[]{:S(2)}) %collective-permute-start.20) | collective-permute-done | bytes 204832 | tf_op jit(solution)/shard_map/ppermute | solution.py:68
  73.5 0.7 broadcast_multiply_fusion
  (49 shorter events, 1.2 us)
Async XLA Ops:
  0.6 8.6 %copy-start.4 = (s32[12]{0:T(128)S(1)}, s32[12]{0:T(128)}, u32[]{:S(2)}) copy-start(s32[12]{0:T(128)} %right_sizes_at.1) | copy-start | bytes 148
  0.6 8.6 %copy-start.5 = (s32[12]{0:T(128)S(1)}, s32[12]{0:T(128)}, u32[]{:S(2)}) copy-start(s32[12]{0:T(128)} %left_sizes_at.1) | copy-start | bytes 148
  0.7 8.6 %copy-start.3 = (s32[8,12]{1,0:T(8,128)S(1)}, s32[8,12]{1,0:T(8,128)}, u32[]{:S(2)}) copy-start(s32[8,12]{1,0:T(8,128)} %coupling_at.1) | copy-start | bytes 1156
  8.6 1.6 %collective-permute-start = (f32[1,1,192,256]{3,2,1,0:T(8,128)S(1)}, f32[1,1,192,256]{3,2,1,0:T(8,128)S(1)}, u32[]{:S(2)}, u32[]{:S(2)}) collective-permute-start(f32[1,1,192,256]{3,2,1,0:T(8,128)S(1)} %get-tuple-element.60), channel_id=1, source_target_pairs={{0,1},{1,0},{2,3},{3,2},{4,5},{5,4},{6,7},{7,6},{8,9},{9,8},{10,11... | collective-permute-start | bytes 589832 | tf_op jit(solution)/shard_map/ppermute | solution.py:65
  9.1 10.7 %collective-permute-start.3 = (f32[1,192,256]{2,1,0:T(8,128)S(1)}, f32[1,192,256]{2,1,0:T(8,128)S(1)}, u32[]{:S(2)}, u32[]{:S(2)}) collective-permute-start(f32[1,192,256]{2,1,0:T(8,128)S(1)} %get-tuple-element.69), channel_id=1, source_target_pairs={{0,1},{1,0},{2,3},{3,2},{4,5},{5,4},{6,7},{7,6},{8,9},{9,8},{10,11... | collective-permute-start | bytes 589832 | tf_op jit(solution)/shard_map/ppermute | solution.py:65
  10.2 9.0 %collective-permute-start.1 = (f32[1,192,256]{2,1,0:T(8,128)S(1)}, f32[1,192,256]{2,1,0:T(8,128)S(1)}, u32[]{:S(2)}, u32[]{:S(2)}) collective-permute-start(f32[1,192,256]{2,1,0:T(8,128)S(1)} %bitcast.72), channel_id=1, source_target_pairs={{0,4},{1,5},{2,6},{3,7},{4,0},{5,1},{6,2},{7,3},{8,12},{9,13},{10,... | collective-permute-start | bytes 589832 | tf_op jit(solution)/shard_map/ppermute | solution.py:75
  19.3 1.5 %collective-permute-start.2 = (f32[1,192,256]{2,1,0:T(8,128)S(1)}, f32[1,192,256]{2,1,0:T(8,128)S(1)}, u32[]{:S(2)}, u32[]{:S(2)}) collective-permute-start(f32[1,192,256]{2,1,0:T(8,128)S(1)} %get-tuple-element.68), channel_id=1, source_target_pairs={{0,1},{1,0},{2,3},{3,2},{4,5},{5,4},{6,7},{7,6},{8,9},{9,8},{10,11... | collective-permute-start | bytes 589832 | tf_op jit(solution)/shard_map/ppermute | solution.py:65
  19.3 1.7 %collective-permute-start.5 = (f32[1,1,192,256]{3,2,1,0:T(8,128)S(1)}, f32[1,1,192,256]{3,2,1,0:T(8,128)S(1)}, u32[]{:S(2)}, u32[]{:S(2)}) collective-permute-start(f32[1,1,192,256]{3,2,1,0:T(8,128)S(1)} %get-tuple-element.72), channel_id=1, source_target_pairs={{0,1},{1,0},{2,3},{3,2},{4,5},{5,4},{6,7},{7,6},{8,9},{9,8},{10,11... | collective-permute-start | bytes 589832 | tf_op jit(solution)/shard_map/ppermute | solution.py:65
  19.8 13.3 %copy-start = (f32[8,256,256]{2,1,0:T(8,128)S(1)}, f32[8,256,256]{2,1,0:T(8,128)}, u32[]{:S(2)}) copy-start(f32[8,256,256]{2,1,0:T(8,128)} %left_ops.2) | copy-start | bytes 6291460
  21.2 8.5 %collective-permute-start.6 = (f32[200,256]{1,0:T(8,128)S(1)}, f32[200,256]{1,0:T(8,128)S(1)}, u32[]{:S(2)}, u32[]{:S(2)}) collective-permute-start(f32[200,256]{1,0:T(8,128)S(1)} %concatenate.14), channel_id=1, source_target_pairs={{0,2},{1,3},{2,0},{3,1},{4,6},{5,7},{6,4},{7,5},{8,10},{9,11},{10,... | collective-permute-start | bytes 614408 | tf_op jit(solution)/shard_map/ppermute | solution.py:68
  22.8 7.0 %collective-permute-start.4 = (f32[192,256]{1,0:T(8,128)}, f32[192,256]{1,0:T(8,128)S(1)}, u32[]{:S(2)}, u32[]{:S(2)}) collective-permute-start(f32[192,256]{1,0:T(8,128)} %bitcast.69), channel_id=1, source_target_pairs={{0,4},{1,5},{2,6},{3,7},{4,0},{5,1},{6,2},{7,3},{8,12},{9,13},{10,... | collective-permute-start | bytes 589832 | tf_op jit(solution)/shard_map/ppermute | solution.py:75
  29.9 9.9 %collective-permute-start.7 = (f32[200,256]{1,0:T(8,128)S(1)}, f32[200,256]{1,0:T(8,128)S(1)}, u32[]{:S(2)}, u32[]{:S(2)}) collective-permute-start(f32[200,256]{1,0:T(8,128)S(1)} %shard_map.79.rest_0_), channel_id=1, source_target_pairs={{0,12},{1,13},{2,14},{3,15},{4,8},{5,9},{6,10},{7,11},{8,4},{9,5},... | collective-permute-start | bytes 614408 | tf_op jit(solution)/shard_map/ppermute | solution.py:78
  32.8 10.8 %collective-permute-start.8 = (f32[200,256]{1,0:T(8,128)S(1)}, f32[200,256]{1,0:T(8,128)S(1)}, u32[]{:S(2)}, u32[]{:S(2)}) collective-permute-start(f32[200,256]{1,0:T(8,128)S(1)} %shard_map.79.rest_0_), channel_id=1, source_target_pairs={{0,4},{1,5},{2,6},{3,7},{4,0},{5,1},{6,2},{7,3},{8,12},{9,13},{10,... | collective-permute-start | bytes 614408 | tf_op jit(solution)/shard_map/ppermute | solution.py:78
  33.1 1.6 %copy-start.1 = (f32[8,256,256]{2,1,0:T(8,128)S(1)}, f32[8,256,256]{2,1,0:T(8,128)}, u32[]{:S(2)}) copy-start(f32[8,256,256]{2,1,0:T(8,128)} %right_ops.2) | copy-start | bytes 6291460
  34.7 1.4 %copy-start.2 = (f32[6,256,256]{2,1,0:T(8,128)S(1)}, f32[6,256,256]{2,1,0:T(8,128)}, u32[]{:S(2)}) copy-start(f32[6,256,256]{2,1,0:T(8,128)} %wave.2) | copy-start | bytes 4718596
  39.8 6.9 %collective-permute-start.9 = (f32[200,256]{1,0:T(8,128)S(1)}, f32[200,256]{1,0:T(8,128)S(1)}, u32[]{:S(2)}, u32[]{:S(2)}) collective-permute-start(f32[200,256]{1,0:T(8,128)S(1)} %broadcast_select_fusion), channel_id=1, source_target_pairs={{0,8},{1,9},{2,10},{3,11},{4,0},{5,1},{6,2},{7,3},{8,12},{9,13},{1... | collective-permute-start | bytes 614408 | tf_op jit(solution)/shard_map/ppermute | solution.py:85
  43.1 3.6 %collective-permute-start.10 = (f32[200,256]{1,0:T(8,128)S(1)}, f32[200,256]{1,0:T(8,128)S(1)}, u32[]{:S(2)}, u32[]{:S(2)}) collective-permute-start(f32[200,256]{1,0:T(8,128)S(1)} %shard_map.79.rest_0_), channel_id=1, source_target_pairs={{0,1},{1,0},{2,3},{3,2},{4,5},{5,4},{6,7},{7,6},{8,9},{9,8},{10,11... | collective-permute-start | bytes 614408 | tf_op jit(solution)/shard_map/ppermute | solution.py:65
  43.1 3.6 %collective-permute-start.13 = (f32[200,256]{1,0:T(8,128)S(1)}, f32[200,256]{1,0:T(8,128)S(1)}, u32[]{:S(2)}, u32[]{:S(2)}) collective-permute-start(f32[200,256]{1,0:T(8,128)S(1)} %collective-permute-done.7.rest_3_), channel_id=1, source_target_pairs={{0,1},{1,0},{2,3},{3,2},{4,5},{5,4},{6,7},{7,6},{8,9},{9,8},{10,11... | collective-permute-start | bytes 614408 | tf_op jit(solution)/shard_map/ppermute | solution.py:65
  43.6 3.1 %collective-permute-start.11 = (f32[200,256]{1,0:T(8,128)S(1)}, f32[200,256]{1,0:T(8,128)S(1)}, u32[]{:S(2)}, u32[]{:S(2)}) collective-permute-start(f32[200,256]{1,0:T(8,128)S(1)} %collective-permute-done.8.rest_1_), channel_id=1, source_target_pairs={{0,1},{1,0},{2,3},{3,2},{4,5},{5,4},{6,7},{7,6},{8,9},{9,8},{10,11... | collective-permute-start | bytes 614408 | tf_op jit(solution)/shard_map/ppermute | solution.py:65
  46.7 1.5 %collective-permute-start.12 = (f32[200,256]{1,0:T(8,128)S(1)}, f32[200,256]{1,0:T(8,128)S(1)}, u32[]{:S(2)}, u32[]{:S(2)}) collective-permute-start(f32[200,256]{1,0:T(8,128)S(1)} %collective-permute-done.9.rest_2_), channel_id=1, source_target_pairs={{0,1},{1,0},{2,3},{3,2},{4,5},{5,4},{6,7},{7,6},{8,9},{9,8},{10,11... | collective-permute-start | bytes 614408 | tf_op jit(solution)/shard_map/ppermute | solution.py:65
  54.7 1.5 %collective-permute-start.14 = (f32[1,1,192,256]{3,2,1,0:T(8,128)S(1)}, f32[1,1,192,256]{3,2,1,0:T(8,128)S(1)}, u32[]{:S(2)}, u32[]{:S(2)}) collective-permute-start(f32[1,1,192,256]{3,2,1,0:T(8,128)S(1)} %get-tuple-element.86), channel_id=1, source_target_pairs={{0,1},{1,0},{2,3},{3,2},{4,5},{5,4},{6,7},{7,6},{8,9},{9,8},{10,11... | collective-permute-start | bytes 589832 | tf_op jit(solution)/shard_map/ppermute | solution.py:65
  56.2 8.2 %collective-permute-start.15 = (f32[1,192,256]{2,1,0:T(8,128)S(1)}, f32[1,192,256]{2,1,0:T(8,128)S(1)}, u32[]{:S(2)}, u32[]{:S(2)}) collective-permute-start(f32[1,192,256]{2,1,0:T(8,128)S(1)} %bitcast.71), channel_id=1, source_target_pairs={{0,4},{1,5},{2,6},{3,7},{4,0},{5,1},{6,2},{7,3},{8,12},{9,13},{10,... | collective-permute-start | bytes 589832 | tf_op jit(solution)/shard_map/ppermute | solution.py:75
  64.4 1.5 %collective-permute-start.19 = (f32[1,1,192,256]{3,2,1,0:T(8,128)S(1)}, f32[1,1,192,256]{3,2,1,0:T(8,128)S(1)}, u32[]{:S(2)}, u32[]{:S(2)}) collective-permute-start(f32[1,1,192,256]{3,2,1,0:T(8,128)S(1)} %get-tuple-element.99), channel_id=1, source_target_pairs={{0,1},{1,0},{2,3},{3,2},{4,5},{5,4},{6,7},{7,6},{8,9},{9,8},{10,11... | collective-permute-start | bytes 589832 | tf_op jit(solution)/shard_map/ppermute | solution.py:65
  64.5 2.1 %collective-permute-start.17 = (f32[1,192,256]{2,1,0:T(8,128)S(1)}, f32[1,192,256]{2,1,0:T(8,128)S(1)}, u32[]{:S(2)}, u32[]{:S(2)}) collective-permute-start(f32[1,192,256]{2,1,0:T(8,128)S(1)} %get-tuple-element.96), channel_id=1, source_target_pairs={{0,1},{1,0},{2,3},{3,2},{4,5},{5,4},{6,7},{7,6},{8,9},{9,8},{10,11... | collective-permute-start | bytes 589832 | tf_op jit(solution)/shard_map/ppermute | solution.py:65
  66.0 7.2 %collective-permute-start.20 = (f32[200,256]{1,0:T(8,128)S(1)}, f32[200,256]{1,0:T(8,128)S(1)}, u32[]{:S(2)}, u32[]{:S(2)}) collective-permute-start(f32[200,256]{1,0:T(8,128)S(1)} %pad_maximum_fusion), channel_id=1, source_target_pairs={{0,2},{1,3},{2,0},{3,1},{4,6},{5,7},{6,4},{7,5},{8,10},{9,11},{10,... | collective-permute-start | bytes 614408 | tf_op jit(solution)/shard_map/ppermute | solution.py:68
  66.7 6.7 %collective-permute-start.18 = (f32[192,256]{1,0:T(8,128)S(1)}, f32[192,256]{1,0:T(8,128)S(1)}, u32[]{:S(2)}, u32[]{:S(2)}) collective-permute-start(f32[192,256]{1,0:T(8,128)S(1)} %bitcast.70), channel_id=1, source_target_pairs={{0,4},{1,5},{2,6},{3,7},{4,0},{5,1},{6,2},{7,3},{8,12},{9,13},{10,... | collective-permute-start | bytes 589832 | tf_op jit(solution)/shard_map/ppermute | solution.py:75
  67.6 5.8 %collective-permute-start.16 = (f32[1,192,256]{2,1,0:T(8,128)S(1)}, f32[1,192,256]{2,1,0:T(8,128)S(1)}, u32[]{:S(2)}, u32[]{:S(2)}) collective-permute-start(f32[1,192,256]{2,1,0:T(8,128)S(1)} %get-tuple-element.95), channel_id=1, source_target_pairs={{0,1},{1,0},{2,3},{3,2},{4,5},{5,4},{6,7},{7,6},{8,9},{9,8},{10,11... | collective-permute-start | bytes 589832 | tf_op jit(solution)/shard_map/ppermute | solution.py:65

commit v6 on v5

--- a/solution.py
+++ b/solution.py
@@ -79,10 +79,6 @@
 
     def flip_sec(self, x, bits):
         return lax.ppermute(x, EVERYONE, self.perm(lambda o, s, r: (o, s ^ bits, r)))
-
-    def onward(self, x):
-        to = {0: 2, 2: 3, 3: 1, 1: 0}
-        return lax.ppermute(x, EVERYONE, self.perm(lambda o, s, r: (to[o], s, r)))
 
 
 def places(plan):
@@ -340,10 +336,8 @@
     if plan.op == 4:
         far = plan.flip_op(piece, 3)
         near = plan.flip_op(piece, 1)
-        op = lax.axis_index("op")
         far, beside = lax.optimization_barrier((far, beside))
-        carried = jnp.where((op == 1) | (op == 2), far, piece)
-        return [piece, near, plan.onward(carried), far], beside
+        return [piece, near, plan.flip_op(far, 1), far], beside
     got = piece[None]
     for bits in powers(plan.op):
         got = jnp.concatenate([got, plan.flip_op(got, bits)])

time: 74.3 us -> 73.4 us (0.988)
  waiting for transfers between devices: 20.6 us -> 23.2 us
  starting transfers between devices: 18.1 us -> 16 us
  local copies, waits for them, and re-layouts: 3.06 us -> 1.65 us
    ppermute x2 -> x3, waiting for transfers between devices: 1.38 us -> 7.13 us  [flip_op(): lax.ppermute(x, EVERYONE, self.perm(lambda o, s, r: (o ^ bits, s, r)))]
    ppermute x1 -> x0, starting transfers between devices: 3.31 us -> none  [onward(): return lax.ppermute(x, EVERYONE, self.perm(lambda o, s, r: (to[o], s, r)))]
    ppermute x1 -> x0, waiting for transfers between devices: 3.08 us -> none  [onward(): return lax.ppermute(x, EVERYONE, self.perm(lambda o, s, r: (to[o], s, r)))]
    ppermute x2 -> x3, starting transfers between devices: 3.24 us -> 5.32 us  [flip_op(): lax.ppermute(x, EVERYONE, self.perm(lambda o, s, r: (o ^ bits, s, r)))]
    unnamed x12, local copies, waits for them, and re-layouts: 3.01 us -> 1.61 us
    ppermute x4, starting transfers between devices: 6.97 us -> 6.02 us  [next_in_half(): return lax.ppermute(x, EVERYONE, self.perm(move))]
  transfers between devices with their start and end apart: 21 -> 21, of which waited for: 10 -> 11; matrix products, arithmetic and copies ran while one was open for 1% -> 1% of each run, Pallas kernels for 21% -> 21%
where the time goes in v6:
time: 73.4 us; the launch traced here: 73.2 us
  Pallas kernels  29.7 us (40%)
  waiting for transfers between devices  23.2 us (32%)
  starting transfers between devices  16 us (22%)
  other arithmetic  1.82 us (2%)
  local copies, waits for them, and re-layouts  1.65 us (2%)
  between operations  0.84 us (1%)
    pallas_call x2, Pallas kernels, along_half(): call(functools.partial(home_kernel, rows_are, names), plan.block, spread(...  12 us
    pallas_call x1, Pallas kernels, on_device(): call(first_kernel, plan.away, spread(plan.half - 1) + (chunks, packed('ho...  7.93 us
    ppermute x3, waiting for transfers between devices, flip_op(): lax.ppermute(x, EVERYONE, self.perm(lambda o, s, r: (o ^ bits, s, r)))  7.13 us
    pallas_call x1, Pallas kernels, on_device(): call(second_kernel, plan.away, spread(plan.half - 1) + (packed('source'),...  6.54 us
    ppermute x4, waiting for transfers between devices, next_in_half(): return lax.ppermute(x, EVERYONE, self.perm(move))  6.31 us
    ppermute x4, starting transfers between devices, next_in_half(): return lax.ppermute(x, EVERYONE, self.perm(move))  6.02 us
    ppermute x2, waiting for transfers between devices, next_sec(): lax.ppermute(x, EVERYONE, self.perm(lambda o, s, r: (o, (s + 1) % self.se...  5.55 us
    ppermute x3, starting transfers between devices, flip_op(): lax.ppermute(x, EVERYONE, self.perm(lambda o, s, r: (o ^ bits, s, r)))  5.32 us
  transfers between devices with their start and end apart: 21, of which 11 were waited for; matrix products, arithmetic and copies ran while one was open for 1% of the time, Pallas kernels for 21%

profile of v6, /device:TPU:0, one launch (start us, length us, event | category | flops | bytes accessed | tf_op | source)
XLA Modules:
  0.0 73.2 jit_solution(2963448405865170323)
XLA Ops:
  0.7 7.9 %shard_map.77 = (f32[2,1,192,256]{3,2,1,0:T(8,128)S(1)}, f32[1,1,192,256]{3,2,1,0:T(8,128)S(1)}, f32[1,192,256]{2,1,0:T(8,128)S(1)}, f32[2,192,256]{2,1,0:T(8,128)S(1)}, bf16[4608,512]{1,0:T(8,128)(2,1)S(1)}) custom-call(s32[8,12]{1,0:T(8,128)} %coupling_at.1, s32[12]{0:T(128)} %left_sizes_at.1, s32[12]{0:T(128)} %right_sizes_at.1, f32[6,256,256]{2,1,0:T(8,128)} %wave.2, ...), custom_call_target="tpu_custom_call" | custom-call | flops 4831838208 | bytes 4194304 | tf_op jit(solution)/shard_map/pallas_call | solution.py:420
  8.6 0.5 collective-permute-start
  9.2 1.0 %collective-permute-done = f32[1,1,192,256]{3,2,1,0:T(8,128)S(1)} collective-permute-done((f32[1,1,192,256]{3,2,1,0:T(8,128)S(1)}, f32[1,1,192,256]{3,2,1,0:T(8,128)S(1)}, u32[]{:S(2)}, u32[]{:S(2)}) %collective-permute-start) | collective-permute-done | bytes 196640 | tf_op jit(solution)/shard_map/ppermute | solution.py:65
  10.2 3.0 %collective-permute-start.1 = (f32[1,192,256]{2,1,0:T(8,128)S(1)}, f32[1,192,256]{2,1,0:T(8,128)S(1)}, u32[]{:S(2)}, u32[]{:S(2)}) collective-permute-start(f32[1,192,256]{2,1,0:T(8,128)S(1)} %bitcast.72), channel_id=1, source_target_pairs={{0,4},{1,5},{2,6},{3,7},{4,0},{5,1},{6,2},{7,3},{8,12},{9,13},{10,... | collective-permute-start | bytes 589832 | tf_op jit(solution)/shard_map/ppermute | solution.py:75
  13.2 6.0 %shard_map.78 = (f32[2,1,192,256]{3,2,1,0:T(8,128)S(1)}, f32[1,1,192,256]{3,2,1,0:T(8,128)S(1)}, f32[1,192,256]{2,1,0:T(8,128)S(1)}) custom-call(s32[10,12]{1,0:T(8,128)S(1)} %pad_add_fusion.tables, bf16[4608,512]{1,0:T(8,128)(2,1)S(1)} %get-tuple-element.63.refs_0_), custom_call_target="tpu_custom_call" | custom-call | flops 4831838208 | bytes 4194304 | tf_op jit(solution)/shard_map/pallas_call | solution.py:397
  19.3 0.5 collective-permute-start.5
  19.8 0.7 multiply_reduce_fusion.1
  20.6 0.2 collective-permute-done.2
  20.8 0.3 collective-permute-done.5
  21.2 1.6 %collective-permute-start.6 = (f32[200,256]{1,0:T(8,128)S(1)}, f32[200,256]{1,0:T(8,128)S(1)}, u32[]{:S(2)}, u32[]{:S(2)}) collective-permute-start(f32[200,256]{1,0:T(8,128)S(1)} %concatenate.14), channel_id=1, source_target_pairs={{0,2},{1,3},{2,0},{3,1},{4,6},{5,7},{6,4},{7,5},{8,10},{9,11},{10,... | collective-permute-start | bytes 614408 | tf_op jit(solution)/shard_map/ppermute | solution.py:68
  22.8 0.9 %collective-permute-start.4 = (f32[192,256]{1,0:T(8,128)}, f32[192,256]{1,0:T(8,128)S(1)}, u32[]{:S(2)}, u32[]{:S(2)}) collective-permute-start(f32[192,256]{1,0:T(8,128)} %bitcast.69), channel_id=1, source_target_pairs={{0,4},{1,5},{2,6},{3,7},{4,0},{5,1},{6,2},{7,3},{8,12},{9,13},{10,... | collective-permute-start | bytes 589832 | tf_op jit(solution)/shard_map/ppermute | solution.py:75
  23.6 6.1 %collective-permute-done.4 = f32[192,256]{1,0:T(8,128)S(1)} collective-permute-done((f32[192,256]{1,0:T(8,128)}, f32[192,256]{1,0:T(8,128)S(1)}, u32[]{:S(2)}, u32[]{:S(2)}) %collective-permute-start.4) | collective-permute-done | bytes 196640 | tf_op jit(solution)/shard_map/ppermute | solution.py:75
  29.9 3.0 %collective-permute-start.7 = (f32[200,256]{1,0:T(8,128)S(1)}, f32[200,256]{1,0:T(8,128)S(1)}, u32[]{:S(2)}, u32[]{:S(2)}) collective-permute-start(f32[200,256]{1,0:T(8,128)S(1)} %shard_map.79.rest_0_), channel_id=1, source_target_pairs={{0,12},{1,13},{2,14},{3,15},{4,8},{5,9},{6,10},{7,11},{8,4},{9,5},... | collective-permute-start | bytes 614408 | tf_op jit(solution)/shard_map/ppermute | solution.py:78
  32.8 0.3 collective-permute-start.8
  33.1 1.6 %copy-done.1 = f32[8,256,256]{2,1,0:T(8,128)S(1)} copy-done((f32[8,256,256]{2,1,0:T(8,128)S(1)}, f32[8,256,256]{2,1,0:T(8,128)}, u32[]{:S(2)}) %copy-start.1) | copy-done | bytes 2097176
  34.7 2.3 %shard_map.80 = (bf16[1024,512]{1,0:T(8,128)(2,1)S(1)}, bf16[3072,512]{1,0:T(8,128)(2,1)S(1)}, f32[6,256,256]{2,1,0:T(8,128)S(1)}) custom-call(s32[10,12]{1,0:T(8,128)S(1)} %pad_add_fusion.tables, f32[6,256,256]{2,1,0:T(8,128)S(1)} %copy-done.2, f32[8,256,256]{2,1,0:T(8,128)S(1)} %copy-done, f32[8,256,256]{2,1,0:T(8,128)S(1)} %copy-done.1), custom_call_target="tpu_custom_call" | custom-call | flops 75497472 | bytes 4194304 | tf_op jit(solution)/shard_map/pallas_call | solution.py:448
  37.0 2.8 %collective-permute-done.7.rest_3_ = f32[200,256]{1,0:T(8,128)S(1)} collective-permute-done((f32[200,256]{1,0:T(8,128)S(1)}, f32[200,256]{1,0:T(8,128)S(1)}, u32[]{:S(2)}, u32[]{:S(2)}) %collective-permute-start.7) | collective-permute-done | bytes 204832 | tf_op jit(solution)/shard_map/ppermute | solution.py:78
  39.8 2.1 %collective-permute-start.9 = (f32[200,256]{1,0:T(8,128)S(1)}, f32[200,256]{1,0:T(8,128)S(1)}, u32[]{:S(2)}, u32[]{:S(2)}) collective-permute-start(f32[200,256]{1,0:T(8,128)S(1)} %collective-permute-done.7.rest_3_), channel_id=1, source_target_pairs={{0,4},{1,5},{2,6},{3,7},{4,0},{5,1},{6,2},{7,3},{8,12},{9,13},{10,... | collective-permute-start | bytes 614408 | tf_op jit(solution)/shard_map/ppermute | solution.py:78
  41.8 0.5 collective-permute-start.13
  42.5 4.2 %collective-permute-done.9.rest_2_ = f32[200,256]{1,0:T(8,128)S(1)} collective-permute-done((f32[200,256]{1,0:T(8,128)S(1)}, f32[200,256]{1,0:T(8,128)S(1)}, u32[]{:S(2)}, u32[]{:S(2)}) %collective-permute-start.9) | collective-permute-done | bytes 204832 | tf_op jit(solution)/shard_map/ppermute | solution.py:78
  46.7 1.4 %collective-permute-done.12.rest_6_ = f32[200,256]{1,0:T(8,128)S(1)} collective-permute-done((f32[200,256]{1,0:T(8,128)S(1)}, f32[200,256]{1,0:T(8,128)S(1)}, u32[]{:S(2)}, u32[]{:S(2)}) %collective-permute-start.12) | collective-permute-done | bytes 204832 | tf_op jit(solution)/shard_map/ppermute | solution.py:65
  48.1 6.5 %shard_map.81 = (f32[2,1,192,256]{3,2,1,0:T(8,128)S(1)}, f32[1,1,192,256]{3,2,1,0:T(8,128)S(1)}, f32[1,192,256]{2,1,0:T(8,128)S(1)}, bf16[1536,512]{1,0:T(8,128)...) custom-call(s32[10,12]{1,0:T(8,128)S(1)} %pad_add_fusion.tables, ...), custom_call_target="tpu_custom_call" | custom-call | flops 4831838208 | bytes 4194304 | tf_op jit(solution)/shard_map/pallas_call | solution.py:454
  54.7 0.2 collective-permute-start.14
  54.9 1.3 %collective-permute-done.14 = f32[1,1,192,256]{3,2,1,0:T(8,128)S(1)} collective-permute-done((f32[1,1,192,256]{3,2,1,0:T(8,128)S(1)}, f32[1,1,192,256]{3,2,1,0:T(8,128)S(1)}, u32[]{:S(2)}, u32[]{:S(2)}) %collective-permute-start.14) | collective-permute-done | bytes 196640 | tf_op jit(solution)/shard_map/ppermute | solution.py:65
  56.2 1.2 %collective-permute-start.15 = (f32[1,192,256]{2,1,0:T(8,128)S(1)}, f32[1,192,256]{2,1,0:T(8,128)S(1)}, u32[]{:S(2)}, u32[]{:S(2)}) collective-permute-start(f32[1,192,256]{2,1,0:T(8,128)S(1)} %bitcast.71), channel_id=1, source_target_pairs={{0,4},{1,5},{2,6},{3,7},{4,0},{5,1},{6,2},{7,3},{8,12},{9,13},{10,... | collective-permute-start | bytes 589832 | tf_op jit(solution)/shard_map/ppermute | solution.py:75
  57.4 6.0 %shard_map.82 = (f32[2,1,192,256]{3,2,1,0:T(8,128)S(1)}, f32[1,1,192,256]{3,2,1,0:T(8,128)S(1)}, f32[1,192,256]{2,1,0:T(8,128)S(1)}) custom-call(s32[10,12]{1,0:T(8,128)S(1)} %pad_add_fusion.tables, bf16[3072,512]{1,0:T(8,128)(2,1)S(1)} %get-tuple-element.89.packed.refs_0_, bf16[1536,512]{1,0:T(8,128)(2,1)S(1)} %get-tuple-element.90.refs_1_), custom_call_target="tpu_custom_call" | custom-call | flops 4831838208 | bytes 4194304 | tf_op jit(solution)/shard_map/pallas_call | solution.py:397
  63.5 0.5 collective-permute-start.17
  64.0 0.9 %shard_map.83 = f32[6,32,256]{2,1,0:T(8,128)} custom-call(f32[6,256,256]{2,1,0:T(8,128)S(1)} %get-tuple-element.101.full), custom_call_target="tpu_custom_call" | custom-call | flops 75497472 | bytes 4194304 | tf_op jit(solution)/shard_map/pallas_call | solution.py:462
  65.1 0.6 collective-permute-start.20
  65.7 1.0 %collective-permute-start.18 = (f32[192,256]{1,0:T(8,128)S(1)}, f32[192,256]{1,0:T(8,128)S(1)}, u32[]{:S(2)}, u32[]{:S(2)}) collective-permute-start(f32[192,256]{1,0:T(8,128)S(1)} %bitcast.70), channel_id=1, source_target_pairs={{0,4},{1,5},{2,6},{3,7},{4,0},{5,1},{6,2},{7,3},{8,12},{9,13},{10,... | collective-permute-start | bytes 589832 | tf_op jit(solution)/shard_map/ppermute | solution.py:75
  66.7 5.5 %collective-permute-done.20 = f32[200,256]{1,0:T(8,128)S(1)} collective-permute-done((f32[200,256]{1,0:T(8,128)S(1)}, f32[200,256]{1,0:T(8,128)S(1)}, u32[]{:S(2)}, u32[]{:S(2)}) %collective-permute-start.20) | collective-permute-done | bytes 204832 | tf_op jit(solution)/shard_map/ppermute | solution.py:68
  72.5 0.7 broadcast_multiply_fusion
  (48 shorter events, 1.1 us)
Async XLA Ops:
  0.6 8.6 %copy-start.4 = (s32[12]{0:T(128)S(1)}, s32[12]{0:T(128)}, u32[]{:S(2)}) copy-start(s32[12]{0:T(128)} %right_sizes_at.1) | copy-start | bytes 148
  0.6 8.6 %copy-start.5 = (s32[12]{0:T(128)S(1)}, s32[12]{0:T(128)}, u32[]{:S(2)}) copy-start(s32[12]{0:T(128)} %left_sizes_at.1) | copy-start | bytes 148
  0.7 8.6 %copy-start.3 = (s32[8,12]{1,0:T(8,128)S(1)}, s32[8,12]{1,0:T(8,128)}, u32[]{:S(2)}) copy-start(s32[8,12]{1,0:T(8,128)} %coupling_at.1) | copy-start | bytes 1156
  8.6 1.6 %collective-permute-start = (f32[1,1,192,256]{3,2,1,0:T(8,128)S(1)}, f32[1,1,192,256]{3,2,1,0:T(8,128)S(1)}, u32[]{:S(2)}, u32[]{:S(2)}) collective-permute-start(f32[1,1,192,256]{3,2,1,0:T(8,128)S(1)} %get-tuple-element.60), channel_id=1, source_target_pairs={{0,1},{1,0},{2,3},{3,2},{4,5},{5,4},{6,7},{7,6},{8,9},{9,8},{10,11... | collective-permute-start | bytes 589832 | tf_op jit(solution)/shard_map/ppermute | solution.py:65
  9.1 10.7 %collective-permute-start.3 = (f32[1,192,256]{2,1,0:T(8,128)S(1)}, f32[1,192,256]{2,1,0:T(8,128)S(1)}, u32[]{:S(2)}, u32[]{:S(2)}) collective-permute-start(f32[1,192,256]{2,1,0:T(8,128)S(1)} %get-tuple-element.69), channel_id=1, source_target_pairs={{0,1},{1,0},{2,3},{3,2},{4,5},{5,4},{6,7},{7,6},{8,9},{9,8},{10,11... | collective-permute-start | bytes 589832 | tf_op jit(solution)/shard_map/ppermute | solution.py:65
  10.2 9.0 %collective-permute-start.1 = (f32[1,192,256]{2,1,0:T(8,128)S(1)}, f32[1,192,256]{2,1,0:T(8,128)S(1)}, u32[]{:S(2)}, u32[]{:S(2)}) collective-permute-start(f32[1,192,256]{2,1,0:T(8,128)S(1)} %bitcast.72), channel_id=1, source_target_pairs={{0,4},{1,5},{2,6},{3,7},{4,0},{5,1},{6,2},{7,3},{8,12},{9,13},{10,... | collective-permute-start | bytes 589832 | tf_op jit(solution)/shard_map/ppermute | solution.py:75
  19.3 1.5 %collective-permute-start.2 = (f32[1,192,256]{2,1,0:T(8,128)S(1)}, f32[1,192,256]{2,1,0:T(8,128)S(1)}, u32[]{:S(2)}, u32[]{:S(2)}) collective-permute-start(f32[1,192,256]{2,1,0:T(8,128)S(1)} %get-tuple-element.68), channel_id=1, source_target_pairs={{0,1},{1,0},{2,3},{3,2},{4,5},{5,4},{6,7},{7,6},{8,9},{9,8},{10,11... | collective-permute-start | bytes 589832 | tf_op jit(solution)/shard_map/ppermute | solution.py:65
  19.3 1.7 %collective-permute-start.5 = (f32[1,1,192,256]{3,2,1,0:T(8,128)S(1)}, f32[1,1,192,256]{3,2,1,0:T(8,128)S(1)}, u32[]{:S(2)}, u32[]{:S(2)}) collective-permute-start(f32[1,1,192,256]{3,2,1,0:T(8,128)S(1)} %get-tuple-element.72), channel_id=1, source_target_pairs={{0,1},{1,0},{2,3},{3,2},{4,5},{5,4},{6,7},{7,6},{8,9},{9,8},{10,11... | collective-permute-start | bytes 589832 | tf_op jit(solution)/shard_map/ppermute | solution.py:65
  19.8 13.3 %copy-start = (f32[8,256,256]{2,1,0:T(8,128)S(1)}, f32[8,256,256]{2,1,0:T(8,128)}, u32[]{:S(2)}) copy-start(f32[8,256,256]{2,1,0:T(8,128)} %left_ops.2) | copy-start | bytes 6291460
  21.2 11.9 %copy-start.2 = (f32[6,256,256]{2,1,0:T(8,128)S(1)}, f32[6,256,256]{2,1,0:T(8,128)}, u32[]{:S(2)}) copy-start(f32[6,256,256]{2,1,0:T(8,128)} %wave.2) | copy-start | bytes 4718596
  21.2 8.5 %collective-permute-start.6 = (f32[200,256]{1,0:T(8,128)S(1)}, f32[200,256]{1,0:T(8,128)S(1)}, u32[]{:S(2)}, u32[]{:S(2)}) collective-permute-start(f32[200,256]{1,0:T(8,128)S(1)} %concatenate.14), channel_id=1, source_target_pairs={{0,2},{1,3},{2,0},{3,1},{4,6},{5,7},{6,4},{7,5},{8,10},{9,11},{10,... | collective-permute-start | bytes 614408 | tf_op jit(solution)/shard_map/ppermute | solution.py:68
  22.8 7.0 %collective-permute-start.4 = (f32[192,256]{1,0:T(8,128)}, f32[192,256]{1,0:T(8,128)S(1)}, u32[]{:S(2)}, u32[]{:S(2)}) collective-permute-start(f32[192,256]{1,0:T(8,128)} %bitcast.69), channel_id=1, source_target_pairs={{0,4},{1,5},{2,6},{3,7},{4,0},{5,1},{6,2},{7,3},{8,12},{9,13},{10,... | collective-permute-start | bytes 589832 | tf_op jit(solution)/shard_map/ppermute | solution.py:75
  29.9 9.9 %collective-permute-start.7 = (f32[200,256]{1,0:T(8,128)S(1)}, f32[200,256]{1,0:T(8,128)S(1)}, u32[]{:S(2)}, u32[]{:S(2)}) collective-permute-start(f32[200,256]{1,0:T(8,128)S(1)} %shard_map.79.rest_0_), channel_id=1, source_target_pairs={{0,12},{1,13},{2,14},{3,15},{4,8},{5,9},{6,10},{7,11},{8,4},{9,5},... | collective-permute-start | bytes 614408 | tf_op jit(solution)/shard_map/ppermute | solution.py:78
  32.8 9.6 %collective-permute-start.8 = (f32[200,256]{1,0:T(8,128)S(1)}, f32[200,256]{1,0:T(8,128)S(1)}, u32[]{:S(2)}, u32[]{:S(2)}) collective-permute-start(f32[200,256]{1,0:T(8,128)S(1)} %shard_map.79.rest_0_), channel_id=1, source_target_pairs={{0,4},{1,5},{2,6},{3,7},{4,0},{5,1},{6,2},{7,3},{8,12},{9,13},{10,... | collective-permute-start | bytes 614408 | tf_op jit(solution)/shard_map/ppermute | solution.py:78
  33.1 1.6 %copy-start.1 = (f32[8,256,256]{2,1,0:T(8,128)S(1)}, f32[8,256,256]{2,1,0:T(8,128)}, u32[]{:S(2)}) copy-start(f32[8,256,256]{2,1,0:T(8,128)} %right_ops.2) | copy-start | bytes 6291460
  39.8 6.9 %collective-permute-start.9 = (f32[200,256]{1,0:T(8,128)S(1)}, f32[200,256]{1,0:T(8,128)S(1)}, u32[]{:S(2)}, u32[]{:S(2)}) collective-permute-start(f32[200,256]{1,0:T(8,128)S(1)} %collective-permute-done.7.rest_3_), channel_id=1, source_target_pairs={{0,4},{1,5},{2,6},{3,7},{4,0},{5,1},{6,2},{7,3},{8,12},{9,13},{10,... | collective-permute-start | bytes 614408 | tf_op jit(solution)/shard_map/ppermute | solution.py:78
  41.8 4.9 %collective-permute-start.10 = (f32[200,256]{1,0:T(8,128)S(1)}, f32[200,256]{1,0:T(8,128)S(1)}, u32[]{:S(2)}, u32[]{:S(2)}) collective-permute-start(f32[200,256]{1,0:T(8,128)S(1)} %shard_map.79.rest_0_), channel_id=1, source_target_pairs={{0,1},{1,0},{2,3},{3,2},{4,5},{5,4},{6,7},{7,6},{8,9},{9,8},{10,11... | collective-permute-start | bytes 614408 | tf_op jit(solution)/shard_map/ppermute | solution.py:65
  41.8 4.9 %collective-permute-start.13 = (f32[200,256]{1,0:T(8,128)S(1)}, f32[200,256]{1,0:T(8,128)S(1)}, u32[]{:S(2)}, u32[]{:S(2)}) collective-permute-start(f32[200,256]{1,0:T(8,128)S(1)} %collective-permute-done.7.rest_3_), channel_id=1, source_target_pairs={{0,1},{1,0},{2,3},{3,2},{4,5},{5,4},{6,7},{7,6},{8,9},{9,8},{10,11... | collective-permute-start | bytes 614408 | tf_op jit(solution)/shard_map/ppermute | solution.py:65
  42.5 4.2 %collective-permute-start.11 = (f32[200,256]{1,0:T(8,128)S(1)}, f32[200,256]{1,0:T(8,128)S(1)}, u32[]{:S(2)}, u32[]{:S(2)}) collective-permute-start(f32[200,256]{1,0:T(8,128)S(1)} %collective-permute-done.8.rest_1_), channel_id=1, source_target_pairs={{0,1},{1,0},{2,3},{3,2},{4,5},{5,4},{6,7},{7,6},{8,9},{9,8},{10,11... | collective-permute-start | bytes 614408 | tf_op jit(solution)/shard_map/ppermute | solution.py:65
  46.7 1.5 %collective-permute-start.12 = (f32[200,256]{1,0:T(8,128)S(1)}, f32[200,256]{1,0:T(8,128)S(1)}, u32[]{:S(2)}, u32[]{:S(2)}) collective-permute-start(f32[200,256]{1,0:T(8,128)S(1)} %collective-permute-done.9.rest_2_), channel_id=1, source_target_pairs={{0,1},{1,0},{2,3},{3,2},{4,5},{5,4},{6,7},{7,6},{8,9},{9,8},{10,11... | collective-permute-start | bytes 614408 | tf_op jit(solution)/shard_map/ppermute | solution.py:65
  54.7 1.5 %collective-permute-start.14 = (f32[1,1,192,256]{3,2,1,0:T(8,128)S(1)}, f32[1,1,192,256]{3,2,1,0:T(8,128)S(1)}, u32[]{:S(2)}, u32[]{:S(2)}) collective-permute-start(f32[1,1,192,256]{3,2,1,0:T(8,128)S(1)} %get-tuple-element.86), channel_id=1, source_target_pairs={{0,1},{1,0},{2,3},{3,2},{4,5},{5,4},{6,7},{7,6},{8,9},{9,8},{10,11... | collective-permute-start | bytes 589832 | tf_op jit(solution)/shard_map/ppermute | solution.py:65
  56.2 7.2 %collective-permute-start.15 = (f32[1,192,256]{2,1,0:T(8,128)S(1)}, f32[1,192,256]{2,1,0:T(8,128)S(1)}, u32[]{:S(2)}, u32[]{:S(2)}) collective-permute-start(f32[1,192,256]{2,1,0:T(8,128)S(1)} %bitcast.71), channel_id=1, source_target_pairs={{0,4},{1,5},{2,6},{3,7},{4,0},{5,1},{6,2},{7,3},{8,12},{9,13},{10,... | collective-permute-start | bytes 589832 | tf_op jit(solution)/shard_map/ppermute | solution.py:75
  63.5 1.5 %collective-permute-start.19 = (f32[1,1,192,256]{3,2,1,0:T(8,128)S(1)}, f32[1,1,192,256]{3,2,1,0:T(8,128)S(1)}, u32[]{:S(2)}, u32[]{:S(2)}) collective-permute-start(f32[1,1,192,256]{3,2,1,0:T(8,128)S(1)} %get-tuple-element.99), channel_id=1, source_target_pairs={{0,1},{1,0},{2,3},{3,2},{4,5},{5,4},{6,7},{7,6},{8,9},{9,8},{10,11... | collective-permute-start | bytes 589832 | tf_op jit(solution)/shard_map/ppermute | solution.py:65
  63.5 2.1 %collective-permute-start.17 = (f32[1,192,256]{2,1,0:T(8,128)S(1)}, f32[1,192,256]{2,1,0:T(8,128)S(1)}, u32[]{:S(2)}, u32[]{:S(2)}) collective-permute-start(f32[1,192,256]{2,1,0:T(8,128)S(1)} %get-tuple-element.96), channel_id=1, source_target_pairs={{0,1},{1,0},{2,3},{3,2},{4,5},{5,4},{6,7},{7,6},{8,9},{9,8},{10,11... | collective-permute-start | bytes 589832 | tf_op jit(solution)/shard_map/ppermute | solution.py:65
  65.1 7.2 %collective-permute-start.20 = (f32[200,256]{1,0:T(8,128)S(1)}, f32[200,256]{1,0:T(8,128)S(1)}, u32[]{:S(2)}, u32[]{:S(2)}) collective-permute-start(f32[200,256]{1,0:T(8,128)S(1)} %pad_maximum_fusion), channel_id=1, source_target_pairs={{0,2},{1,3},{2,0},{3,1},{4,6},{5,7},{6,4},{7,5},{8,10},{9,11},{10,... | collective-permute-start | bytes 614408 | tf_op jit(solution)/shard_map/ppermute | solution.py:68
  65.7 6.7 %collective-permute-start.18 = (f32[192,256]{1,0:T(8,128)S(1)}, f32[192,256]{1,0:T(8,128)S(1)}, u32[]{:S(2)}, u32[]{:S(2)}) collective-permute-start(f32[192,256]{1,0:T(8,128)S(1)} %bitcast.70), channel_id=1, source_target_pairs={{0,4},{1,5},{2,6},{3,7},{4,0},{5,1},{6,2},{7,3},{8,12},{9,13},{10,... | collective-permute-start | bytes 589832 | tf_op jit(solution)/shard_map/ppermute | solution.py:75
  66.7 5.8 %collective-permute-start.16 = (f32[1,192,256]{2,1,0:T(8,128)S(1)}, f32[1,192,256]{2,1,0:T(8,128)S(1)}, u32[]{:S(2)}, u32[]{:S(2)}) collective-permute-start(f32[1,192,256]{2,1,0:T(8,128)S(1)} %get-tuple-element.95), channel_id=1, source_target_pairs={{0,1},{1,0},{2,3},{3,2},{4,5},{5,4},{6,7},{7,6},{8,9},{9,8},{10,11... | collective-permute-start | bytes 589832 | tf_op jit(solution)/shard_map/ppermute | solution.py:65

commit v7 on v6

--- a/solution.py
+++ b/solution.py
@@ -398,8 +398,8 @@
             functools.partial(home_kernel, rows_are, names), plan.block, spread(1),
             [smem] + [vmem] * len(names), work(plan.block),
         )(tables, *home_args)
-        others, kept = lax.optimization_barrier((others, kept))
         keep, send_others, send_ours = kept
+        others, send_ours = lax.optimization_barrier((others, send_ours))
         others = others + (keep[1:] + plan.across_cores(send_others))[:, 0]
         home = (keep[0] + plan.across_cores(send_ours))[0]
         going, _ = lax.optimization_barrier((sent, keep))

time: 73.4 us -> 73.2 us (level)
  transfers between devices with their start and end apart: 21 -> 21, of which waited for: 11 -> 10; matrix products, arithmetic and copies ran while one was open for 1% -> 1% of each run, Pallas kernels for 21% -> 21%
where the time goes in v7:
time: 73.2 us; the launch traced here: 73.1 us
  Pallas kernels  29.6 us (40%)
  waiting for transfers between devices  23.4 us (32%)
  starting transfers between devices  15.7 us (21%)
  other arithmetic  1.86 us (3%)
  local copies, waits for them, and re-layouts  1.65 us (2%)
  between operations  0.83 us (1%)
    pallas_call x2, Pallas kernels, along_half(): call(functools.partial(home_kernel, rows_are, names), plan.block, spread(...  11.9 us
    pallas_call x1, Pallas kernels, on_device(): call(first_kernel, plan.away, spread(plan.half - 1) + (chunks, packed('ho...  7.91 us
    ppermute x3, waiting for transfers between devices, flip_op(): lax.ppermute(x, EVERYONE, self.perm(lambda o, s, r: (o ^ bits, s, r)))  7.13 us
    ppermute x4, waiting for transfers between devices, next_in_half(): return lax.ppermute(x, EVERYONE, self.perm(move))  6.54 us
    pallas_call x1, Pallas kernels, on_device(): call(second_kernel, plan.away, spread(plan.half - 1) + (packed('source'),...  6.51 us
    ppermute x4, starting transfers between devices, next_in_half(): return lax.ppermute(x, EVERYONE, self.perm(move))  5.78 us
    ppermute x2, waiting for transfers between devices, next_sec(): lax.ppermute(x, EVERYONE, self.perm(lambda o, s, r: (o, (s + 1) % self.se...  5.55 us
    ppermute x3, starting transfers between devices, flip_op(): lax.ppermute(x, EVERYONE, self.perm(lambda o, s, r: (o ^ bits, s, r)))  5.32 us
  transfers between devices with their start and end apart: 21, of which 10 were waited for; matrix products, arithmetic and copies ran while one was open for 1% of the time, Pallas kernels for 21%

profile of v7, /device:TPU:0, one launch (start us, length us, event | category | flops | bytes accessed | tf_op | source)
XLA Modules:
  0.0 73.1 jit_solution(8539474354383137920)
XLA Ops:
  0.7 7.9 %shard_map.77 = (f32[2,1,192,256]{3,2,1,0:T(8,128)S(1)}, f32[1,1,192,256]{3,2,1,0:T(8,128)S(1)}, f32[1,192,256]{2,1,0:T(8,128)S(1)}, f32[2,192,256]{2,1,0:T(8,128)S(1)}, bf16[4608,512]{1,0:T(8,128)(2,1)S(1)}) custom-call(s32[8,12]{1,0:T(8,128)} %coupling_at.1, s32[12]{0:T(128)} %left_sizes_at.1, s32[12]{0:T(128)} %right_sizes_at.1, f32[6,256,256]{2,1,0:T(8,128)} %wave.2, ...), custom_call_target="tpu_custom_call" | custom-call | flops 4831838208 | bytes 4194304 | tf_op jit(solution)/shard_map/pallas_call | solution.py:420
  8.6 0.5 collective-permute-start
  9.2 1.0 %collective-permute-done = f32[1,1,192,256]{3,2,1,0:T(8,128)S(1)} collective-permute-done((f32[1,1,192,256]{3,2,1,0:T(8,128)S(1)}, f32[1,1,192,256]{3,2,1,0:T(8,128)S(1)}, u32[]{:S(2)}, u32[]{:S(2)}) %collective-permute-start) | collective-permute-done | bytes 196640 | tf_op jit(solution)/shard_map/ppermute | solution.py:65
  10.2 3.0 %collective-permute-start.1 = (f32[1,192,256]{2,1,0:T(8,128)S(1)}, f32[1,192,256]{2,1,0:T(8,128)S(1)}, u32[]{:S(2)}, u32[]{:S(2)}) collective-permute-start(f32[1,192,256]{2,1,0:T(8,128)S(1)} %bitcast.72), channel_id=1, source_target_pairs={{0,4},{1,5},{2,6},{3,7},{4,0},{5,1},{6,2},{7,3},{8,12},{9,13},{10,... | collective-permute-start | bytes 589832 | tf_op jit(solution)/shard_map/ppermute | solution.py:75
  13.2 6.0 %shard_map.78 = (f32[2,1,192,256]{3,2,1,0:T(8,128)S(1)}, f32[1,1,192,256]{3,2,1,0:T(8,128)S(1)}, f32[1,192,256]{2,1,0:T(8,128)S(1)}) custom-call(s32[10,12]{1,0:T(8,128)S(1)} %pad_add_fusion.tables, bf16[4608,512]{1,0:T(8,128)(2,1)S(1)} %get-tuple-element.58.refs_0_), custom_call_target="tpu_custom_call" | custom-call | flops 4831838208 | bytes 4194304 | tf_op jit(solution)/shard_map/pallas_call | solution.py:397
  19.3 0.5 collective-permute-start.2
  19.8 0.7 multiply_reduce_fusion.1
  20.5 0.2 collective-permute-done.5
  20.7 0.3 collective-permute-done.2
  21.2 1.6 %collective-permute-start.6 = (f32[200,256]{1,0:T(8,128)S(1)}, f32[200,256]{1,0:T(8,128)S(1)}, u32[]{:S(2)}, u32[]{:S(2)}) collective-permute-start(f32[200,256]{1,0:T(8,128)S(1)} %concatenate.14), channel_id=1, source_target_pairs={{0,2},{1,3},{2,0},{3,1},{4,6},{5,7},{6,4},{7,5},{8,10},{9,11},{10,... | collective-permute-start | bytes 614408 | tf_op jit(solution)/shard_map/ppermute | solution.py:68
  22.7 0.6 collective-permute-start.4
  23.4 6.3 %collective-permute-done.4 = f32[192,256]{1,0:T(8,128)S(1)} collective-permute-done((f32[192,256]{1,0:T(8,128)}, f32[192,256]{1,0:T(8,128)S(1)}, u32[]{:S(2)}, u32[]{:S(2)}) %collective-permute-start.4) | collective-permute-done | bytes 196640 | tf_op jit(solution)/shard_map/ppermute | solution.py:75
  29.8 2.6 %collective-permute-start.7 = (f32[200,256]{1,0:T(8,128)S(1)}, f32[200,256]{1,0:T(8,128)S(1)}, u32[]{:S(2)}, u32[]{:S(2)}) collective-permute-start(f32[200,256]{1,0:T(8,128)S(1)} %shard_map.79.rest_0_), channel_id=1, source_target_pairs={{0,12},{1,13},{2,14},{3,15},{4,8},{5,9},{6,10},{7,11},{8,4},{9,5},... | collective-permute-start | bytes 614408 | tf_op jit(solution)/shard_map/ppermute | solution.py:78
  32.5 0.6 collective-permute-start.8
  33.1 1.6 %copy-done.1 = f32[8,256,256]{2,1,0:T(8,128)S(1)} copy-done((f32[8,256,256]{2,1,0:T(8,128)S(1)}, f32[8,256,256]{2,1,0:T(8,128)}, u32[]{:S(2)}) %copy-start.1) | copy-done | bytes 2097176
  34.7 2.2 %shard_map.80 = (bf16[1024,512]{1,0:T(8,128)(2,1)S(1)}, bf16[3072,512]{1,0:T(8,128)(2,1)S(1)}, f32[6,256,256]{2,1,0:T(8,128)S(1)}) custom-call(s32[10,12]{1,0:T(8,128)S(1)} %pad_add_fusion.tables, f32[6,256,256]{2,1,0:T(8,128)S(1)} %copy-done.2, f32[8,256,256]{2,1,0:T(8,128)S(1)} %copy-done, f32[8,256,256]{2,1,0:T(8,128)S(1)} %copy-done.1), custom_call_target="tpu_custom_call" | custom-call | flops 75497472 | bytes 4194304 | tf_op jit(solution)/shard_map/pallas_call | solution.py:448
  36.9 2.8 %collective-permute-done.7.rest_3_ = f32[200,256]{1,0:T(8,128)S(1)} collective-permute-done((f32[200,256]{1,0:T(8,128)S(1)}, f32[200,256]{1,0:T(8,128)S(1)}, u32[]{:S(2)}, u32[]{:S(2)}) %collective-permute-start.7) | collective-permute-done | bytes 204832 | tf_op jit(solution)/shard_map/ppermute | solution.py:78
  39.7 2.1 %collective-permute-start.9 = (f32[200,256]{1,0:T(8,128)S(1)}, f32[200,256]{1,0:T(8,128)S(1)}, u32[]{:S(2)}, u32[]{:S(2)}) collective-permute-start(f32[200,256]{1,0:T(8,128)S(1)} %collective-permute-done.7.rest_3_), channel_id=1, source_target_pairs={{0,4},{1,5},{2,6},{3,7},{4,0},{5,1},{6,2},{7,3},{8,12},{9,13},{10,... | collective-permute-start | bytes 614408 | tf_op jit(solution)/shard_map/ppermute | solution.py:78
  41.8 0.5 collective-permute-start.13
  42.4 4.3 %collective-permute-done.9.rest_2_ = f32[200,256]{1,0:T(8,128)S(1)} collective-permute-done((f32[200,256]{1,0:T(8,128)S(1)}, f32[200,256]{1,0:T(8,128)S(1)}, u32[]{:S(2)}, u32[]{:S(2)}) %collective-permute-start.9) | collective-permute-done | bytes 204832 | tf_op jit(solution)/shard_map/ppermute | solution.py:78
  46.7 1.4 %collective-permute-done.12.rest_6_ = f32[200,256]{1,0:T(8,128)S(1)} collective-permute-done((f32[200,256]{1,0:T(8,128)S(1)}, f32[200,256]{1,0:T(8,128)S(1)}, u32[]{:S(2)}, u32[]{:S(2)}) %collective-permute-start.12) | collective-permute-done | bytes 204832 | tf_op jit(solution)/shard_map/ppermute | solution.py:65
  48.1 6.5 %shard_map.81 = (f32[2,1,192,256]{3,2,1,0:T(8,128)S(1)}, f32[1,1,192,256]{3,2,1,0:T(8,128)S(1)}, f32[1,192,256]{2,1,0:T(8,128)S(1)}, bf16[1536,512]{1,0:T(8,128)...) custom-call(s32[10,12]{1,0:T(8,128)S(1)} %pad_add_fusion.tables, ...), custom_call_target="tpu_custom_call" | custom-call | flops 4831838208 | bytes 4194304 | tf_op jit(solution)/shard_map/pallas_call | solution.py:454
  54.6 0.2 collective-permute-start.14
  54.8 1.3 %collective-permute-done.14 = f32[1,1,192,256]{3,2,1,0:T(8,128)S(1)} collective-permute-done((f32[1,1,192,256]{3,2,1,0:T(8,128)S(1)}, f32[1,1,192,256]{3,2,1,0:T(8,128)S(1)}, u32[]{:S(2)}, u32[]{:S(2)}) %collective-permute-start.14) | collective-permute-done | bytes 196640 | tf_op jit(solution)/shard_map/ppermute | solution.py:65
  56.2 1.2 %collective-permute-start.15 = (f32[1,192,256]{2,1,0:T(8,128)S(1)}, f32[1,192,256]{2,1,0:T(8,128)S(1)}, u32[]{:S(2)}, u32[]{:S(2)}) collective-permute-start(f32[1,192,256]{2,1,0:T(8,128)S(1)} %bitcast.70), channel_id=1, source_target_pairs={{0,4},{1,5},{2,6},{3,7},{4,0},{5,1},{6,2},{7,3},{8,12},{9,13},{10,... | collective-permute-start | bytes 589832 | tf_op jit(solution)/shard_map/ppermute | solution.py:75
  57.4 6.0 %shard_map.82 = (f32[2,1,192,256]{3,2,1,0:T(8,128)S(1)}, f32[1,1,192,256]{3,2,1,0:T(8,128)S(1)}, f32[1,192,256]{2,1,0:T(8,128)S(1)}) custom-call(s32[10,12]{1,0:T(8,128)S(1)} %pad_add_fusion.tables, bf16[3072,512]{1,0:T(8,128)(2,1)S(1)} %get-tuple-element.82.packed.refs_0_, bf16[1536,512]{1,0:T(8,128)(2,1)S(1)} %get-tuple-element.83.refs_1_), custom_call_target="tpu_custom_call" | custom-call | flops 4831838208 | bytes 4194304 | tf_op jit(solution)/shard_map/pallas_call | solution.py:397
  63.4 0.5 collective-permute-start.17
  63.9 0.9 %shard_map.83 = f32[6,32,256]{2,1,0:T(8,128)} custom-call(f32[6,256,256]{2,1,0:T(8,128)S(1)} %get-tuple-element.93.full), custom_call_target="tpu_custom_call" | custom-call | flops 75497472 | bytes 4194304 | tf_op jit(solution)/shard_map/pallas_call | solution.py:462
  65.0 0.6 collective-permute-start.20
  65.6 0.9 %collective-permute-start.18 = (f32[192,256]{1,0:T(8,128)S(1)}, f32[192,256]{1,0:T(8,128)S(1)}, u32[]{:S(2)}, u32[]{:S(2)}) collective-permute-start(f32[192,256]{1,0:T(8,128)S(1)} %bitcast.71), channel_id=1, source_target_pairs={{0,4},{1,5},{2,6},{3,7},{4,0},{5,1},{6,2},{7,3},{8,12},{9,13},{10,... | collective-permute-start | bytes 589832 | tf_op jit(solution)/shard_map/ppermute | solution.py:75
  66.6 5.6 %collective-permute-done.20 = f32[200,256]{1,0:T(8,128)S(1)} collective-permute-done((f32[200,256]{1,0:T(8,128)S(1)}, f32[200,256]{1,0:T(8,128)S(1)}, u32[]{:S(2)}, u32[]{:S(2)}) %collective-permute-start.20) | collective-permute-done | bytes 204832 | tf_op jit(solution)/shard_map/ppermute | solution.py:68
  72.4 0.7 broadcast_multiply_fusion
  (48 shorter events, 1.0 us)
Async XLA Ops:
  0.6 8.5 %copy-start.4 = (s32[12]{0:T(128)S(1)}, s32[12]{0:T(128)}, u32[]{:S(2)}) copy-start(s32[12]{0:T(128)} %right_sizes_at.1) | copy-start | bytes 148
  0.6 8.5 %copy-start.5 = (s32[12]{0:T(128)S(1)}, s32[12]{0:T(128)}, u32[]{:S(2)}) copy-start(s32[12]{0:T(128)} %left_sizes_at.1) | copy-start | bytes 148
  0.7 8.5 %copy-start.3 = (s32[8,12]{1,0:T(8,128)S(1)}, s32[8,12]{1,0:T(8,128)}, u32[]{:S(2)}) copy-start(s32[8,12]{1,0:T(8,128)} %coupling_at.1) | copy-start | bytes 1156
  8.6 1.6 %collective-permute-start = (f32[1,1,192,256]{3,2,1,0:T(8,128)S(1)}, f32[1,1,192,256]{3,2,1,0:T(8,128)S(1)}, u32[]{:S(2)}, u32[]{:S(2)}) collective-permute-start(f32[1,1,192,256]{3,2,1,0:T(8,128)S(1)} %get-tuple-element.56), channel_id=1, source_target_pairs={{0,1},{1,0},{2,3},{3,2},{4,5},{5,4},{6,7},{7,6},{8,9},{9,8},{10,11... | collective-permute-start | bytes 589832 | tf_op jit(solution)/shard_map/ppermute | solution.py:65
  9.1 10.7 %collective-permute-start.3 = (f32[1,192,256]{2,1,0:T(8,128)S(1)}, f32[1,192,256]{2,1,0:T(8,128)S(1)}, u32[]{:S(2)}, u32[]{:S(2)}) collective-permute-start(f32[1,192,256]{2,1,0:T(8,128)S(1)} %get-tuple-element.63), channel_id=1, source_target_pairs={{0,1},{1,0},{2,3},{3,2},{4,5},{5,4},{6,7},{7,6},{8,9},{9,8},{10,11... | collective-permute-start | bytes 589832 | tf_op jit(solution)/shard_map/ppermute | solution.py:65
  10.2 9.1 %collective-permute-start.1 = (f32[1,192,256]{2,1,0:T(8,128)S(1)}, f32[1,192,256]{2,1,0:T(8,128)S(1)}, u32[]{:S(2)}, u32[]{:S(2)}) collective-permute-start(f32[1,192,256]{2,1,0:T(8,128)S(1)} %bitcast.72), channel_id=1, source_target_pairs={{0,4},{1,5},{2,6},{3,7},{4,0},{5,1},{6,2},{7,3},{8,12},{9,13},{10,... | collective-permute-start | bytes 589832 | tf_op jit(solution)/shard_map/ppermute | solution.py:75
  19.2 1.5 %collective-permute-start.5 = (f32[1,1,192,256]{3,2,1,0:T(8,128)S(1)}, f32[1,1,192,256]{3,2,1,0:T(8,128)S(1)}, u32[]{:S(2)}, u32[]{:S(2)}) collective-permute-start(f32[1,1,192,256]{3,2,1,0:T(8,128)S(1)} %get-tuple-element.66), channel_id=1, source_target_pairs={{0,1},{1,0},{2,3},{3,2},{4,5},{5,4},{6,7},{7,6},{8,9},{9,8},{10,11... | collective-permute-start | bytes 589832 | tf_op jit(solution)/shard_map/ppermute | solution.py:65
  19.3 1.7 %collective-permute-start.2 = (f32[1,192,256]{2,1,0:T(8,128)S(1)}, f32[1,192,256]{2,1,0:T(8,128)S(1)}, u32[]{:S(2)}, u32[]{:S(2)}) collective-permute-start(f32[1,192,256]{2,1,0:T(8,128)S(1)} %get-tuple-element.62), channel_id=1, source_target_pairs={{0,1},{1,0},{2,3},{3,2},{4,5},{5,4},{6,7},{7,6},{8,9},{9,8},{10,11... | collective-permute-start | bytes 589832 | tf_op jit(solution)/shard_map/ppermute | solution.py:65
  19.8 13.3 %copy-start = (f32[8,256,256]{2,1,0:T(8,128)S(1)}, f32[8,256,256]{2,1,0:T(8,128)}, u32[]{:S(2)}) copy-start(f32[8,256,256]{2,1,0:T(8,128)} %left_ops.2) | copy-start | bytes 6291460
  21.2 11.9 %copy-start.2 = (f32[6,256,256]{2,1,0:T(8,128)S(1)}, f32[6,256,256]{2,1,0:T(8,128)}, u32[]{:S(2)}) copy-start(f32[6,256,256]{2,1,0:T(8,128)} %wave.2) | copy-start | bytes 4718596
  21.2 8.5 %collective-permute-start.6 = (f32[200,256]{1,0:T(8,128)S(1)}, f32[200,256]{1,0:T(8,128)S(1)}, u32[]{:S(2)}, u32[]{:S(2)}) collective-permute-start(f32[200,256]{1,0:T(8,128)S(1)} %concatenate.14), channel_id=1, source_target_pairs={{0,2},{1,3},{2,0},{3,1},{4,6},{5,7},{6,4},{7,5},{8,10},{9,11},{10,... | collective-permute-start | bytes 614408 | tf_op jit(solution)/shard_map/ppermute | solution.py:68
  22.7 7.0 %collective-permute-start.4 = (f32[192,256]{1,0:T(8,128)}, f32[192,256]{1,0:T(8,128)S(1)}, u32[]{:S(2)}, u32[]{:S(2)}) collective-permute-start(f32[192,256]{1,0:T(8,128)} %bitcast.69), channel_id=1, source_target_pairs={{0,4},{1,5},{2,6},{3,7},{4,0},{5,1},{6,2},{7,3},{8,12},{9,13},{10,... | collective-permute-start | bytes 589832 | tf_op jit(solution)/shard_map/ppermute | solution.py:75
  29.8 9.9 %collective-permute-start.7 = (f32[200,256]{1,0:T(8,128)S(1)}, f32[200,256]{1,0:T(8,128)S(1)}, u32[]{:S(2)}, u32[]{:S(2)}) collective-permute-start(f32[200,256]{1,0:T(8,128)S(1)} %shard_map.79.rest_0_), channel_id=1, source_target_pairs={{0,12},{1,13},{2,14},{3,15},{4,8},{5,9},{6,10},{7,11},{8,4},{9,5},... | collective-permute-start | bytes 614408 | tf_op jit(solution)/shard_map/ppermute | solution.py:78
  32.5 9.9 %collective-permute-start.8 = (f32[200,256]{1,0:T(8,128)S(1)}, f32[200,256]{1,0:T(8,128)S(1)}, u32[]{:S(2)}, u32[]{:S(2)}) collective-permute-start(f32[200,256]{1,0:T(8,128)S(1)} %shard_map.79.rest_0_), channel_id=1, source_target_pairs={{0,4},{1,5},{2,6},{3,7},{4,0},{5,1},{6,2},{7,3},{8,12},{9,13},{10,... | collective-permute-start | bytes 614408 | tf_op jit(solution)/shard_map/ppermute | solution.py:78
  33.1 1.6 %copy-start.1 = (f32[8,256,256]{2,1,0:T(8,128)S(1)}, f32[8,256,256]{2,1,0:T(8,128)}, u32[]{:S(2)}) copy-start(f32[8,256,256]{2,1,0:T(8,128)} %right_ops.2) | copy-start | bytes 6291460
  39.7 6.9 %collective-permute-start.9 = (f32[200,256]{1,0:T(8,128)S(1)}, f32[200,256]{1,0:T(8,128)S(1)}, u32[]{:S(2)}, u32[]{:S(2)}) collective-permute-start(f32[200,256]{1,0:T(8,128)S(1)} %collective-permute-done.7.rest_3_), channel_id=1, source_target_pairs={{0,4},{1,5},{2,6},{3,7},{4,0},{5,1},{6,2},{7,3},{8,12},{9,13},{10,... | collective-permute-start | bytes 614408 | tf_op jit(solution)/shard_map/ppermute | solution.py:78
  41.8 4.9 %collective-permute-start.10 = (f32[200,256]{1,0:T(8,128)S(1)}, f32[200,256]{1,0:T(8,128)S(1)}, u32[]{:S(2)}, u32[]{:S(2)}) collective-permute-start(f32[200,256]{1,0:T(8,128)S(1)} %shard_map.79.rest_0_), channel_id=1, source_target_pairs={{0,1},{1,0},{2,3},{3,2},{4,5},{5,4},{6,7},{7,6},{8,9},{9,8},{10,11... | collective-permute-start | bytes 614408 | tf_op jit(solution)/shard_map/ppermute | solution.py:65
  41.8 4.9 %collective-permute-start.13 = (f32[200,256]{1,0:T(8,128)S(1)}, f32[200,256]{1,0:T(8,128)S(1)}, u32[]{:S(2)}, u32[]{:S(2)}) collective-permute-start(f32[200,256]{1,0:T(8,128)S(1)} %collective-permute-done.7.rest_3_), channel_id=1, source_target_pairs={{0,1},{1,0},{2,3},{3,2},{4,5},{5,4},{6,7},{7,6},{8,9},{9,8},{10,11... | collective-permute-start | bytes 614408 | tf_op jit(solution)/shard_map/ppermute | solution.py:65
  42.4 4.3 %collective-permute-start.11 = (f32[200,256]{1,0:T(8,128)S(1)}, f32[200,256]{1,0:T(8,128)S(1)}, u32[]{:S(2)}, u32[]{:S(2)}) collective-permute-start(f32[200,256]{1,0:T(8,128)S(1)} %collective-permute-done.8.rest_1_), channel_id=1, source_target_pairs={{0,1},{1,0},{2,3},{3,2},{4,5},{5,4},{6,7},{7,6},{8,9},{9,8},{10,11... | collective-permute-start | bytes 614408 | tf_op jit(solution)/shard_map/ppermute | solution.py:65
  46.7 1.5 %collective-permute-start.12 = (f32[200,256]{1,0:T(8,128)S(1)}, f32[200,256]{1,0:T(8,128)S(1)}, u32[]{:S(2)}, u32[]{:S(2)}) collective-permute-start(f32[200,256]{1,0:T(8,128)S(1)} %collective-permute-done.9.rest_2_), channel_id=1, source_target_pairs={{0,1},{1,0},{2,3},{3,2},{4,5},{5,4},{6,7},{7,6},{8,9},{9,8},{10,11... | collective-permute-start | bytes 614408 | tf_op jit(solution)/shard_map/ppermute | solution.py:65
  54.6 1.5 %collective-permute-start.14 = (f32[1,1,192,256]{3,2,1,0:T(8,128)S(1)}, f32[1,1,192,256]{3,2,1,0:T(8,128)S(1)}, u32[]{:S(2)}, u32[]{:S(2)}) collective-permute-start(f32[1,1,192,256]{3,2,1,0:T(8,128)S(1)} %get-tuple-element.80), channel_id=1, source_target_pairs={{0,1},{1,0},{2,3},{3,2},{4,5},{5,4},{6,7},{7,6},{8,9},{9,8},{10,11... | collective-permute-start | bytes 589832 | tf_op jit(solution)/shard_map/ppermute | solution.py:65
  56.2 8.7 %collective-permute-start.15 = (f32[1,192,256]{2,1,0:T(8,128)S(1)}, f32[1,192,256]{2,1,0:T(8,128)S(1)}, u32[]{:S(2)}, u32[]{:S(2)}) collective-permute-start(f32[1,192,256]{2,1,0:T(8,128)S(1)} %bitcast.70), channel_id=1, source_target_pairs={{0,4},{1,5},{2,6},{3,7},{4,0},{5,1},{6,2},{7,3},{8,12},{9,13},{10,... | collective-permute-start | bytes 589832 | tf_op jit(solution)/shard_map/ppermute | solution.py:75
  63.3 1.5 %collective-permute-start.19 = (f32[1,1,192,256]{3,2,1,0:T(8,128)S(1)}, f32[1,1,192,256]{3,2,1,0:T(8,128)S(1)}, u32[]{:S(2)}, u32[]{:S(2)}) collective-permute-start(f32[1,1,192,256]{3,2,1,0:T(8,128)S(1)} %get-tuple-element.91), channel_id=1, source_target_pairs={{0,1},{1,0},{2,3},{3,2},{4,5},{5,4},{6,7},{7,6},{8,9},{9,8},{10,11... | collective-permute-start | bytes 589832 | tf_op jit(solution)/shard_map/ppermute | solution.py:65
  63.4 2.2 %collective-permute-start.17 = (f32[1,192,256]{2,1,0:T(8,128)S(1)}, f32[1,192,256]{2,1,0:T(8,128)S(1)}, u32[]{:S(2)}, u32[]{:S(2)}) collective-permute-start(f32[1,192,256]{2,1,0:T(8,128)S(1)} %get-tuple-element.88), channel_id=1, source_target_pairs={{0,1},{1,0},{2,3},{3,2},{4,5},{5,4},{6,7},{7,6},{8,9},{9,8},{10,11... | collective-permute-start | bytes 589832 | tf_op jit(solution)/shard_map/ppermute | solution.py:65
  65.0 7.2 %collective-permute-start.20 = (f32[200,256]{1,0:T(8,128)S(1)}, f32[200,256]{1,0:T(8,128)S(1)}, u32[]{:S(2)}, u32[]{:S(2)}) collective-permute-start(f32[200,256]{1,0:T(8,128)S(1)} %pad_maximum_fusion), channel_id=1, source_target_pairs={{0,2},{1,3},{2,0},{3,1},{4,6},{5,7},{6,4},{7,5},{8,10},{9,11},{10,... | collective-permute-start | bytes 614408 | tf_op jit(solution)/shard_map/ppermute | solution.py:68
  65.6 6.7 %collective-permute-start.18 = (f32[192,256]{1,0:T(8,128)S(1)}, f32[192,256]{1,0:T(8,128)S(1)}, u32[]{:S(2)}, u32[]{:S(2)}) collective-permute-start(f32[192,256]{1,0:T(8,128)S(1)} %bitcast.71), channel_id=1, source_target_pairs={{0,4},{1,5},{2,6},{3,7},{4,0},{5,1},{6,2},{7,3},{8,12},{9,13},{10,... | collective-permute-start | bytes 589832 | tf_op jit(solution)/shard_map/ppermute | solution.py:75
  66.6 5.8 %collective-permute-start.16 = (f32[1,192,256]{2,1,0:T(8,128)S(1)}, f32[1,192,256]{2,1,0:T(8,128)S(1)}, u32[]{:S(2)}, u32[]{:S(2)}) collective-permute-start(f32[1,192,256]{2,1,0:T(8,128)S(1)} %get-tuple-element.87), channel_id=1, source_target_pairs={{0,1},{1,0},{2,3},{3,2},{4,5},{5,4},{6,7},{7,6},{8,9},{9,8},{10,11... | collective-permute-start | bytes 589832 | tf_op jit(solution)/shard_map/ppermute | solution.py:65
